TPU v7x, 256 devices: a whole 4x4x8 slice. The times are simulated.
256 devices in a mesh: ens: 4 (over z_lo), space: 64 (over z_hi, x, y, core).
Axes of the slice: x: 4, y: 4, z: 8 (z_hi: 2, z_lo: 4; z = z_hi * 4 + z_lo), core: 2. Of those that a mesh axis runs over, the one named last changes fastest.
Arguments:
- latent: bfloat16 [8, 8192, 1024], P('ens', 'space'), may hold values from -6 to 6
- src_weight: bfloat16 [1024, 1024], replicated, may hold values from -0.1875 to 0.1875
- decoder_projection: bfloat16 [1024, 100], replicated, may hold values from -0.1875 to 0.1875
- verifying_truth: float32 [100, 16384], P(None, 'space'), may hold values from -3 to 3
- area_weight: float32 [16384], P('space'), may hold values from 0.5 to 4
- var_weight: float32 [100], replicated, may hold values from 0.5 to 4
- edge_src: int32 [128, 512], P('space'), may hold values from 0 to 383, as said below
- edge_dst: int32 [128, 512], P('space'), may hold values from 0 to 127
- edge_weight: float32 [128, 512], P('space'), may hold values from 0.2 to 1
- edge_count: int32 [128], P('space'), may hold values from 170 to 512, as said below
Outputs:
- score_field: float32 [100, 16384], P(None, 'space')
- grad_latent: bfloat16 [8, 8192, 1024], P('ens', 'space')
- grad_src: float32 [1024, 1024], P('space')
- grad_out: float32 [1024, 100], P('space')
Inputs may be any that keep to these rules, and one draw needn't show every extreme that they name: `edge_src`: rows of a device's extended latent rows: first the last 128 nodes of the previous index of space (wrapping around), then its own 128, then the first 128 of the next. Block b of a device (b = t mod 2) reads rows b * 64 to b * 64 + 128 / 2 + 2 * 128 - 1. `edge_count`: slots from this count on are padding.
All inputs are finite; a program needn't handle non-finite values.
Results may differ from a plain program's by a relative error of at most 0.015.
The roundings to bfloat16 on the way count: a program that leaves them out, or rounds other values in their place, can miss the bound.
Values may be sent and summed in bfloat16 or wider, within the bound.
No kernel may reach another device: no remote copies, remote signals or barrier semaphores. Data moves between devices by JAX's collectives and lax.ppermute only.
A program may use at most 64 MiB of HBM per device.

v0:
```python
import math

import jax
import jax.numpy as jnp
from jax import lax
from jax.sharding import PartitionSpec as P

HALO = 128
BLK = 128


ALPHA = 0.95
DELTA = 0.05


def extended_2(cells, sides, width):
    for axis, dim in sides:
        count = lax.axis_size(axis)
        head = lax.slice_in_dim(cells, 0, width, axis=dim)
        tail = lax.slice_in_dim(cells, cells.shape[dim] - width, cells.shape[dim], axis=dim)
        cells = jnp.concatenate(
            [
                lax.ppermute(tail, axis, [(i, (i + 1) % count) for i in range(count)]),
                cells,
                lax.ppermute(head, axis, [((i + 1) % count, i) for i in range(count)]),
            ],
            axis=dim,
        )
    return cells


def from_behind(value, axis, by):
    size = lax.axis_size(axis)
    return lax.ppermute(value, axis, [(i, (i + by) % size) for i in range(size)])


def smooth_abs(distance):
    return jnp.sqrt(distance * distance + DELTA * DELTA)


def smoothed_signum(distance):
    return distance / jnp.sqrt(distance * distance + DELTA * DELTA)


def edge_matrix(edge_dst, edge_weight, edge_count):
    slot_ids = jnp.arange(edge_dst.shape[-1], dtype=jnp.int32)
    is_valid = slot_ids[None, :] < edge_count[:, None]
    edge_coefs = jnp.where(is_valid, edge_weight, 0.0).astype(jnp.bfloat16)
    points = jnp.arange(BLK, dtype=jnp.int32)
    return jnp.where(
        edge_dst[:, None, :] == points[None, :, None],
        edge_coefs[:, None, :],
        jnp.zeros((), jnp.bfloat16),
    )


def pair_factor(realization_number):
    fair_eps = (1.0 - ALPHA) / realization_number
    return (1.0 - fair_eps) / (2.0 * realization_number * (realization_number - 1))


def crps_score(collected_sequence, verifying_truth):
    realization_number = len(collected_sequence)
    couple_factor = pair_factor(realization_number)
    skill_sum = smooth_abs(collected_sequence[0] - verifying_truth)
    for realization_position in range(1, realization_number):
        skill_sum = skill_sum + smooth_abs(
            collected_sequence[realization_position] - verifying_truth
        )
    spread = jnp.zeros_like(skill_sum)
    for realization_position in range(realization_number):
        for other_number in range(realization_position + 1, realization_number):
            spread = spread + smooth_abs(
                collected_sequence[realization_position] - collected_sequence[other_number]
            )
    return skill_sum / realization_number - couple_factor * 2.0 * spread


def realization_adjoint(local_prediction, collected_sequence, verifying_truth, multiplier_array):
    realization_number = len(collected_sequence)
    couple_factor = pair_factor(realization_number)
    mutual_difference_sum = jnp.zeros_like(local_prediction)
    for companion_realization in collected_sequence:
        mutual_difference_sum = mutual_difference_sum + smoothed_signum(
            local_prediction - companion_realization
        )
    return multiplier_array * (
        smoothed_signum(local_prediction - verifying_truth) / realization_number
        - 2.0 * couple_factor * mutual_difference_sum
    )


def body(
    latent,
    src_weight,
    decoder_projection,
    verifying_truth,
    area_weight,
    var_weight,
    edge_src,
    edge_dst,
    edge_weight,
    edge_count,
):
    locally_held_realizations = latent.shape[0]
    hid_rows = latent.shape[1]
    members = locally_held_realizations * lax.axis_size("ens")
    grid_all = verifying_truth.shape[1] * lax.axis_size("space")
    project = jnp.einsum(
        "mnd,de->mne", latent, src_weight, preferred_element_type=jnp.float32
    ).astype(jnp.bfloat16)
    extended = extended_2(project, (("space", 1),), HALO)
    blocks = edge_src.shape[0]
    stride = hid_rows // blocks
    window = stride + 2 * HALO
    matrix = edge_matrix(edge_dst, edge_weight, edge_count)
    starts = jnp.arange(blocks, dtype=jnp.int32) * stride
    relative = edge_src - starts[:, None]
    source_hot = (
        relative[:, :, None] == jnp.arange(window, dtype=jnp.int32)[None, None, :]
    ).astype(jnp.bfloat16)
    coef = jnp.einsum("bps,bsr->bpr", matrix, source_hot, preferred_element_type=jnp.float32)
    coef_high = coef.astype(jnp.bfloat16)
    coef_low = (coef - coef_high.astype(jnp.float32)).astype(jnp.bfloat16)
    windows = jax.vmap(lambda start: lax.dynamic_slice_in_dim(extended, start, window, 1))(starts)
    summed = jnp.einsum("bpr,bmrd->mbpd", coef_high, windows, preferred_element_type=jnp.float32)
    summed = summed + jnp.einsum(
        "bpr,bmrd->mbpd", coef_low, windows, preferred_element_type=jnp.float32
    )
    summed = summed.reshape(locally_held_realizations, blocks * BLK, summed.shape[3])
    latent_activation, gelu_back = jax.vjp(jax.nn.gelu, summed)
    latent_activation = latent_activation.astype(jnp.bfloat16)
    realization_prediction = jnp.einsum(
        "uyf,fc->ucy", latent_activation, decoder_projection, preferred_element_type=jnp.float32
    )
    multiplier_array = var_weight[:, None] * area_weight[None, :]
    local_sequence = [
        realization_prediction[realization_position]
        for realization_position in range(locally_held_realizations)
    ]
    collected_realizations = lax.all_gather(realization_prediction, "ens", axis=0, tiled=True)
    collected_sequence = [
        collected_realizations[realization_position] for realization_position in range(members)
    ]
    score_field = crps_score(collected_sequence, verifying_truth)
    prediction_adjoint = jnp.stack(
        [
            realization_adjoint(
                local_prediction, collected_sequence, verifying_truth, multiplier_array
            )
            for local_prediction in local_sequence
        ]
    ).astype(jnp.bfloat16)
    output_gradient = jnp.einsum(
        "rvs,rhv->sh", latent_activation, prediction_adjoint, preferred_element_type=jnp.float32
    )
    hidden_grad = jnp.einsum(
        "bhr,fh->brf", prediction_adjoint, decoder_projection, preferred_element_type=jnp.float32
    )
    summed_grad = gelu_back(hidden_grad)[0].astype(jnp.bfloat16)
    summed_grad = summed_grad.reshape(locally_held_realizations, blocks, BLK, summed_grad.shape[2])
    window_grads = jnp.einsum(
        "bpr,mbpd->bmrd", coef_high, summed_grad, preferred_element_type=jnp.float32
    )
    window_grads = window_grads + jnp.einsum(
        "bpr,mbpd->bmrd", coef_low, summed_grad, preferred_element_type=jnp.float32
    )

    def add_window(block_number, accumulated):
        start = block_number * stride
        current = lax.dynamic_slice_in_dim(accumulated, start, window, 1)
        return lax.dynamic_update_slice_in_dim(
            accumulated, current + window_grads[block_number], start, 1
        )

    ext_grad = lax.fori_loop(0, blocks, add_window, jnp.zeros(extended.shape, jnp.float32))
    from_right = from_behind(ext_grad[:, :HALO], "space", -1)
    from_left = from_behind(ext_grad[:, HALO + hid_rows :], "space", 1)
    own_grad = ext_grad[:, HALO : HALO + hid_rows]
    own_grad = own_grad.at[:, :HALO].add(from_left).at[:, hid_rows - HALO :].add(from_right)
    own_grad = own_grad.astype(jnp.bfloat16)
    grad_latent = jnp.einsum(
        "mne,de->mnd", own_grad, src_weight, preferred_element_type=jnp.float32
    ).astype(jnp.bfloat16)
    src_grad = jnp.einsum("mnd,mne->de", latent, own_grad, preferred_element_type=jnp.float32)
    scaling = 1.0 / math.sqrt(members * grid_all)
    rows_device = src_grad.shape[0] // lax.axis_size("space")
    src_sum, out_sum = lax.psum((src_grad, output_gradient), ("ens", "space"))
    offset_row = lax.axis_index("space") * rows_device
    src_sum = lax.dynamic_slice_in_dim(src_sum, offset_row, rows_device, 0)
    out_sum = lax.dynamic_slice_in_dim(out_sum, offset_row, rows_device, 0)
    return (score_field, grad_latent, src_sum * scaling, out_sum * scaling)


def solution(mesh):
    return jax.shard_map(
        body,
        mesh=mesh,
        in_specs=(
            P("ens", "space", None),
            P(),
            P(),
            P(None, "space"),
            P("space"),
            P(),
            P("space", None),
            P("space", None),
            P("space", None),
            P("space"),
        ),
        out_specs=(P(None, "space"), P("ens", "space", None), P("space", None), P("space", None)),
        check_vma=False,
    )
```

profile of v0, /device:TPU:8, one launch (start us, length us, event | category | flops | bytes accessed | tf_op | source)
XLA Modules:
  0.0 413.8 jit_solution(2903033543891534158)
XLA Ops:
  7.2 0.0 all-reduce.3.cloned.1.call-start
  7.3 1.5 copy-done
  8.8 1.7 fusion.16
  10.5 0.1 collective-permute-start.1
  10.6 0.5 collective-permute-start
  11.1 0.1 pad_add_fusion
  11.2 0.1 fusion.45
  11.3 0.1 broadcast_subtract_fusion
  11.4 0.4 fusion.15
  11.7 5.6 %collective-permute-done.1 = bf16[2,128,1024]{2,1,0:T(8,128)(2,1)S(1)} collective-permute-done((bf16[2,128,1024]{2,1,0:T(8,128)(2,1)S(1)}, bf16[2,128,1024]{2,1,0:T(8,128)(2,1)S(1)}, u32[]{:S(2)}, u32[]{:S(2)}) %collective-permute-start.1) | collective-permute-done | bytes 524320 | tf_op jit(solution)/shard_map/ppermute | solution.py:25
  17.3 2.6 collective-permute-done
  19.9 2.3 pad_maximum_fusion
  22.2 7.9 %while.19 = (s32[]{:T(128)}, bf16[2,384,1024]{2,1,0:T(8,128)(2,1)}, s32[2,3]{1,0:T(2,128)S(1)}, bf16[2,2,320,1024]{3,2,1,0:T(8,128)(2,1)}, s32[]{:T(128)}) while((s32[]{:T(128)}, bf16[2,384,1024]{2,1,0:T(8,128)(2,1)}, s32[2,3]{1,0:T(2,128)S(1)}, bf16[2,2,320,1024]{3,2,1,0:T(8,128)(2,1)}, s32[]{:T(128)}) %tuple.62), condition=%wide.while_cond.2, body=%wide.while_body.2.sunk | while | flops 2 | bytes 2622061 | solution.py:125
  22.2 0.6 slice.217
  22.8 3.4 bitcast_dynamic-update-slice_fusion.2
  26.2 0.6 slice.217
  26.7 3.4 bitcast_dynamic-update-slice_fusion.2
  30.1 2.6 fusion.33
  32.8 0.8 add_bitcast_fusion.1
  33.6 0.1 copy.25
  33.7 0.7 fusion.4
  34.5 0.2 copy-done.6
  34.7 0.5 convolution_bitcast_fusion.2
  35.1 21.1 %all_gather.3 = f32[8,100,256]{2,1,0:T(8,128)S(1)} all-gather(f32[2,100,256]{2,1,0:T(8,128)S(1)} %convolution_bitcast_fusion.2), channel_id=1, replica_groups=mesh['ens'=4,'space'=64] {'ens'}, dimensions={0}, use_global_device_ids=true | all-gather | bytes 1024000 | tf_op jit(solution)/shard_map/all_gather | solution.py:141
  56.2 0.2 fusion.42
  56.4 0.8 copy-done.2
  57.2 0.2 fusion.41
  57.5 1.2 fusion.7
  58.7 0.8 fusion.22
  59.5 3.2 add_bitcast_fusion
  62.7 2.1 broadcast_in_dim.21
  64.8 9.6 %while.18 = (s32[]{:T(128)}, f32[2,384,1024]{2,1,0:T(8,128)}, f32[2,2,320,1024]{3,2,1,0:T(8,128)}, s32[]{:T(128)}, s32[]{:T(128)}, /*index=5*/s32[]{:T(128)}, s32[]{:T(128)}) while((s32[]{:T(128)}, f32[2,384,1024]{2,1,0:T(8,128)}, f32[2,2,320,1024]{3,2,1,0:T(8,128)}, s32[]{:T(128)}, s32[]{:T(128)}, /*index=5*/s32[]{:T(128)}, s32[]{:T(128)}) %tuple.65), condition=%wide.region_1.2_spmd, body=%wide.region_0.1_spmd.sunk | while | flops 655366 | bytes 7864459 | solution.py:176
  64.8 4.8 %fusion.59 = f32[2,384,1024]{2,1,0:T(8,128)} fusion(f32[2,384,1024]{2,1,0:T(8,128)} %get-tuple-element.216, s32[]{:T(128)S(6)} %select_n.46, f32[2,2,320,1024]{3,2,1,0:T(8,128)} %get-tuple-element.224, s32[]{:T(128)S(6)} %copy.49), kind=kLoop, calls=%fused_computation.1.clone.1 | loop fusion | flops 655360 | bytes 7864328 | tf_op jit(solution)/shard_map/while/body/eval_jaxpr/dynamic_update_slice | solution.py:172
  69.6 4.8 %fusion.59 = f32[2,384,1024]{2,1,0:T(8,128)} fusion(f32[2,384,1024]{2,1,0:T(8,128)} %get-tuple-element.216, s32[]{:T(128)S(6)} %select_n.46, f32[2,2,320,1024]{3,2,1,0:T(8,128)} %get-tuple-element.224, s32[]{:T(128)S(6)} %copy.49), kind=kLoop, calls=%fused_computation.1.clone.1 | loop fusion | flops 655360 | bytes 7864328 | tf_op jit(solution)/shard_map/while/body/eval_jaxpr/dynamic_update_slice | solution.py:172
  74.5 1.7 fusion.49
  76.1 0.1 collective-permute-start.2
  76.2 1.7 collective-permute-start.3
  78.0 1.3 convolution_bitcast_fusion.1
  79.2 11.2 %collective-permute-done.2 = f32[2,128,1024]{2,1,0:T(8,128)S(1)} collective-permute-done((f32[2,128,1024]{2,1,0:T(8,128)S(1)}, f32[2,128,1024]{2,1,0:T(8,128)S(1)}, u32[]{:S(2)}, u32[]{:S(2)}) %collective-permute-start.2) | collective-permute-done | bytes 1048608 | tf_op jit(solution)/shard_map/ppermute | solution.py:34
  90.4 1.5 add_convert_fusion
  91.9 2.8 convolution_bitcast_fusion
  94.7 1.1 copy-done.3
  95.9 2.9 multiply_subtract_fusion
  98.8 1.5 fusion.19
  100.3 303.3 %all-reduce.3.cloned.1.call-done = (f32[1024,1024]{0,1:T(8,128)}, f32[1024,100]{1,0:T(8,128)}) async-done(((f32[1024,1024]{0,1:T(8,128)}, f32[1024,100]{1,0:T(8,128)}), (f32[1024,1024]{0,1:T(8,128)}, f32[1024,100]{1,0:T(8,128)})) %all-reduce.3.cloned.1.call-update) | async-done | bytes 4603920 | tf_op jit(solution)/shard_map/psum | solution.py:188
  403.6 1.2 dynamic-slice_multiply_fusion
  404.8 1.3 dynamic-slice_multiply_fusion.1
  406.1 0.8 copy.30
  (34 shorter events, 0.1 us)
Async XLA Ops:
  7.2 1.6 copy-start
  7.2 4.0 copy-start.13
  7.2 4.0 copy-start.11
  7.2 4.1 copy-start.10
  7.2 4.1 %copy-start.14 = (s32[2,512]{1,0:T(2,128)S(1)}, s32[2,512]{1,0:T(2,128)}, u32[]{:S(2)}) copy-start(s32[2,512]{1,0:T(2,128)} %param.27) | copy-start | bytes 12292
  7.2 396.4 %all-reduce.3.cloned.1.call-start = ((), (), s32[]{:S(2)}) async-start(), calls=%async_computation | async-start | bytes 9437184 | tf_op jit(solution)/shard_map/psum | solution.py:188
  10.5 6.8 %collective-permute-start.1 = (bf16[2,128,1024]{2,1,0:T(8,128)(2,1)S(1)}, bf16[2,128,1024]{2,1,0:T(8,128)(2,1)S(1)}, u32[]{:S(2)}, u32[]{:S(2)}) collective-permute-start(bf16[2,128,1024]{2,1,0:T(8,128)(2,1)S(1)} %fusion.16), channel_id=1, source_target_pairs={{1,0},{2,1},{3,2},{4,3},{5,4},{6,5},{7,6},{8,7},{9,8},{10,9},{11,1... | collective-permute-start | bytes 1572872 | tf_op jit(solution)/shard_map/ppermute | solution.py:25
  10.6 9.3 %collective-permute-start = (bf16[2,128,1024]{2,1,0:T(8,128)(2,1)S(1)}, bf16[2,128,1024]{2,1,0:T(8,128)(2,1)}, u32[]{:S(2)}, u32[]{:S(2)}) collective-permute-start(bf16[2,128,1024]{2,1,0:T(8,128)(2,1)S(1)} %fusion.16), channel_id=1, source_target_pairs={{0,1},{1,2},{2,3},{3,4},{4,5},{5,6},{6,7},{7,8},{8,9},{9,10},{10,1... | collective-permute-start | bytes 1572872 | tf_op jit(solution)/shard_map/ppermute | solution.py:23
  30.1 2.7 copy-start.1
  33.7 0.9 copy-start.6
  34.4 21.8 %copy-start.5 = (f32[100,256]{1,0:T(8,128)S(1)}, f32[100,256]{1,0:T(8,128)}, u32[]{:S(2)}) copy-start(f32[100,256]{1,0:T(8,128)} %param.23) | copy-start | bytes 307204
  34.4 21.8 %copy-start.9 = (f32[256]{0:T(256)S(1)}, f32[256]{0:T(256)}, u32[]{:S(2)}) copy-start(f32[256]{0:T(256)} %param.24) | copy-start | bytes 3076
  34.4 21.8 %copy-start.12 = (f32[100]{0:T(128)S(1)}, f32[100]{0:T(128)}, u32[]{:S(2)}) copy-start(f32[100]{0:T(128)} %param.25) | copy-start | bytes 1204
  56.2 1.0 copy-start.2
  57.4 1.2 copy-start.7
  74.5 3.5 copy-start.8
  76.1 14.3 %collective-permute-start.2 = (f32[2,128,1024]{2,1,0:T(8,128)S(1)}, f32[2,128,1024]{2,1,0:T(8,128)S(1)}, u32[]{:S(2)}, u32[]{:S(2)}) collective-permute-start(f32[2,128,1024]{2,1,0:T(8,128)S(1)} %get-tuple-element.145), channel_id=1, source_target_pairs={{0,1},{1,2},{2,3},{3,4},{4,5},{5,6},{6,7},{7,8},{8,9},{9,10},{10,1... | collective-permute-start | bytes 3145736 | tf_op jit(solution)/shard_map/ppermute | solution.py:34
  76.2 14.2 %collective-permute-start.3 = (f32[2,128,1024]{2,1,0:T(8,128)S(1)}, f32[2,128,1024]{2,1,0:T(8,128)S(1)}, u32[]{:S(2)}, u32[]{:S(2)}) collective-permute-start(f32[2,128,1024]{2,1,0:T(8,128)S(1)} %get-tuple-element.146), channel_id=1, source_target_pairs={{0,63},{1,0},{2,1},{3,2},{4,3},{5,4},{6,5},{7,6},{8,7},{9,8},{10,9... | collective-permute-start | bytes 3145736 | tf_op jit(solution)/shard_map/ppermute | solution.py:34
  79.2 12.7 %copy-start.4 = (bf16[2,128,1024]{2,1,0:T(8,128)(2,1)S(1)}, bf16[2,128,1024]{2,1,0:T(8,128)(2,1)}, u32[]{:S(2)}) copy-start(bf16[2,128,1024]{2,1,0:T(8,128)(2,1)} %param.20) | copy-start | bytes 1572868
  94.7 1.2 copy-start.3
Sparse Core Ops, SparseCore 0:
  94.9 308.6 all-reduce.2
where the time goes:
time: 415 us; the launch traced here: 414 us
  waiting for transfers between devices  323 us (78%)
  blocking collectives  21.1 us (5%)
  other arithmetic  20.2 us (5%)
  matrix products  16.8 us (4%)
  local copies, waits for them, and re-layouts  16.3 us (4%)
  between operations  14.3 us (3%)
    psum x1, waiting for transfers between devices, body(): src_sum, out_sum = lax.psum((src_grad, output_gradient), ('ens', 'space'))  303 us
    all_gather x1, blocking collectives, body(): lax.all_gather(realization_prediction, 'ens', axis=0, tiled=True)  21.1 us
    ppermute x2, waiting for transfers between devices, from_behind(): lax.ppermute(value, axis, [(i, (i + by) % size) for i in range(size)])  11.2 us
    dynamic_update_slice x2, other arithmetic, add_window(): lax.dynamic_update_slice_in_dim(accumulated, current + window_grads[block...  9.63 us
  transfers between devices with their start and end apart: 5, of which 4 were waited for; matrix products, arithmetic and copies ran while one was open for 2% of the time, Pallas kernels for 0%

commit v1 on v0

v1 whole, which is shorter than its diff:
```python
import math

import jax
import jax.numpy as jnp
from jax import lax
from jax.sharding import PartitionSpec as P

HALO = 128
BLK = 128
ALPHA = 0.95
DELTA = 0.05
SPACE = ("zhi", "x", "y", "core")
QMAX = 32000.0


def smooth_abs(distance):
    return jnp.sqrt(distance * distance + DELTA * DELTA)


def smoothed_signum(distance):
    return distance * lax.rsqrt(distance * distance + DELTA * DELTA)


def edge_matrix(edge_dst, edge_weight, edge_count):
    slot_ids = jnp.arange(edge_dst.shape[-1], dtype=jnp.int32)
    is_valid = slot_ids[None, :] < edge_count[:, None]
    edge_coefs = jnp.where(is_valid, edge_weight, 0.0).astype(jnp.bfloat16)
    points = jnp.arange(BLK, dtype=jnp.int32)
    return jnp.where(
        edge_dst[:, None, :] == points[None, :, None],
        edge_coefs[:, None, :],
        jnp.zeros((), jnp.bfloat16),
    )


def pair_factor(members):
    fair_eps = (1.0 - ALPHA) / members
    return (1.0 - fair_eps) / (2.0 * members * (members - 1))


def crps_score(collected, truth):
    members = len(collected)
    skill = sum(smooth_abs(f - truth) for f in collected)
    spread = jnp.zeros_like(skill)
    for m in range(members):
        for o in range(m + 1, members):
            spread = spread + smooth_abs(collected[m] - collected[o])
    return skill / members - pair_factor(members) * 2.0 * spread


def member_adjoint(own, collected, truth, multiplier):
    members = len(collected)
    mutual = sum(smoothed_signum(own - f) for f in collected)
    return multiplier * (
        smoothed_signum(own - truth) / members - 2.0 * pair_factor(members) * mutual
    )


def make_body(count):
    odd_pairs = [(i, (i + 1) % count if i % 2 else (i - 1) % count) for i in range(count)]
    far = [p for p in odd_pairs if abs(p[0] - p[1]) > 1 or p[0] // 32 != p[1] // 32]
    near = [p for p in odd_pairs if p not in far]
    swap = [(0, 1), (1, 0)]

    def body(
        latent, src_weight, decoder_projection, truth, area_weight, var_weight,
        edge_src, edge_dst, edge_weight, edge_count,
    ):
        local = latent.shape[0]
        rows = latent.shape[1]
        ens = lax.axis_size("ens")
        members = local * ens
        core = lax.axis_index("core")
        depth = latent.shape[2]
        nvar = decoder_projection.shape[1]
        points = truth.shape[1]
        grid_all = points * count

        odd_lat = lax.ppermute(latent, SPACE, odd_pairs)
        core_lat = lax.ppermute(latent, "core", swap)
        ext = jnp.concatenate([latent, core_lat, odd_lat], axis=1)
        window = ext.shape[1]

        side = edge_src // HALO
        left = jnp.where(core == 0, 2 * HALO, HALO)
        right = jnp.where(core == 0, HALO, 2 * HALO)
        place = jnp.where(side == 0, left, jnp.where(side == 1, 0, right))
        source = edge_src - side * HALO + place
        matrix = edge_matrix(edge_dst, edge_weight, edge_count)
        hot = (source[:, :, None] == jnp.arange(window, dtype=jnp.int32)).astype(jnp.bfloat16)
        coef = jnp.einsum("bps,bsr->bpr", matrix, hot, preferred_element_type=jnp.float32)
        coef = coef.reshape(points, window)
        high = coef.astype(jnp.bfloat16)
        low = (coef - high.astype(jnp.float32)).astype(jnp.bfloat16)

        def gather(values):
            return jnp.einsum(
                "pr,mrd->mpd", high, values, preferred_element_type=jnp.float32
            ) + jnp.einsum("pr,mrd->mpd", low, values, preferred_element_type=jnp.float32)

        project = jnp.einsum(
            "mnd,de->mne", ext, src_weight, preferred_element_type=jnp.float32
        ).astype(jnp.bfloat16)
        summed = gather(project)
        hidden, gelu_back = jax.vjp(jax.nn.gelu, summed)
        hidden = hidden.astype(jnp.bfloat16)
        forecast = jnp.einsum(
            "mpd,dv->mvp", hidden, decoder_projection, preferred_element_type=jnp.float32
        )
        largest = jnp.max(jnp.abs(forecast), axis=2, keepdims=True)
        power = jnp.ceil(jnp.log2(jnp.maximum(largest, 1e-30)) + 1e-3)
        coded = jnp.round(forecast * (jnp.exp2(-power) * QMAX)).astype(jnp.int16)
        power16 = jnp.broadcast_to(power, (local, nvar, 128)).astype(jnp.int16)
        coded = jnp.concatenate([coded, power16], axis=2)
        everyone = lax.all_gather(coded, "ens", axis=0, tiled=True)
        decoded = everyone[:, :, :points].astype(jnp.float32) * (
            jnp.exp2(everyone[:, :, points : points + 1].astype(jnp.float32)) * (1.0 / QMAX)
        )
        collected = [decoded[m] for m in range(members)]
        at = lax.axis_index("ens") * local
        own = lax.dynamic_slice_in_dim(decoded, at, local, 0)
        multiplier = var_weight[:, None] * area_weight[None, :]
        adjoint = jnp.stack(
            [member_adjoint(own[m], collected, truth, multiplier) for m in range(local)]
        ).astype(jnp.bfloat16)
        score = crps_score(collected, truth)

        agg = gather(ext).astype(jnp.bfloat16)
        out_sum = jnp.einsum("mpd,mvp->dv", hidden, adjoint, preferred_element_type=jnp.float32)
        hidden_grad = jnp.einsum(
            "mvp,dv->mpd", adjoint, decoder_projection, preferred_element_type=jnp.float32
        )
        summed_grad = gelu_back(hidden_grad)[0].astype(jnp.bfloat16)
        src_sum = jnp.einsum("mpd,mpe->de", agg, summed_grad, preferred_element_type=jnp.float32)

        partial = jnp.concatenate(
            [src_sum, jnp.pad(out_sum, ((0, 0), (0, 128 - nvar)))], axis=1
        ).astype(jnp.bfloat16)
        cols = partial.shape[1]
        per = depth // count
        partial = partial.reshape(2, 16, 2, per, cols)
        mine = lax.dynamic_index_in_dim(partial, core, 2, keepdims=False)
        theirs = lax.dynamic_index_in_dim(partial, 1 - core, 2, keepdims=False)
        theirs = lax.ppermute(theirs, "core", swap)

        row_grad = jnp.einsum(
            "pr,mpd->mrd", high, summed_grad, preferred_element_type=jnp.float32
        ) + jnp.einsum("pr,mpd->mrd", low, summed_grad, preferred_element_type=jnp.float32)
        send = row_grad[:, rows:].astype(jnp.bfloat16)
        far_grad = lax.ppermute(send[:, HALO:], SPACE, far)

        half = (mine.astype(jnp.float32) + theirs.astype(jnp.float32)).astype(jnp.bfloat16)
        half = half.transpose(1, 0, 2, 3)
        got = lax.all_to_all(half, ("x", "y"), 0, 0, tiled=True)
        plane = jnp.sum(got.astype(jnp.float32), axis=0).astype(jnp.bfloat16)
        near_grad = lax.ppermute(send[:, HALO:], SPACE, near)
        core_grad = lax.ppermute(send[:, :HALO], "core", swap)
        copies = jnp.broadcast_to(plane[:, None], (2, ens, per, cols)).reshape(2 * ens, per, cols)
        got = lax.all_to_all(copies, ("zhi", "ens"), 0, 0, tiled=True)
        total = jnp.sum(got.astype(jnp.float32), axis=0) * (1.0 / math.sqrt(members * grid_all))

        own_grad = (
            row_grad[:, :rows]
            + core_grad.astype(jnp.float32)
            + far_grad.astype(jnp.float32)
            + near_grad.astype(jnp.float32)
        ).astype(jnp.bfloat16)
        grad_latent = jnp.einsum(
            "mne,de->mnd", own_grad, src_weight, preferred_element_type=jnp.float32
        ).astype(jnp.bfloat16)
        return score, grad_latent, total[:, :depth], total[:, depth : depth + nvar]

    return body


def solution(mesh):
    fine = jax.sharding.Mesh(
        mesh.devices.reshape(mesh.devices.shape[0], 2, 4, 4, 2), ("ens",) + SPACE
    )
    return jax.shard_map(
        make_body(mesh.devices.shape[1]),
        mesh=fine,
        in_specs=(
            P("ens", SPACE, None), P(), P(), P(None, SPACE), P(SPACE), P(),
            P(SPACE, None), P(SPACE, None), P(SPACE, None), P(SPACE),
        ),
        out_specs=(P(None, SPACE), P("ens", SPACE, None), P(SPACE, None), P(SPACE, None)),
        check_vma=False,
    )
```

time: 415 us -> 118 us (0.28)
  waiting for transfers between devices: 323 us -> 21.2 us
  starting transfers between devices: 2.43 us -> 28.7 us
  between operations: 14.3 us -> 0.96 us
  matrix products: 16.8 us -> 27.1 us
  other arithmetic: 20.2 us -> 10 us
  local copies, waits for them, and re-layouts: 16.3 us -> 10.1 us
    psum x1 -> x0, waiting for transfers between devices: 303 us -> none  [body(): src_sum, out_sum = lax.psum((src_grad, output_gradient), ('ens', 'space'))]
    all_to_all x0 -> x2, starting transfers between devices: none -> 22.3 us  [the longest x1 16.2 us: body(): got = lax.all_to_all(half, ('x', 'y'), 0, 0, tiled=True)]
    all_to_all x0 -> x2, waiting for transfers between devices: none -> 15.1 us  [the longest x1 9.51 us: body(): got = lax.all_to_all(half, ('x', 'y'), 0, 0, tiled=True)]
    ppermute x4 -> x6, waiting for transfers between devices: 19.3 us -> 6.13 us  [the longest x1 3.29 us: body(): odd_lat = lax.ppermute(latent, SPACE, odd_pairs)]
    dynamic_update_slice x2 -> x0, other arithmetic: 9.63 us -> none  [add_window(): lax.dynamic_update_slice_in_dim(accumulated, current + window_grads[block...]
    dot_general x10 -> x11, matrix products: 15.3 us -> 23.9 us  [the longest x1 6.12 us: body(): jnp.einsum('mpd,mpe->de', agg, summed_grad, preferred_element_type=jnp.fl...]
    gather x6 -> x0, local copies, waits for them, and re-layouts: 7.93 us -> none
  transfers between devices with their start and end apart: 5 -> 8, of which waited for: 4 -> 4; matrix products, arithmetic and copies ran while one was open for 2% -> 14% of each run, Pallas kernels for 0% -> 0%
where the time goes in v1:
time: 118 us; the launch traced here: 117 us
  starting transfers between devices  28.7 us (24%)
  matrix products  27.1 us (23%)
  waiting for transfers between devices  21.2 us (18%)
  blocking collectives  18.7 us (16%)
  local copies, waits for them, and re-layouts  10.1 us (9%)
  other arithmetic  10 us (8%)
    all_gather x1, blocking collectives, body(): everyone = lax.all_gather(coded, 'ens', axis=0, tiled=True)  18.7 us
    all_to_all x1, starting transfers between devices, body(): got = lax.all_to_all(half, ('x', 'y'), 0, 0, tiled=True)  16.2 us
    all_to_all x1, waiting for transfers between devices, body(): got = lax.all_to_all(half, ('x', 'y'), 0, 0, tiled=True)  9.51 us
    dot_general x1, matrix products, body(): jnp.einsum('mpd,mpe->de', agg, summed_grad, preferred_element_type=jnp.fl...  6.12 us
    all_to_all x1, starting transfers between devices, body(): got = lax.all_to_all(copies, ('zhi', 'ens'), 0, 0, tiled=True)  6.1 us
    all_to_all x1, waiting for transfers between devices, body(): got = lax.all_to_all(copies, ('zhi', 'ens'), 0, 0, tiled=True)  5.58 us
    dot_general x2, matrix products, gather(): jnp.einsum('pr,mrd->mpd', low, values, preferred_element_type=jnp.float32)  4.67 us
    unnamed x31, local copies, waits for them, and re-layouts  4.12 us
  transfers between devices with their start and end apart: 8, of which 4 were waited for; matrix products, arithmetic and copies ran while one was open for 14% of the time, Pallas kernels for 0%

profile of v1, /device:TPU:8, one launch (start us, length us, event | category | flops | bytes accessed | tf_op | source)
XLA Modules:
  0.0 116.8 jit_solution(9087008184472165338)
XLA Ops:
  0.6 0.0 copy-start
  0.7 0.1 collective-permute-start
  0.8 2.3 %collective-permute-start.1 = (bf16[2,128,1024]{2,1,0:T(8,128)(2,1)}, bf16[2,128,1024]{2,1,0:T(8,128)(2,1)}, u32[]{:S(2)}, u32[]{:S(2)}) collective-permute-start(bf16[2,128,1024]{2,1,0:T(8,128)(2,1)} %param.10), channel_id=1, source_target_pairs={{0,63},{1,2},{2,1},{3,4},{4,3},{5,6},{6,5},{7,8},{8,7},{9,10},{10,... | collective-permute-start | bytes 1572872 | tf_op jit(solution)/shard_map/ppermute | solution.py:79
  3.0 0.8 fusion.56
  3.8 0.7 fusion.57
  4.5 1.2 %fusion.18 = f32[2,128,384]{2,1,0:T(8,128)S(1)} fusion(s32[2,512]{1,0:T(2,128)S(1)} %fusion.57, s32[2,512]{1,0:T(2,128)} %param.17, bf16[2,512]{1,0:T(2,128)(2,1)S(1)} %fusion.56), kind=kOutput, calls=%fused_computation.30 | convolution fusion | flops 101318656 | bytes 403456 | tf_op jit(solution)/shard_map/bps,bsr->bpr/dot_general | solution.py:91
  5.9 1.1 constant_dynamic-update-slice_fusion.1
  6.9 3.3 %collective-permute-done.1 = bf16[2,128,1024]{2,1,0:T(8,128)(2,1)} collective-permute-done((bf16[2,128,1024]{2,1,0:T(8,128)(2,1)}, bf16[2,128,1024]{2,1,0:T(8,128)(2,1)}, u32[]{:S(2)}, u32[]{:S(2)}) %collective-permute-start.1) | collective-permute-done | bytes 524320 | tf_op jit(solution)/shard_map/ppermute | solution.py:79
  10.2 1.1 constant_dynamic-update-slice_fusion
  11.3 1.8 %fusion.15 = bf16[2,384,1024]{2,1,0:T(8,128)(2,1)S(1)} fusion(bf16[2,384,1024]{2,1,0:T(8,128)(2,1)S(1)} %constant_dynamic-update-slice_fusion, bf16[1024,1024]{1,0:T(8,128)(2,1)S(1)} %copy-done), kind=kOutput, calls=%fused_computation.27 | convolution fusion | flops 1611399168 | bytes 5242880 | tf_op jit(solution)/shard_map/mnd,de->mne/dot_general | solution.py:101
  13.2 2.1 %fusion.39 = f32[2,1024,256]{2,1,0:T(8,128)} fusion(bf16[2,384,1024]{2,1,0:T(8,128)(2,1)S(1)} %constant_dynamic-update-slice_fusion, bf16[256,384]{1,0:T(8,128)(2,1)S(1)} %fusion.33), kind=kOutput, calls=%fused_computation.58 | convolution fusion | flops 402653184 | bytes 3866624 | tf_op jit(solution)/shard_map/pr,mrd->mpd/dot_general | solution.py:99
  15.3 0.8 fusion.47
  16.0 2.6 %fusion.10 = (bf16[2,256,1024]{1,2,0:T(8,128)(2,1)S(1)}, f32[2,1024,256]{2,1,0:T(8,128)}) fusion(f32[2,1024,256]{2,1,0:T(8,128)S(1)} %fusion.47, bf16[2,384,1024]{2,1,0:T(8,128)(2,1)S(1)} %fusion.15, bf16[256,384]{1,0:T(8,128)(2,1)S(1)} %fusion.33), kind=kOutput, calls=%fused_computation.21 | convolution fusion | flops 407896064 | bytes 7012352 | tf_op jit(solution)/shard_map/pr,mrd->mpd/dot_general | solution.py:99
  18.6 1.0 copy-done.1
  19.6 0.4 abs_reduce_fusion
  20.0 0.1 fusion.53
  20.1 0.1 broadcast_in_dim.52
  20.3 18.7 %all_gather.3 = s16[8,100,384]{2,1,0:T(8,128)(2,1)S(1)} all-gather(s16[2,100,384]{2,1,0:T(8,128)(2,1)S(1)} %pad_add_fusion), channel_id=1, replica_groups=mesh['ens'=4,'zhi'=2,'x'=4,'y'=4,'core'=2] {'ens'}, dimensions={0}, use_global_device_ids=true | all-gather | bytes 768000 | tf_op jit(solution)/shard_map/all_gather | solution.py:115
  39.0 0.8 copy-done.4
  39.8 0.2 copy.70
  40.1 1.2 %convert_multiply_fusion = f32[8,100,256]{2,1,0:T(8,128)S(1)} fusion(s16[8,100,384]{2,1,0:T(8,128)(2,1)} %copy-done.4, f32[8,100]{1,0:T(8,128)S(1)} %multiply_bitcast_fusion), kind=kLoop, calls=%fused_computation.44 | loop fusion | flops 409600 | bytes 1232000 | tf_op jit(solution)/shard_map/mul | solution.py:116
  41.3 0.2 fusion.55
  41.5 0.2 fusion.54
  41.8 1.9 %fusion.23 = bf16[1024,100]{0,1:T(8,128)(2,1)S(1)} fusion(bf16[2,256,1024]{1,2,0:T(8,128)(2,1)} %copy-done.1, bf16[1,100,256]{2,1,0:T(8,128)(2,1)S(1)} %fusion.54, bf16[1,100,256]{2,1,0:T(8,128)(2,1)S(1)} %fusion.55), kind=kOutput, calls=%fused_computation.34 | convolution fusion | flops 105011200 | bytes 1355776 | tf_op jit(solution)/shard_map/mpd,mvp->dv/dot_general | solution.py:129
  43.7 2.6 %fusion.7 = bf16[2,256,1024]{1,2,0:T(8,128)(2,1)} fusion(f32[2,1024,256]{2,1,0:T(8,128)S(1)} %copy-done.12, bf16[1024,100]{0,1:T(8,128)(2,1)S(1)} %copy-done.9, bf16[1,100,256]{2,1,0:T(8,128)(2,1)S(1)} %fusion.54, bf16[1,100,256]{2,1,0:T(8,128)(2,1)S(1)} %fusion.55), kind=kOutput, calls=%fused_computation.16 | convolution fusion | flops 115394560 | bytes 3452928 | tf_op jit(solution)/shard_map/mvp,dv->mpd/dot_general | solution.py:130
  46.3 0.9 copy.73
  47.2 1.7 %pad.5.clone = bf16[1024,128]{1,0:T(8,128)(2,1)} pad(bf16[1024,100]{1,0:T(8,128)(2,1)} %copy.73, bf16[]{:T(256)} %constant.33.clone.1), padding=0_0x0_28 | pad | bytes 466946 | tf_op jit(solution)/shard_map/jit(_pad)/pad | solution.py:137
  48.9 6.1 %bitcast_convert_fusion = bf16[1024,1024]{1,0:T(8,128)(2,1)} fusion(bf16[2,256,1024]{1,2,0:T(8,128)(2,1)} %fusion.7, f32[2,1024,256]{2,1,0:T(8,128)} %fusion.39, bf16[2,384,1024]{2,1,0:T(8,128)(2,1)} %copy-done.3, bf16[256,384]{1,0:T(8,128)(2,1)S(1)} %bitcast_convert_fusion.1), kind=kOutput, calls=%fused_computation | convolution fusion | flops 1478492160 | bytes 7012352 | tf_op jit(solution)/shard_map/mpd,mpe->de/dot_general | solution.py:134
  55.0 1.8 %fusion.25 = (bf16[2,16,1,16,1152]{4,3,2,1,0:T(8,128)(2,1)S(1)}, bf16[2,16,1,16,1152]{4,3,2,1,0:T(8,128)(2,1)S(1)}) fusion(s32[]{:T(128)S(6)} %select_n.46, bf16[2,16,2,16,1024]{4,3,2,1,0:T(8,128)(2,1)} %bitcast.210, bf16[2,16,2,16,128]{4,3,2,1,0:T(8,128)(2,1)} %bitcast.212, s32[]{:T(128)S(6)} %select_n.47), kind=kLoop, calls=%fused_computation.36 | loop fusion | flops 4718592 | bytes 4718600 | tf_op jit(solution)/shard_map/concatenate | solution.py:136
  56.8 0.1 copy.78
  56.9 0.3 collective-permute-start.5
  57.2 2.8 %collective-permute-done.5 = bf16[2,16,16,1152]{3,2,0,1:T(8,128)(2,1)S(1)} collective-permute-done((bf16[2,16,16,1152]{3,2,0,1:T(8,128)(2,1)S(1)}, bf16[2,16,16,1152]{3,2,0,1:T(8,128)(2,1)S(1)}, u32[]{:S(2)}, u32[]{:S(2)}) %collective-permute-start.5) | collective-permute-done | bytes 1179680 | tf_op jit(solution)/shard_map/ppermute | solution.py:144
  60.1 1.4 %fusion.26 = bf16[16,2,16,1152]{3,2,1,0:T(8,128)(2,1)} fusion(bf16[2,16,16,1152]{3,2,0,1:T(8,128)(2,1)S(1)} %collective-permute-done.5, bf16[2,16,1,16,1152]{4,3,2,1,0:T(8,128)(2,1)S(1)} %get-tuple-element.4), kind=kLoop, calls=%fused_computation.37 | loop fusion | flops 2359296 | bytes 3538944 | tf_op jit(solution)/shard_map/transpose | solution.py:153
  61.4 16.2 %all-to-all-start = ((bf16[16,2,16,1152]{3,2,1,0:T(8,128)(2,1)}), bf16[16,2,16,1152]{3,2,1,0:T(8,128)(2,1)}, u32[]{:S(2)}, u32[]{:S(2)}) async-start(bf16[16,2,16,1152]{3,2,1,0:T(8,128)(2,1)} %fusion.26), calls=%async_computation | async-start | bytes 2359296 | tf_op jit(solution)/shard_map/all_to_all | solution.py:154
  77.6 2.0 %fusion.45 = f32[2,1024,384]{2,1,0:T(8,128)S(1)} fusion(bf16[2,256,1024]{1,2,0:T(8,128)(2,1)} %fusion.7, bf16[256,384]{1,0:T(8,128)(2,1)S(1)} %bitcast_convert_fusion.1), kind=kOutput, calls=%fused_computation.63 | convolution fusion | flops 402653184 | bytes 4390912 | tf_op jit(solution)/shard_map/pr,mpd->mrd/dot_general | solution.py:146
  79.6 2.4 %fusion.63 = (bf16[2,384,1024]{1,2,0:T(8,128)(2,1)S(1)}, f32[2,384,1024]{1,2,0:T(8,128)}) fusion(f32[2,1024,384]{2,1,0:T(8,128)S(1)} %fusion.45, bf16[2,256,1024]{1,2,0:T(8,128)(2,1)S(1)} %copy-done.2, bf16[256,384]{1,0:T(8,128)(2,1)S(1)} %fusion.33), kind=kOutput, calls=%fused_computation.110 | convolution fusion | flops 404226048 | bytes 9109504 | tf_op jit(solution)/shard_map/pr,mpd->mrd/dot_general | solution.py:148
  82.0 1.1 fusion.62
  83.1 2.3 %collective-permute-start.4 = (bf16[2,128,1024]{1,2,0:T(8,128)(2,1)}, bf16[2,128,1024]{1,2,0:T(8,128)(2,1)}, u32[]{:S(2)}, u32[]{:S(2)}) collective-permute-start(bf16[2,128,1024]{1,2,0:T(8,128)(2,1)} %get-tuple-element.7), channel_id=1, source_target_pairs={{1,2},{2,1},{3,4},{4,3},{5,6},{6,5},{7,8},{8,7},{9,10},{10,9},{11,... | collective-permute-start | bytes 1572872 | tf_op jit(solution)/shard_map/ppermute | solution.py:156
  85.4 1.5 %collective-permute-start.3 = (bf16[2,128,1024]{1,2,0:T(8,128)(2,1)}, bf16[2,128,1024]{1,2,0:T(8,128)(2,1)}, u32[]{:S(2)}, u32[]{:S(2)}) collective-permute-start(bf16[2,128,1024]{1,2,0:T(8,128)(2,1)} %get-tuple-element.7), channel_id=1, source_target_pairs={{0,63},{31,32},{32,31},{63,0},{64,127},{95,96},{96,95},{127,64},{1... | collective-permute-start | bytes 1572872 | tf_op jit(solution)/shard_map/ppermute | solution.py:150
  86.9 9.5 %all-to-all-done = bf16[16,2,16,1152]{3,2,1,0:T(8,128)(2,1)} async-done(((bf16[16,2,16,1152]{3,2,1,0:T(8,128)(2,1)}), bf16[16,2,16,1152]{3,2,1,0:T(8,128)(2,1)}, u32[]{:S(2)}, u32[]{:S(2)}) %all-to-all-start) | async-done | bytes 1179680 | tf_op jit(solution)/shard_map/all_to_all | solution.py:154
  96.4 1.4 %reduce_sum.21 = bf16[2,16,1152]{2,1,0:T(8,128)(2,1)S(1)} reduce(bf16[16,2,16,1152]{3,2,1,0:T(8,128)(2,1)} %all-to-all-done, bf16[]{:T(256)} %constant.33.clone.1), dimensions={0}, to_apply=%region_1.2 | reduce | flops 552960 | bytes 1253378 | tf_op jit(solution)/shard_map/reduce_sum | solution.py:155
  97.8 0.7 broadcast_in_dim.53
  98.6 6.1 %all-to-all-start.1 = ((bf16[8,16,1152]{2,1,0:T(8,128)(2,1)}), bf16[8,16,1152]{2,1,0:T(8,128)(2,1)S(1)}, u32[]{:S(2)}, u32[]{:S(2)}) async-start(bf16[8,16,1152]{2,1,0:T(8,128)(2,1)} %bitcast.29), calls=%async_computation.1 | async-start | bytes 589824 | tf_op jit(solution)/shard_map/all_to_all | solution.py:159
  104.7 2.0 %multiply_subtract_fusion = f32[100,256]{1,0:T(8,128)} fusion(f32[100,256]{1,0:T(8,128)S(1)} %copy-done.7, f32[8,100,256]{2,1,0:T(8,128)S(1)} %convert_multiply_fusion), kind=kLoop, calls=%fused_computation.86 | loop fusion | flops 3712000 | bytes 1024000 | tf_op jit(solution)/shard_map/sub | solution.py:48
  106.7 3.3 %fusion.20 = bf16[2,128,1024]{2,1,0:T(8,128)(2,1)} fusion(bf16[1024,1024]{1,0:T(8,128)(2,1)S(1)} %copy-done, f32[2,384,1024]{1,2,0:T(8,128)} %get-tuple-element.15, bf16[2,128,1024]{1,2,0:T(8,128)(2,1)} %collective-permute-done.4, bf16[2,128,1024]{1,2,0:T(8,128)(2,1)} %collective-permute-done.3, bf16[2,128,1024]{1,2,0:T(8,128)(2,1)} %collective-permute-done.2), kind=kOutput, calls=%fused_computation.32 | convolution fusion | flops 538968064 | bytes 5242880 | tf_op jit(solution)/shard_map/mne,de->mnd/dot_general | solution.py:168
  110.0 5.6 %all-to-all-done.1 = bf16[8,16,1152]{2,1,0:T(8,128)(2,1)S(1)} async-done(((bf16[8,16,1152]{2,1,0:T(8,128)(2,1)}), bf16[8,16,1152]{2,1,0:T(8,128)(2,1)S(1)}, u32[]{:S(2)}, u32[]{:S(2)}) %all-to-all-start.1) | async-done | bytes 294944 | tf_op jit(solution)/shard_map/all_to_all | solution.py:159
  115.6 0.6 slice.87
  116.2 0.6 slice.86
  (37 shorter events, 0.3 us)
Async XLA Ops:
  0.6 10.7 %copy-start = (bf16[1024,1024]{1,0:T(8,128)(2,1)S(1)}, bf16[1024,1024]{1,0:T(8,128)(2,1)}, u32[]{:S(2)}) copy-start(bf16[1024,1024]{1,0:T(8,128)(2,1)} %param.11) | copy-start | bytes 6291460
  0.6 5.1 %copy-start.5 = (bf16[2,128,1024]{2,1,0:T(8,128)(2,1)S(1)}, bf16[2,128,1024]{2,1,0:T(8,128)(2,1)}, u32[]{:S(2)}) copy-start(bf16[2,128,1024]{2,1,0:T(8,128)(2,1)} %param.10) | copy-start | bytes 1572868
  0.7 5.2 %collective-permute-start = (bf16[2,128,1024]{2,1,0:T(8,128)(2,1)}, bf16[2,128,1024]{2,1,0:T(8,128)(2,1)}, u32[]{:S(2)}, u32[]{:S(2)}) collective-permute-start(bf16[2,128,1024]{2,1,0:T(8,128)(2,1)} %param.10), channel_id=1, source_target_pairs={{0,1},{1,0},{2,3},{3,2},{4,5},{5,4},{6,7},{7,6},{8,9},{9,8},{10,11... | collective-permute-start | bytes 1572872 | tf_op jit(solution)/shard_map/ppermute | solution.py:80
  0.8 9.5 %collective-permute-start.1 = (bf16[2,128,1024]{2,1,0:T(8,128)(2,1)}, bf16[2,128,1024]{2,1,0:T(8,128)(2,1)}, u32[]{:S(2)}, u32[]{:S(2)}) collective-permute-start(bf16[2,128,1024]{2,1,0:T(8,128)(2,1)} %param.10), channel_id=1, source_target_pairs={{0,63},{1,2},{2,1},{3,4},{4,3},{5,6},{6,5},{7,8},{8,7},{9,10},{10,... | collective-permute-start | bytes 1572872 | tf_op jit(solution)/shard_map/ppermute | solution.py:79
  11.3 1.8 %copy-start.3 = (bf16[2,384,1024]{2,1,0:T(8,128)(2,1)}, bf16[2,384,1024]{2,1,0:T(8,128)(2,1)S(1)}, u32[]{:S(2)}) copy-start(bf16[2,384,1024]{2,1,0:T(8,128)(2,1)S(1)} %constant_dynamic-update-slice_fusion) | copy-start | bytes 4718596
  16.0 3.6 %copy-start.8 = (bf16[1024,100]{0,1:T(8,128)(2,1)S(1)}, bf16[1024,100]{0,1:T(8,128)(2,1)}, u32[]{:S(2)}) copy-start(bf16[1024,100]{0,1:T(8,128)(2,1)} %param.12) | copy-start | bytes 614404
  18.6 1.0 copy-start.1
  19.6 21.7 %copy-start.6 = (f32[100,256]{1,0:T(8,128)S(1)}, f32[100,256]{1,0:T(8,128)}, u32[]{:S(2)}) copy-start(f32[100,256]{1,0:T(8,128)} %param.13) | copy-start | bytes 307204
  19.6 21.7 %copy-start.10 = (f32[256]{0:T(256)S(1)}, f32[256]{0:T(256)}, u32[]{:S(2)}) copy-start(f32[256]{0:T(256)} %param.14) | copy-start | bytes 3076
  19.6 21.7 %copy-start.11 = (f32[100]{0:T(128)S(1)}, f32[100]{0:T(128)}, u32[]{:S(2)}) copy-start(f32[100]{0:T(128)} %param.15) | copy-start | bytes 1204
  39.0 0.8 copy-start.4
  41.3 2.4 %copy-start.9 = (bf16[1024,100]{0,1:T(8,128)(2,1)S(1)}, bf16[1024,100]{0,1:T(8,128)(2,1)}, u32[]{:S(2)}) copy-start(bf16[1024,100]{0,1:T(8,128)(2,1)} %param.12) | copy-start | bytes 614404
  41.3 2.4 %copy-start.12 = (f32[2,1024,256]{2,1,0:T(8,128)S(1)}, f32[2,1024,256]{2,1,0:T(8,128)}, u32[]{:S(2)}) copy-start(f32[2,1024,256]{2,1,0:T(8,128)} %get-tuple-element.11) | copy-start | bytes 6291460
  56.9 3.1 %collective-permute-start.5 = (bf16[2,16,16,1152]{3,2,0,1:T(8,128)(2,1)S(1)}, bf16[2,16,16,1152]{3,2,0,1:T(8,128)(2,1)S(1)}, u32[]{:S(2)}, u32[]{:S(2)}) collective-permute-start(bf16[2,16,16,1152]{3,2,0,1:T(8,128)(2,1)S(1)} %bitcast.211), channel_id=1, source_target_pairs={{0,1},{1,0},{2,3},{3,2},{4,5},{5,4},{6,7},{7,6},{8,9},{9,8},{10,11... | collective-permute-start | bytes 3538952 | tf_op jit(solution)/shard_map/ppermute | solution.py:144
  61.4 35.0 %all-to-all-start = ((bf16[16,2,16,1152]{3,2,1,0:T(8,128)(2,1)}), bf16[16,2,16,1152]{3,2,1,0:T(8,128)(2,1)}, u32[]{:S(2)}, u32[]{:S(2)}) async-start(bf16[16,2,16,1152]{3,2,1,0:T(8,128)(2,1)} %fusion.26), calls=%async_computation | async-start | bytes 2359296 | tf_op jit(solution)/shard_map/all_to_all | solution.py:154
  77.6 2.0 %copy-start.2 = (bf16[2,256,1024]{1,2,0:T(8,128)(2,1)S(1)}, bf16[2,256,1024]{1,2,0:T(8,128)(2,1)}, u32[]{:S(2)}) copy-start(bf16[2,256,1024]{1,2,0:T(8,128)(2,1)} %fusion.7) | copy-start | bytes 3145732
  82.0 22.7 %copy-start.7 = (f32[100,256]{1,0:T(8,128)S(1)}, f32[100,256]{1,0:T(8,128)}, u32[]{:S(2)}) copy-start(f32[100,256]{1,0:T(8,128)} %param.13) | copy-start | bytes 307204
  83.1 23.6 %collective-permute-start.2 = (bf16[2,128,1024]{1,2,0:T(8,128)(2,1)}, bf16[2,128,1024]{1,2,0:T(8,128)(2,1)}, u32[]{:S(2)}, u32[]{:S(2)}) collective-permute-start(bf16[2,128,1024]{1,2,0:T(8,128)(2,1)} %get-tuple-element.6), channel_id=1, source_target_pairs={{0,1},{1,0},{2,3},{3,2},{4,5},{5,4},{6,7},{7,6},{8,9},{9,8},{10,11... | collective-permute-start | bytes 1572872 | tf_op jit(solution)/shard_map/ppermute | solution.py:157
  83.1 23.6 %collective-permute-start.4 = (bf16[2,128,1024]{1,2,0:T(8,128)(2,1)}, bf16[2,128,1024]{1,2,0:T(8,128)(2,1)}, u32[]{:S(2)}, u32[]{:S(2)}) collective-permute-start(bf16[2,128,1024]{1,2,0:T(8,128)(2,1)} %get-tuple-element.7), channel_id=1, source_target_pairs={{1,2},{2,1},{3,4},{4,3},{5,6},{6,5},{7,8},{8,7},{9,10},{10,9},{11,... | collective-permute-start | bytes 1572872 | tf_op jit(solution)/shard_map/ppermute | solution.py:156
  85.4 21.3 %collective-permute-start.3 = (bf16[2,128,1024]{1,2,0:T(8,128)(2,1)}, bf16[2,128,1024]{1,2,0:T(8,128)(2,1)}, u32[]{:S(2)}, u32[]{:S(2)}) collective-permute-start(bf16[2,128,1024]{1,2,0:T(8,128)(2,1)} %get-tuple-element.7), channel_id=1, source_target_pairs={{0,63},{31,32},{32,31},{63,0},{64,127},{95,96},{96,95},{127,64},{1... | collective-permute-start | bytes 1572872 | tf_op jit(solution)/shard_map/ppermute | solution.py:150
  98.6 17.0 %all-to-all-start.1 = ((bf16[8,16,1152]{2,1,0:T(8,128)(2,1)}), bf16[8,16,1152]{2,1,0:T(8,128)(2,1)S(1)}, u32[]{:S(2)}, u32[]{:S(2)}) async-start(bf16[8,16,1152]{2,1,0:T(8,128)(2,1)} %bitcast.29), calls=%async_computation.1 | async-start | bytes 589824 | tf_op jit(solution)/shard_map/all_to_all | solution.py:159

commit v2 on v1

v2 whole, which is shorter than its diff:
```python
import functools
import math

import jax
import jax.numpy as jnp
from jax import lax
from jax.experimental import pallas as pl
from jax.experimental.pallas import tpu as pltpu
from jax.sharding import PartitionSpec as P

HALO = 128
BLK = 128
ALPHA = 0.95
DELTA = 0.05
SPACE = ("zhi", "x", "y", "core")
QMAX = 32000.0
VPAD = 128
VROWS = 112
VUSE = 104
TILE = 256
GELU_C = math.sqrt(2.0 / math.pi)
MIB = 1 << 20
F32 = jnp.float32
BF16 = jnp.bfloat16


def dot(a, b):
    return jnp.dot(a, b, preferred_element_type=F32)


def dot_nt(a, b):
    return lax.dot_general(a, b, (((1,), (1,)), ((), ())), preferred_element_type=F32)


def vmem(count):
    return [pl.BlockSpec(memory_space=pltpu.VMEM)] * count


def smem(count):
    return [pl.BlockSpec(memory_space=pltpu.SMEM)] * count


def cost(flops, nbytes):
    return pl.CostEstimate(flops=flops, bytes_accessed=nbytes, transcendentals=0)


def params(mib):
    return pltpu.CompilerParams(vmem_limit_bytes=mib * MIB)


def pair_factor(members):
    fair_eps = (1.0 - ALPHA) / members
    return (1.0 - fair_eps) / (2.0 * members * (members - 1))


def smooth_abs(distance):
    return jnp.sqrt(distance * distance + DELTA * DELTA)


def signum(distance):
    return distance * lax.rsqrt(distance * distance + DELTA * DELTA)


def prepare_kernel(
    where_ref, count_ref, src_ref, dst_ref, wt_ref, lat_ref, clat_ref, w_ref,
    cf_ref, cfo_ref, cft_ref, part_ref, x_ref,
):
    core = where_ref[0]
    slots = src_ref.shape[1]
    window = cf_ref.shape[1] // 2
    points = cf_ref.shape[0]
    for b in range(src_ref.shape[0]):
        src = src_ref[b : b + 1, :]
        slot = lax.broadcasted_iota(jnp.int32, (1, slots), 1)
        wt = jnp.where(slot < count_ref[b], wt_ref[b : b + 1, :], 0.0)
        left = 2 * HALO - HALO * core
        right = HALO + HALO * core
        place = jnp.where(
            src < HALO,
            src + left,
            jnp.where(src < 2 * HALO, src - HALO, src - 2 * HALO + right),
        )
        rows = lax.broadcasted_iota(jnp.int32, (window, slots), 0)
        hot = jnp.where(rows == place, 1.0, 0.0).astype(BF16)
        pts = lax.broadcasted_iota(jnp.int32, (BLK, slots), 0)
        mat = jnp.where(pts == dst_ref[b : b + 1, :], wt, 0.0).astype(BF16)
        coef = dot_nt(mat, hot)
        high = coef.astype(BF16)
        low = (coef - high.astype(F32)).astype(BF16)
        at = slice(b * BLK, (b + 1) * BLK)
        cf_ref[at, :window] = high
        cf_ref[at, window:] = low
        cfo_ref[at, :HALO] = high[:, 2 * HALO :]
        cfo_ref[at, HALO:] = low[:, 2 * HALO :]
        coef_t = dot_nt(hot, mat)
        high_t = coef_t.astype(BF16)
        cft_ref[:, b * BLK : (b + 1) * BLK] = high_t
        cft_ref[:, points + b * BLK : points + (b + 1) * BLK] = (
            coef_t - high_t.astype(F32)
        ).astype(BF16)
    local = lat_ref.shape[0]
    for m in range(local):
        x_ref[2 * m * HALO : (2 * m + 1) * HALO, :] = lat_ref[m]
        x_ref[(2 * m + 1) * HALO : (2 * m + 2) * HALO, :] = clat_ref[m]
    x = x_ref[...]
    high = cf_ref[:, : 2 * HALO]
    low = cf_ref[:, window : window + 2 * HALO]
    for j in range(w_ref.shape[1] // TILE):
        at = slice(j * TILE, (j + 1) * TILE)
        p = dot(x, w_ref[:, at]).astype(BF16)
        for m in range(local):
            pm = p[2 * m * HALO : (2 * m + 2) * HALO]
            part_ref[m, :, at] = dot(high, pm) + dot(low, pm)


def forward_kernel(
    odd_ref, w_ref, cfo_ref, part_ref, dpt_ref, summed_ref, hidden_ref, coded_ref, f_ref
):
    j = pl.program_id(0)
    local = part_ref.shape[0]

    @pl.when(j == 0)
    def _():
        f_ref[...] = jnp.zeros_like(f_ref)

    p = dot(odd_ref[...], w_ref[...]).astype(BF16)
    for m in range(local):
        pm = p[m * HALO : (m + 1) * HALO]
        s = part_ref[m] + dot(cfo_ref[...], jnp.concatenate([pm, pm], axis=0))
        summed_ref[m] = s
        t = jnp.tanh(GELU_C * (s + 0.044715 * (s * s * s)))
        h = (0.5 * s * (1.0 + t)).astype(BF16)
        hidden_ref[m] = h
        f_ref[m] += dot_nt(dpt_ref[...], h)

    @pl.when(j == pl.num_programs(0) - 1)
    def _():
        for m in range(local):
            f = f_ref[m]
            largest = jnp.maximum(jnp.max(jnp.abs(f), axis=1, keepdims=True), 1e-30)
            power = jnp.ceil(jnp.log(largest) * (1.0 / math.log(2.0)) + 1e-3)
            power = jnp.broadcast_to(power, (VPAD, VPAD))
            q = f * (jnp.exp2(-power[:, :1]) * QMAX)
            q = jnp.where(q >= 0.0, q + 0.5, q - 0.5)
            row = jnp.concatenate([power.T[:8], jnp.zeros((8, f.shape[1] - VPAD), F32)], axis=1)
            row = jnp.where(row >= 0.0, row + 0.5, row - 0.5)
            code = jnp.concatenate([q[:VUSE], row], axis=0).astype(jnp.int32).astype(jnp.int16)
            for e in range(coded_ref.shape[0]):
                coded_ref[e, m] = code


def factors_kernel(
    where_ref, lat_ref, clat_ref, olat_ref, cf_ref, summed_ref, hidden_ref,
    aggt_ref, hidt_ref, slope_ref, x_ref,
):
    core = where_ref[0]
    window = cf_ref.shape[1] // 2
    depth = lat_ref.shape[2]
    local = lat_ref.shape[0]
    points = cf_ref.shape[0]
    high = cf_ref[:, :window]
    low = cf_ref[:, window:]
    for m in range(local):
        x_ref[:HALO] = lat_ref[m]
        x_ref[HALO : 2 * HALO] = clat_ref[m]
        x_ref[2 * HALO :] = olat_ref[m * HALO : (m + 1) * HALO]
        cols = slice(m * points, (m + 1) * points)
        for j in range(depth // TILE):
            at = slice(j * TILE, (j + 1) * TILE)
            x = x_ref[:, at]
            agg = (dot(high, x) + dot(low, x)).T.astype(BF16)
            hid = hidden_ref[m, :, at].astype(F32).T.astype(BF16)
            for k in range(TILE // 16):
                block = j * (TILE // 16) + k
                zhi, rest = divmod(block, 32)
                xy, c = divmod(rest, 2)
                to = lax.bitwise_xor(core, c) * (depth // 2) + (xy * 32 + zhi * 16)
                to = pl.ds(pl.multiple_of(to, 16), 16)
                aggt_ref[to, cols] = agg[k * 16 : (k + 1) * 16]
                hidt_ref[to, cols] = hid[k * 16 : (k + 1) * 16]
            s = summed_ref[m, :, at]
            t = jnp.tanh(GELU_C * (s + 0.044715 * (s * s * s)))
            slope_ref[m, :, at] = 0.5 * (1.0 + t) + (0.5 * GELU_C) * s * (1.0 - t * t) * (
                1.0 + 3.0 * 0.044715 * (s * s)
            )


def decode(code_ref, index):
    code = code_ref[index].astype(jnp.int32).astype(F32)
    power = jnp.broadcast_to(code[VUSE : VUSE + 1, :VPAD], (VPAD, VPAD)).T
    return code[:VUSE] * (jnp.exp2(power[:VUSE, :1]) * (1.0 / QMAX))


def score_kernel(code_ref, truth_ref, score_ref):
    members = code_ref.shape[0]
    nvar = truth_ref.shape[0]
    collected = [decode(code_ref, m)[:nvar] for m in range(members)]
    truth = truth_ref[...]
    skill = sum(smooth_abs(f - truth) for f in collected)
    spread = jnp.zeros_like(skill)
    for m in range(members):
        for o in range(m + 1, members):
            spread = spread + smooth_abs(collected[m] - collected[o])
    score_ref[...] = skill * (1.0 / members) - (pair_factor(members) * 2.0) * spread


def backward_kernel(
    where_ref, code_ref, truth_ref, var_ref, area_ref, dpt_ref, aggt_ref, hidt_ref, slope_ref,
    mine_ref, theirs_ref, sg_ref, f_ref, sgs_ref,
):
    members = code_ref.shape[0]
    local = slope_ref.shape[0]
    points = slope_ref.shape[1]
    depth = slope_ref.shape[2]
    half = depth // 2
    for m in range(members):
        f_ref[m] = decode(code_ref, m)
    first = where_ref[1] * local
    truth = truth_ref[...]
    multiplier = var_ref[...] * area_ref[...]
    grads = []
    for m in range(local):
        own = f_ref[first + m]
        mutual = sum(signum(own - f_ref[o]) for o in range(members))
        g = multiplier * (
            signum(own - truth) * (1.0 / members) - (2.0 * pair_factor(members)) * mutual
        )
        g = jnp.concatenate([g, jnp.zeros((VPAD - VUSE, points), F32)], axis=0)
        grads.append(g.T.astype(BF16))
    grad = jnp.concatenate(grads, axis=0)
    out = dot(hidt_ref[...], grad).astype(BF16)
    mine_ref[:, depth:] = out[:half]
    theirs_ref[:, depth:] = out[half:]
    aggt = aggt_ref[...]
    for j in range(depth // TILE):
        at = slice(j * TILE, (j + 1) * TILE)
        hg = dot(grad, dpt_ref[:, at])
        for m in range(local):
            s = (hg[m * points : (m + 1) * points] * slope_ref[m, :, at]).astype(BF16)
            sg_ref[m, :, at] = s
            sgs_ref[m * points : (m + 1) * points, :] = s
        part = dot(aggt, sgs_ref[...]).astype(BF16)
        mine_ref[:, at] = part[:half]
        theirs_ref[:, at] = part[half:]


def rows_kernel(cft_ref, sg_ref, own_ref, core_ref, odd_ref):
    points = sg_ref.shape[1]
    high = cft_ref[:, :points]
    low = cft_ref[:, points:]
    for m in range(sg_ref.shape[0]):
        for j in range(sg_ref.shape[2] // TILE):
            at = slice(j * TILE, (j + 1) * TILE)
            s = sg_ref[m, :, at]
            g = dot(high, s) + dot(low, s)
            own_ref[m, :, at] = g[:HALO]
            core_ref[m, :, at] = g[HALO : 2 * HALO].astype(BF16)
            odd_ref[m, :, at] = g[2 * HALO :].astype(BF16)


def plane_kernel(got_ref, out_ref):
    ens = out_ref.shape[1]
    per = out_ref.shape[2]
    total = got_ref[0].astype(F32)
    for k in range(1, got_ref.shape[0]):
        total = total + got_ref[k].astype(F32)
    total = total.astype(BF16)
    for z in range(out_ref.shape[0]):
        for e in range(ens):
            out_ref[z, e] = total[z * per : (z + 1) * per]


def final_kernel(got_ref, src_ref, out_ref, *, scaling):
    total = got_ref[0].astype(F32)
    for k in range(1, got_ref.shape[0]):
        total = total + got_ref[k].astype(F32)
    total = total * scaling
    depth = src_ref.shape[1]
    src_ref[...] = total[:, :depth]
    out_ref[...] = total[:, depth : depth + out_ref.shape[1]]


def latent_kernel(own_ref, core_ref, far_ref, near_ref, w_ref, out_ref, g_ref):
    local = own_ref.shape[0]
    for m in range(local):
        g = (
            own_ref[m]
            + core_ref[m].astype(F32)
            + far_ref[m].astype(F32)
            + near_ref[m].astype(F32)
        )
        g_ref[m * HALO : (m + 1) * HALO] = g.astype(BF16)
    for j in range(w_ref.shape[0] // TILE):
        at = slice(j * TILE, (j + 1) * TILE)
        r = dot_nt(g_ref[...], w_ref[at, :]).astype(BF16)
        for m in range(local):
            out_ref[m, :, at] = r[m * HALO : (m + 1) * HALO]


def shape(dims, dtype):
    return jax.ShapeDtypeStruct(dims, dtype)


def make_body(count):
    odd_pairs = [(i, (i + 1) % count if i % 2 else (i - 1) % count) for i in range(count)]
    far = [p for p in odd_pairs if abs(p[0] - p[1]) > 1 or p[0] // 32 != p[1] // 32]
    near = [p for p in odd_pairs if p not in far]
    swap = [(0, 1), (1, 0)]

    def body(
        latent, src_weight, decoder_projection, truth, area_weight, var_weight,
        edge_src, edge_dst, edge_weight, edge_count,
    ):
        local, rows, depth = latent.shape
        ens = lax.axis_size("ens")
        members = local * ens
        nvar = decoder_projection.shape[1]
        points = truth.shape[1]
        window = rows + 2 * HALO
        per = depth // count
        cols = depth + VPAD
        where = jnp.stack([lax.axis_index("core"), lax.axis_index("ens")]).astype(jnp.int32)

        odd_lat = lax.ppermute(latent, SPACE, odd_pairs).reshape(local * rows, depth)
        core_lat = lax.ppermute(latent, "core", swap)
        dpt = jnp.pad(decoder_projection.T, ((0, VPAD - nvar), (0, 0)))

        cf, cfo, cft, part = pl.pallas_call(
            prepare_kernel,
            out_shape=(
                shape((points, 2 * window), BF16),
                shape((points, 2 * HALO), BF16),
                shape((window, 2 * points), BF16),
                shape((local, points, depth), F32),
            ),
            in_specs=smem(2) + vmem(6),
            out_specs=tuple(vmem(4)),
            scratch_shapes=[pltpu.VMEM((local * 2 * HALO, depth), BF16)],
            compiler_params=params(24),
            cost_estimate=cost(3 * 10**9, 6 * 10**6),
            name="prepare",
        )(where, edge_count, edge_src, edge_dst, edge_weight, latent, core_lat, src_weight)

        steps = depth // TILE
        summed, hidden, coded = pl.pallas_call(
            forward_kernel,
            grid=(steps,),
            out_shape=(
                shape((local, points, depth), F32),
                shape((local, points, depth), BF16),
                shape((ens, local, VROWS, points), jnp.int16),
            ),
            in_specs=[
                pl.BlockSpec((local * rows, depth), lambda j: (0, 0)),
                pl.BlockSpec((depth, TILE), lambda j: (0, j)),
                pl.BlockSpec((points, 2 * HALO), lambda j: (0, 0)),
                pl.BlockSpec((local, points, TILE), lambda j: (0, 0, j)),
                pl.BlockSpec((VPAD, TILE), lambda j: (0, j)),
            ],
            out_specs=(
                pl.BlockSpec((local, points, TILE), lambda j: (0, 0, j)),
                pl.BlockSpec((local, points, TILE), lambda j: (0, 0, j)),
                pl.BlockSpec((ens, local, VROWS, points), lambda j: (0, 0, 0, 0)),
            ),
            scratch_shapes=[pltpu.VMEM((local, VPAD, points), F32)],
            compiler_params=params(24),
            cost_estimate=cost(2 * 10**9, 8 * 10**6),
            name="forward",
        )(odd_lat, src_weight, cfo, part, dpt)

        everyone = lax.all_to_all(coded, "ens", 0, 0, tiled=True)
        everyone = everyone.reshape(members, VROWS, points)

        aggt, hidt, slope = pl.pallas_call(
            factors_kernel,
            out_shape=(
                shape((depth, local * points), BF16),
                shape((depth, local * points), BF16),
                shape((local, points, depth), F32),
            ),
            in_specs=smem(1) + vmem(6),
            out_specs=tuple(vmem(3)),
            scratch_shapes=[pltpu.VMEM((window, depth), BF16)],
            compiler_params=params(24),
            cost_estimate=cost(3 * 10**9, 10 * 10**6),
            name="factors",
        )(where, latent, core_lat, odd_lat, cf, summed, hidden)

        tall = jnp.pad(truth, ((0, VUSE - nvar), (0, 0)))
        var_col = jnp.pad(var_weight, (0, VUSE - nvar)).reshape(VUSE, 1)
        mine, theirs, summed_grad = pl.pallas_call(
            backward_kernel,
            out_shape=(
                shape((depth // 2, cols), BF16),
                shape((depth // 2, cols), BF16),
                shape((local, points, depth), BF16),
            ),
            in_specs=smem(1) + vmem(8),
            out_specs=tuple(vmem(3)),
            scratch_shapes=[
                pltpu.VMEM((members, VUSE, points), F32),
                pltpu.VMEM((local * points, TILE), BF16),
            ],
            compiler_params=params(24),
            cost_estimate=cost(2 * 10**9, 8 * 10**6),
            name="backward",
        )(
            where, everyone, tall, var_col, area_weight.reshape(1, points), dpt,
            aggt, hidt, slope,
        )

        theirs = lax.ppermute(theirs, "core", swap)
        own_rows, core_send, odd_send = pl.pallas_call(
            rows_kernel,
            out_shape=(
                shape((local, rows, depth), F32),
                shape((local, HALO, depth), BF16),
                shape((local, HALO, depth), BF16),
            ),
            in_specs=vmem(2),
            out_specs=tuple(vmem(3)),
            compiler_params=params(16),
            cost_estimate=cost(10**9, 4 * 10**6),
            name="rows",
        )(cft, summed_grad)
        far_grad = lax.ppermute(odd_send, SPACE, far)

        half = (mine.astype(F32) + theirs.astype(F32)).astype(BF16).reshape(16, 2 * per, cols)
        got = lax.all_to_all(half, ("x", "y"), 0, 0, tiled=True)
        near_grad = lax.ppermute(odd_send, SPACE, near)
        core_grad = lax.ppermute(core_send, "core", swap)
        plane = pl.pallas_call(
            plane_kernel,
            out_shape=shape((2, ens, per, cols), BF16),
            in_specs=vmem(1),
            out_specs=vmem(1)[0],
            compiler_params=params(16),
            cost_estimate=cost(10**6, 2 * 10**6),
            name="plane",
        )(got)
        got = lax.all_to_all(plane.reshape(2 * ens, per, cols), ("zhi", "ens"), 0, 0, tiled=True)

        score = pl.pallas_call(
            score_kernel,
            out_shape=shape(truth.shape, F32),
            in_specs=vmem(2),
            out_specs=vmem(1)[0],
            compiler_params=params(16),
            cost_estimate=cost(10**7, 10**6),
            name="score",
        )(everyone, truth)
        grad_latent = pl.pallas_call(
            latent_kernel,
            out_shape=shape(latent.shape, BF16),
            in_specs=vmem(5),
            out_specs=vmem(1)[0],
            scratch_shapes=[pltpu.VMEM((local * rows, depth), BF16)],
            compiler_params=params(16),
            cost_estimate=cost(10**9, 5 * 10**6),
            name="latent",
        )(own_rows, core_grad, far_grad, near_grad, src_weight)

        grad_src, grad_out = pl.pallas_call(
            functools.partial(
                final_kernel, scaling=1.0 / math.sqrt(members * points * count)
            ),
            out_shape=(shape((per, depth), F32), shape((per, nvar), F32)),
            in_specs=vmem(1),
            out_specs=tuple(vmem(2)),
            compiler_params=params(16),
            cost_estimate=cost(10**5, 4 * 10**5),
            name="final",
        )(got)
        return score, grad_latent, grad_src, grad_out

    return body


def solution(mesh):
    fine = jax.sharding.Mesh(
        mesh.devices.reshape(mesh.devices.shape[0], 2, 4, 4, 2), ("ens",) + SPACE
    )
    return jax.shard_map(
        make_body(mesh.devices.shape[1]),
        mesh=fine,
        in_specs=(
            P("ens", SPACE, None), P(), P(), P(None, SPACE), P(SPACE), P(),
            P(SPACE, None), P(SPACE, None), P(SPACE, None), P(SPACE),
        ),
        out_specs=(P(None, SPACE), P("ens", SPACE, None), P(SPACE, None), P(SPACE, None)),
        check_vma=False,
    )
```

time: 118 us -> 111 us (0.941)
  Pallas kernels: 0 us -> 27.4 us
  matrix products: 27.1 us -> 0 us
  local copies, waits for them, and re-layouts: 10.1 us -> 29.7 us
  blocking collectives: 18.7 us -> 0 us
  other arithmetic: 10 us -> 1.43 us
  starting transfers between devices: 28.7 us -> 34.3 us
  waiting for transfers between devices: 21.2 us -> 16 us
    pallas_call x0 -> x9, Pallas kernels: none -> 27.4 us  [the longest x1 6.76 us: body(): pl.pallas_call(forward_kernel, grid=(steps,), out_shape=(shape((local, po...]
    dot_general x12 -> x0, matrix products: 27.1 us -> none  [the longest x1 6.12 us: body(): jnp.einsum('mpd,mpe->de', agg, summed_grad, preferred_element_type=jnp.fl...]
    unnamed x31 -> x68, local copies, waits for them, and re-layouts: 4.12 us -> 28.7 us
    all_gather x1 -> x0, blocking collectives: 18.7 us -> none  [body(): everyone = lax.all_gather(coded, 'ens', axis=0, tiled=True)]
    all_to_all x1 -> x2, starting transfers between devices: 6.1 us -> 15.1 us  [the longest x1 10.5 us: body(): lax.all_to_all(plane.reshape(2 * ens, per, cols), ('zhi', 'ens'), 0, 0, t...]
    ppermute x4, waiting for transfers between devices: 3.29 us -> 0.01 us  [the longest x1 0.01 us: body(): lax.ppermute(latent, SPACE, odd_pairs).reshape(local * rows, depth)]
    all_to_all x1, starting transfers between devices: 16.2 us -> 13.2 us  [body(): got = lax.all_to_all(half, ('x', 'y'), 0, 0, tiled=True)]
    slice x4 -> x0, local copies, waits for them, and re-layouts: 2.4 us -> none  [the longest x2 1.23 us: body(): return (score, grad_latent, total[:, :depth], total[:, depth:depth + nvar])]
  transfers between devices with their start and end apart: 8 -> 9, of which waited for: 4 -> 4; matrix products, arithmetic and copies ran while one was open for 14% -> 1% of each run, Pallas kernels for 0% -> 15%
where the time goes in v2:
time: 111 us; the launch traced here: 110 us
  starting transfers between devices  34.3 us (31%)
  local copies, waits for them, and re-layouts  29.7 us (27%)
  Pallas kernels  27.4 us (25%)
  waiting for transfers between devices  16 us (14%)
  other arithmetic  1.43 us (1%)
    unnamed x68, local copies, waits for them, and re-layouts  28.7 us
    all_to_all x1, starting transfers between devices, body(): got = lax.all_to_all(half, ('x', 'y'), 0, 0, tiled=True)  13.2 us
    all_to_all x1, starting transfers between devices, body(): lax.all_to_all(plane.reshape(2 * ens, per, cols), ('zhi', 'ens'), 0, 0, t...  10.5 us
    all_to_all x1, waiting for transfers between devices, body(): got = lax.all_to_all(half, ('x', 'y'), 0, 0, tiled=True)  9.91 us
    pallas_call x1, Pallas kernels, body(): pl.pallas_call(forward_kernel, grid=(steps,), out_shape=(shape((local, po...  6.76 us
    all_to_all x1, starting transfers between devices, body(): everyone = lax.all_to_all(coded, 'ens', 0, 0, tiled=True)  4.67 us
    pallas_call x1, Pallas kernels, body(): pl.pallas_call(prepare_kernel, out_shape=(shape((points, 2 * window), BF1...  4.59 us
    pallas_call x1, Pallas kernels, body(): pl.pallas_call(factors_kernel, out_shape=(shape((depth, local * points),...  4.06 us
  transfers between devices with their start and end apart: 9, of which 4 were waited for; matrix products, arithmetic and copies ran while one was open for 1% of the time, Pallas kernels for 15%

profile of v2, /device:TPU:8, one launch (start us, length us, event | category | flops | bytes accessed | tf_op | source)
XLA Modules:
  0.0 109.7 jit_solution(4166572543330696070)
XLA Ops:
  0.7 2.3 %collective-permute-start = (bf16[2,128,1024]{2,1,0:T(8,128)(2,1)}, bf16[2,128,1024]{2,1,0:T(8,128)(2,1)}, u32[]{:S(2)}, u32[]{:S(2)}) collective-permute-start(bf16[2,128,1024]{2,1,0:T(8,128)(2,1)} %lat_ref.3), channel_id=1, source_target_pairs={{0,63},{1,2},{2,1},{3,4},{4,3},{5,6},{6,5},{7,8},{8,7},{9,10},{10,... | collective-permute-start | bytes 1572872 | tf_op jit(solution)/shard_map/ppermute | solution.py:324
  3.0 1.0 pad.12.dpt_ref
  4.1 1.6 %copy-done = bf16[1024,1024]{1,0:T(8,128)(2,1)S(1)} copy-done((bf16[1024,1024]{1,0:T(8,128)(2,1)S(1)}, bf16[1024,1024]{1,0:T(8,128)(2,1)}, u32[]{:S(2)}) %copy-start) | copy-done | bytes 2097176
  5.7 1.0 copy-done.8
  6.7 0.7 copy-done.12
  7.4 0.7 copy-done.13
  8.1 0.7 copy-done.14
  8.8 0.7 copy-done.16
  9.4 4.6 %prepare.1 = (bf16[256,768]{1,0:T(8,128)(2,1)S(1)}, bf16[256,256]{1,0:T(8,128)(2,1)S(1)}, bf16[384,512]{1,0:T(8,128)(2,1)S(1)}, f32[2,256,1024]{2,1,0:T(8,128)S(1)}) custom-call(s32[2]{0:T(128)S(1)} %pad_add_fusion.where_ref, s32[2]{0:T(128)S(1)} %copy-done.16, s32[2,512]{1,0:T(2,128)S(1)} %copy-done.12, s32[2,512]{1,0:T(2,128)S(1)} %copy-done.13, ...), custom_call_target="tpu_custom_call" | custom-call | flops 3000000000 | bytes 6000000 | tf_op jit(solution)/shard_map/prepare/pallas_call | solution.py:328
  14.0 0.8 copy-done.29
  14.8 0.8 copy-done.31
  15.6 6.8 %forward.1 = (f32[2,256,1024]{2,1,0:T(8,128)S(1)}, bf16[2,256,1024]{2,1,0:T(8,128)(2,1)S(1)}, s16[4,2,112,256]{3,2,1,0:T(8,128)(2,1)}) custom-call(bf16[256,1024]{1,0:T(8,128)(2,1)} %bitcast.odd_ref.olat_ref, bf16[1024,1024]{1,0:T(8,128)(2,1)S(1)} %copy-done.1, bf16[256,256]{1,0:T(8,128)(2,1)S(1)} %get-tuple-element.22.cfo_ref, ...), custom_call_target="tpu_custom_call" | custom-call | flops 2000000000 | bytes 8000000 | tf_op jit(solution)/shard_map/forward/pallas_call | solution.py:345
  22.3 1.3 %copy-done.17 = f32[2,256,1024]{2,1,0:T(8,128)} copy-done((f32[2,256,1024]{2,1,0:T(8,128)}, f32[2,256,1024]{2,1,0:T(8,128)S(1)}, u32[]{:S(2)}) %copy-start.17) | copy-done | bytes 2097176
  23.7 1.0 copy-done.23
  24.6 4.7 %all-to-all-start = ((s16[4,2,112,256]{3,2,1,0:T(8,128)(2,1)}), s16[4,2,112,256]{3,2,1,0:T(8,128)(2,1)S(1)}, u32[]{:S(2)}, u32[]{:S(2)}) async-start(s16[4,2,112,256]{3,2,1,0:T(8,128)(2,1)} %get-tuple-element.24), calls=%async_computation | async-start | bytes 917504 | tf_op jit(solution)/shard_map/all_to_all | solution.py:371
  29.4 1.0 copy-done.9
  30.5 1.0 copy-done.11
  31.5 1.6 %copy-done.18 = f32[2,256,1024]{2,1,0:T(8,128)S(1)} copy-done((f32[2,256,1024]{2,1,0:T(8,128)S(1)}, f32[2,256,1024]{2,1,0:T(8,128)}, u32[]{:S(2)}) %copy-start.18) | copy-done | bytes 2097176
  33.1 1.2 %copy-done.24 = bf16[2,256,1024]{2,1,0:T(8,128)(2,1)S(1)} copy-done((bf16[2,256,1024]{2,1,0:T(8,128)(2,1)S(1)}, bf16[2,256,1024]{2,1,0:T(8,128)(2,1)}, u32[]{:S(2)}) %copy-start.24) | copy-done | bytes 1048600
  34.3 1.0 copy-done.32
  35.3 4.1 %factors.1 = (bf16[1024,512]{1,0:T(8,128)(2,1)S(1)}, bf16[1024,512]{1,0:T(8,128)(2,1)S(1)}, f32[2,256,1024]{2,1,0:T(8,128)S(1)}) custom-call(s32[2]{0:T(128)S(1)} %pad_add_fusion.where_ref, bf16[2,128,1024]{2,1,0:T(8,128)(2,1)S(1)} %copy-done.9, bf16[2,128,1024]{2,1,0:T(8,128)(2,1)S(1)} %copy-done.11, bf16[256,1024]{1,0:T(8,128)(2,1)} %bitcast.odd_ref.olat_ref, ...), custom_call_target="tpu_custom_call" | custom-call | flops 3000000000 | bytes 10000000 | tf_op jit(solution)/shard_map/factors/pallas_call | solution.py:374
  39.4 1.3 %copy-done.19 = f32[2,256,1024]{2,1,0:T(8,128)} copy-done((f32[2,256,1024]{2,1,0:T(8,128)}, f32[2,256,1024]{2,1,0:T(8,128)S(1)}, u32[]{:S(2)}) %copy-start.19) | copy-done | bytes 2097176
  40.7 1.0 copy-done.25
  41.7 1.0 copy-done.27
  42.7 0.6 all-to-all-done
  43.3 1.8 %copy-done.20 = f32[2,256,1024]{2,1,0:T(8,128)S(1)} copy-done((f32[2,256,1024]{2,1,0:T(8,128)S(1)}, f32[2,256,1024]{2,1,0:T(8,128)}, u32[]{:S(2)}) %copy-start.20) | copy-done | bytes 2097176
  45.0 1.2 %copy-done.26 = bf16[1024,512]{1,0:T(8,128)(2,1)S(1)} copy-done((bf16[1024,512]{1,0:T(8,128)(2,1)S(1)}, bf16[1024,512]{1,0:T(8,128)(2,1)}, u32[]{:S(2)}) %copy-start.26) | copy-done | bytes 1048600
  46.3 1.2 %copy-done.28 = bf16[1024,512]{1,0:T(8,128)(2,1)S(1)} copy-done((bf16[1024,512]{1,0:T(8,128)(2,1)S(1)}, bf16[1024,512]{1,0:T(8,128)(2,1)}, u32[]{:S(2)}) %copy-start.28) | copy-done | bytes 1048600
  47.5 3.3 %backward.1 = (bf16[512,1152]{1,0:T(8,128)(2,1)S(1)}, bf16[512,1152]{1,0:T(8,128)(2,1)S(1)}, bf16[2,256,1024]{2,1,0:T(8,128)(2,1)S(1)}) custom-call(s32[2]{0:T(128)S(1)} %pad_add_fusion.where_ref, s16[8,112,256]{2,1,0:T(8,128)(2,1)S(1)} %bitcast.10, f32[104,256]{1,0:T(8,128)S(1)} %pad.13.truth_ref, f32[104,1]{1,0:T(8,128)S(1)} %copy.14.var_ref, ...), custom_call_target="tpu_custom_call" | custom-call | flops 2000000000 | bytes 8000000 | tf_op jit(solution)/shard_map/backward/pallas_call | solution.py:391
  50.9 2.8 %collective-permute-done.5 = bf16[512,1152]{1,0:T(8,128)(2,1)S(1)} collective-permute-done((bf16[512,1152]{1,0:T(8,128)(2,1)S(1)}, bf16[512,1152]{1,0:T(8,128)(2,1)S(1)}, u32[]{:S(2)}, u32[]{:S(2)}) %collective-permute-start.5) | collective-permute-done | bytes 1179680 | tf_op jit(solution)/shard_map/ppermute | solution.py:412
  53.7 1.4 %add_convert_fusion = bf16[512,1152]{1,0:T(8,128)(2,1)} fusion(bf16[512,1152]{1,0:T(8,128)(2,1)S(1)} %collective-permute-done.5, bf16[512,1152]{1,0:T(8,128)(2,1)S(1)} %get-tuple-element.36), kind=kLoop, calls=%fused_computation | loop fusion | flops 2359296 | bytes 3538944 | tf_op jit(solution)/shard_map/convert_element_type | solution.py:428
  55.1 13.2 %all-to-all-start.1 = ((bf16[16,32,1152]{2,1,0:T(8,128)(2,1)}), bf16[16,32,1152]{2,1,0:T(8,128)(2,1)S(1)}, u32[]{:S(2)}, u32[]{:S(2)}) async-start(bf16[16,32,1152]{2,1,0:T(8,128)(2,1)} %bitcast.14), calls=%async_computation.1 | async-start | bytes 2359296 | tf_op jit(solution)/shard_map/all_to_all | solution.py:429
  68.2 1.2 %copy-done.22 = bf16[2,256,1024]{2,1,0:T(8,128)(2,1)S(1)} copy-done((bf16[2,256,1024]{2,1,0:T(8,128)(2,1)S(1)}, bf16[2,256,1024]{2,1,0:T(8,128)(2,1)}, u32[]{:S(2)}) %copy-start.22) | copy-done | bytes 1048600
  69.5 1.0 copy-done.30
  70.4 1.9 %rows.1 = (f32[2,128,1024]{2,1,0:T(8,128)S(1)}, bf16[2,128,1024]{2,1,0:T(8,128)(2,1)}, bf16[2,128,1024]{2,1,0:T(8,128)(2,1)}) custom-call(bf16[384,512]{1,0:T(8,128)(2,1)S(1)} %copy-done.30, bf16[2,256,1024]{2,1,0:T(8,128)(2,1)S(1)} %copy-done.22), custom_call_target="tpu_custom_call" | custom-call | flops 1000000000 | bytes 4000000 | tf_op jit(solution)/shard_map/rows/pallas_call | solution.py:413
  72.4 1.0 copy-done.5
  73.3 1.4 %collective-permute-start.3 = (bf16[2,128,1024]{2,1,0:T(8,128)(2,1)}, bf16[2,128,1024]{2,1,0:T(8,128)(2,1)}, u32[]{:S(2)}, u32[]{:S(2)}) collective-permute-start(bf16[2,128,1024]{2,1,0:T(8,128)(2,1)} %get-tuple-element.35), channel_id=1, source_target_pairs={{0,63},{31,32},{32,31},{63,0},{64,127},{95,96},{96,95},{127,64},{1... | collective-permute-start | bytes 1572872 | tf_op jit(solution)/shard_map/ppermute | solution.py:426
  74.8 2.1 %collective-permute-start.4 = (bf16[2,128,1024]{2,1,0:T(8,128)(2,1)}, bf16[2,128,1024]{2,1,0:T(8,128)(2,1)}, u32[]{:S(2)}, u32[]{:S(2)}) collective-permute-start(bf16[2,128,1024]{2,1,0:T(8,128)(2,1)} %get-tuple-element.35), channel_id=1, source_target_pairs={{1,2},{2,1},{3,4},{4,3},{5,6},{6,5},{7,8},{8,7},{9,10},{10,9},{11,... | collective-permute-start | bytes 1572872 | tf_op jit(solution)/shard_map/ppermute | solution.py:430
  76.9 9.9 %all-to-all-done.1.got_ref = bf16[16,32,1152]{2,1,0:T(8,128)(2,1)S(1)} async-done(((bf16[16,32,1152]{2,1,0:T(8,128)(2,1)}), bf16[16,32,1152]{2,1,0:T(8,128)(2,1)S(1)}, u32[]{:S(2)}, u32[]{:S(2)}) %all-to-all-start.1) | async-done | bytes 1179680 | tf_op jit(solution)/shard_map/all_to_all | solution.py:429
  86.8 0.2 plane.1
  87.0 0.7 copy-done.4
  87.7 10.5 %all-to-all-start.2 = ((bf16[8,16,1152]{2,1,0:T(8,128)(2,1)}), bf16[8,16,1152]{2,1,0:T(8,128)(2,1)S(1)}, u32[]{:S(2)}, u32[]{:S(2)}) async-start(bf16[8,16,1152]{2,1,0:T(8,128)(2,1)} %bitcast.12), calls=%async_computation.2 | async-start | bytes 589824 | tf_op jit(solution)/shard_map/all_to_all | solution.py:441
  98.2 1.0 copy-done.3
  99.2 3.0 %score.1 = f32[100,256]{1,0:T(8,128)} custom-call(s16[8,112,256]{2,1,0:T(8,128)(2,1)S(1)} %bitcast.11, f32[100,256]{1,0:T(8,128)S(1)} %copy-done.7), custom_call_target="tpu_custom_call" | custom-call | flops 10000000 | bytes 1000000 | tf_op jit(solution)/shard_map/score/pallas_call | solution.py:443
  102.2 1.2 %copy-done.6 = f32[2,128,1024]{2,1,0:T(8,128)S(1)} copy-done((f32[2,128,1024]{2,1,0:T(8,128)S(1)}, f32[2,128,1024]{2,1,0:T(8,128)}, u32[]{:S(2)}) %copy-start.6) | copy-done | bytes 1048600
  103.5 2.9 %latent.1 = bf16[2,128,1024]{2,1,0:T(8,128)(2,1)} custom-call(f32[2,128,1024]{2,1,0:T(8,128)S(1)} %copy-done.6, bf16[2,128,1024]{2,1,0:T(8,128)(2,1)} %collective-permute-done.2.core_ref, bf16[2,128,1024]{2,1,0:T(8,128)(2,1)} %collective-permute-done.3.far_ref, bf16[2,128,1024]{2,1,0:T(8,128)(2,1)} %collective-permute-done.4.near_ref, ...), custom_call_target="tpu_custom_call" | custom-call | flops 1000000000 | bytes 5000000 | tf_op jit(solution)/shard_map/latent/pallas_call | solution.py:452
  106.4 2.6 %all-to-all-done.2.got_ref = bf16[8,16,1152]{2,1,0:T(8,128)(2,1)S(1)} async-done(((bf16[8,16,1152]{2,1,0:T(8,128)(2,1)}), bf16[8,16,1152]{2,1,0:T(8,128)(2,1)S(1)}, u32[]{:S(2)}, u32[]{:S(2)}) %all-to-all-start.2) | async-done | bytes 294944 | tf_op jit(solution)/shard_map/all_to_all | solution.py:441
  109.0 0.7 final.1
  (53 shorter events, 0.5 us)
Async XLA Ops:
  0.6 3.4 %collective-permute-start.1 = (bf16[2,128,1024]{2,1,0:T(8,128)(2,1)}, bf16[2,128,1024]{2,1,0:T(8,128)(2,1)S(1)}, u32[]{:S(2)}, u32[]{:S(2)}) collective-permute-start(bf16[2,128,1024]{2,1,0:T(8,128)(2,1)} %lat_ref.3), channel_id=1, source_target_pairs={{0,1},{1,0},{2,3},{3,2},{4,5},{5,4},{6,7},{7,6},{8,9},{9,8},{10,11... | collective-permute-start | bytes 1572872 | tf_op jit(solution)/shard_map/ppermute | solution.py:325
  0.7 14.8 %collective-permute-start = (bf16[2,128,1024]{2,1,0:T(8,128)(2,1)}, bf16[2,128,1024]{2,1,0:T(8,128)(2,1)}, u32[]{:S(2)}, u32[]{:S(2)}) collective-permute-start(bf16[2,128,1024]{2,1,0:T(8,128)(2,1)} %lat_ref.3), channel_id=1, source_target_pairs={{0,63},{1,2},{2,1},{3,4},{4,3},{5,6},{6,5},{7,8},{8,7},{9,10},{10,... | collective-permute-start | bytes 1572872 | tf_op jit(solution)/shard_map/ppermute | solution.py:324
  4.1 1.6 %copy-start = (bf16[1024,1024]{1,0:T(8,128)(2,1)S(1)}, bf16[1024,1024]{1,0:T(8,128)(2,1)}, u32[]{:S(2)}) copy-start(bf16[1024,1024]{1,0:T(8,128)(2,1)} %w_ref.5) | copy-start | bytes 6291460
  5.7 1.0 copy-start.8
  6.7 0.7 copy-start.12
  7.4 0.7 copy-start.13
  8.1 0.7 copy-start.14
  8.8 0.7 copy-start.16
  9.4 4.6 %copy-start.10 = (bf16[2,128,1024]{2,1,0:T(8,128)(2,1)}, bf16[2,128,1024]{2,1,0:T(8,128)(2,1)S(1)}, u32[]{:S(2)}) copy-start(bf16[2,128,1024]{2,1,0:T(8,128)(2,1)S(1)} %collective-permute-done.1.clat_ref) | copy-start | bytes 1572868
  9.4 6.1 %copy-start.1 = (bf16[1024,1024]{1,0:T(8,128)(2,1)S(1)}, bf16[1024,1024]{1,0:T(8,128)(2,1)}, u32[]{:S(2)}) copy-start(bf16[1024,1024]{1,0:T(8,128)(2,1)} %w_ref.5) | copy-start | bytes 6291460
  14.0 0.8 copy-start.29
  14.8 0.8 copy-start.31
  15.5 13.7 %copy-start.33 = (f32[100]{0:T(128)S(1)}, f32[100]{0:T(128)}, u32[]{:S(2)}) copy-start(f32[100]{0:T(128)} %param.15) | copy-start | bytes 1204
  15.5 13.9 %copy-start.7 = (f32[100,256]{1,0:T(8,128)S(1)}, f32[100,256]{1,0:T(8,128)}, u32[]{:S(2)}) copy-start(f32[100,256]{1,0:T(8,128)} %truth_ref.1) | copy-start | bytes 307204
  22.3 1.3 %copy-start.17 = (f32[2,256,1024]{2,1,0:T(8,128)}, f32[2,256,1024]{2,1,0:T(8,128)S(1)}, u32[]{:S(2)}) copy-start(f32[2,256,1024]{2,1,0:T(8,128)S(1)} %get-tuple-element.27.summed_ref) | copy-start | bytes 6291460
  23.7 1.0 copy-start.23
  24.6 18.6 %all-to-all-start = ((s16[4,2,112,256]{3,2,1,0:T(8,128)(2,1)}), s16[4,2,112,256]{3,2,1,0:T(8,128)(2,1)S(1)}, u32[]{:S(2)}, u32[]{:S(2)}) async-start(s16[4,2,112,256]{3,2,1,0:T(8,128)(2,1)} %get-tuple-element.24), calls=%async_computation | async-start | bytes 917504 | tf_op jit(solution)/shard_map/all_to_all | solution.py:371
  29.4 1.0 copy-start.9
  30.5 1.0 copy-start.11
  31.5 1.6 %copy-start.18 = (f32[2,256,1024]{2,1,0:T(8,128)S(1)}, f32[2,256,1024]{2,1,0:T(8,128)}, u32[]{:S(2)}) copy-start(f32[2,256,1024]{2,1,0:T(8,128)} %copy-done.17) | copy-start | bytes 6291460
  33.1 1.2 %copy-start.24 = (bf16[2,256,1024]{2,1,0:T(8,128)(2,1)S(1)}, bf16[2,256,1024]{2,1,0:T(8,128)(2,1)}, u32[]{:S(2)}) copy-start(bf16[2,256,1024]{2,1,0:T(8,128)(2,1)} %copy-done.23) | copy-start | bytes 3145732
  34.3 1.0 copy-start.32
  35.3 7.9 %copy-start.15 = (f32[256]{0:T(256)S(1)}, f32[256]{0:T(256)}, u32[]{:S(2)}) copy-start(f32[256]{0:T(256)} %param.14) | copy-start | bytes 3076
  39.4 1.3 %copy-start.19 = (f32[2,256,1024]{2,1,0:T(8,128)}, f32[2,256,1024]{2,1,0:T(8,128)S(1)}, u32[]{:S(2)}) copy-start(f32[2,256,1024]{2,1,0:T(8,128)S(1)} %get-tuple-element.31.slope_ref) | copy-start | bytes 6291460
  40.7 1.0 copy-start.25
  41.7 1.0 copy-start.27
  43.3 7.5 %copy-start.2 = (s16[4,2,112,256]{3,2,1,0:T(8,128)(2,1)}, s16[4,2,112,256]{3,2,1,0:T(8,128)(2,1)S(1)}, u32[]{:S(2)}) copy-start(s16[4,2,112,256]{3,2,1,0:T(8,128)(2,1)S(1)} %all-to-all-done) | copy-start | bytes 1376260
  43.3 1.8 %copy-start.20 = (f32[2,256,1024]{2,1,0:T(8,128)S(1)}, f32[2,256,1024]{2,1,0:T(8,128)}, u32[]{:S(2)}) copy-start(f32[2,256,1024]{2,1,0:T(8,128)} %copy-done.19) | copy-start | bytes 6291460
  45.0 1.2 %copy-start.26 = (bf16[1024,512]{1,0:T(8,128)(2,1)S(1)}, bf16[1024,512]{1,0:T(8,128)(2,1)}, u32[]{:S(2)}) copy-start(bf16[1024,512]{1,0:T(8,128)(2,1)} %copy-done.25) | copy-start | bytes 3145732
  46.2 1.2 %copy-start.28 = (bf16[1024,512]{1,0:T(8,128)(2,1)S(1)}, bf16[1024,512]{1,0:T(8,128)(2,1)}, u32[]{:S(2)}) copy-start(bf16[1024,512]{1,0:T(8,128)(2,1)} %copy-done.27) | copy-start | bytes 3145732
  50.8 4.3 %copy-start.21 = (bf16[2,256,1024]{2,1,0:T(8,128)(2,1)}, bf16[2,256,1024]{2,1,0:T(8,128)(2,1)S(1)}, u32[]{:S(2)}) copy-start(bf16[2,256,1024]{2,1,0:T(8,128)(2,1)S(1)} %get-tuple-element.32.sg_ref) | copy-start | bytes 3145732
  50.8 2.9 %collective-permute-start.5 = (bf16[512,1152]{1,0:T(8,128)(2,1)S(1)}, bf16[512,1152]{1,0:T(8,128)(2,1)S(1)}, u32[]{:S(2)}, u32[]{:S(2)}) collective-permute-start(bf16[512,1152]{1,0:T(8,128)(2,1)S(1)} %get-tuple-element.37), channel_id=1, source_target_pairs={{0,1},{1,0},{2,3},{3,2},{4,5},{5,4},{6,7},{7,6},{8,9},{9,8},{10,11... | collective-permute-start | bytes 3538952 | tf_op jit(solution)/shard_map/ppermute | solution.py:412
  55.1 31.8 %all-to-all-start.1 = ((bf16[16,32,1152]{2,1,0:T(8,128)(2,1)}), bf16[16,32,1152]{2,1,0:T(8,128)(2,1)S(1)}, u32[]{:S(2)}, u32[]{:S(2)}) async-start(bf16[16,32,1152]{2,1,0:T(8,128)(2,1)} %bitcast.14), calls=%async_computation.1 | async-start | bytes 2359296 | tf_op jit(solution)/shard_map/all_to_all | solution.py:429
  68.2 1.2 %copy-start.22 = (bf16[2,256,1024]{2,1,0:T(8,128)(2,1)S(1)}, bf16[2,256,1024]{2,1,0:T(8,128)(2,1)}, u32[]{:S(2)}) copy-start(bf16[2,256,1024]{2,1,0:T(8,128)(2,1)} %copy-done.21) | copy-start | bytes 3145732
  69.4 1.0 copy-start.30
  72.4 1.0 copy-start.5
  73.3 28.9 %collective-permute-start.2 = (bf16[2,128,1024]{2,1,0:T(8,128)(2,1)}, bf16[2,128,1024]{2,1,0:T(8,128)(2,1)}, u32[]{:S(2)}, u32[]{:S(2)}) collective-permute-start(bf16[2,128,1024]{2,1,0:T(8,128)(2,1)} %get-tuple-element.34), channel_id=1, source_target_pairs={{0,1},{1,0},{2,3},{3,2},{4,5},{5,4},{6,7},{7,6},{8,9},{9,8},{10,11... | collective-permute-start | bytes 1572872 | tf_op jit(solution)/shard_map/ppermute | solution.py:431
  73.3 28.9 %collective-permute-start.3 = (bf16[2,128,1024]{2,1,0:T(8,128)(2,1)}, bf16[2,128,1024]{2,1,0:T(8,128)(2,1)}, u32[]{:S(2)}, u32[]{:S(2)}) collective-permute-start(bf16[2,128,1024]{2,1,0:T(8,128)(2,1)} %get-tuple-element.35), channel_id=1, source_target_pairs={{0,63},{31,32},{32,31},{63,0},{64,127},{95,96},{96,95},{127,64},{1... | collective-permute-start | bytes 1572872 | tf_op jit(solution)/shard_map/ppermute | solution.py:426
  74.8 27.4 %collective-permute-start.4 = (bf16[2,128,1024]{2,1,0:T(8,128)(2,1)}, bf16[2,128,1024]{2,1,0:T(8,128)(2,1)}, u32[]{:S(2)}, u32[]{:S(2)}) collective-permute-start(bf16[2,128,1024]{2,1,0:T(8,128)(2,1)} %get-tuple-element.35), channel_id=1, source_target_pairs={{1,2},{2,1},{3,4},{4,3},{5,6},{6,5},{7,8},{8,7},{9,10},{10,9},{11,... | collective-permute-start | bytes 1572872 | tf_op jit(solution)/shard_map/ppermute | solution.py:430
  87.0 0.7 copy-start.4
  87.7 21.3 %all-to-all-start.2 = ((bf16[8,16,1152]{2,1,0:T(8,128)(2,1)}), bf16[8,16,1152]{2,1,0:T(8,128)(2,1)S(1)}, u32[]{:S(2)}, u32[]{:S(2)}) async-start(bf16[8,16,1152]{2,1,0:T(8,128)(2,1)} %bitcast.12), calls=%async_computation.2 | async-start | bytes 589824 | tf_op jit(solution)/shard_map/all_to_all | solution.py:441
  98.2 1.0 copy-start.3
  102.2 1.2 %copy-start.6 = (f32[2,128,1024]{2,1,0:T(8,128)S(1)}, f32[2,128,1024]{2,1,0:T(8,128)}, u32[]{:S(2)}) copy-start(f32[2,128,1024]{2,1,0:T(8,128)} %copy-done.5) | copy-start | bytes 3145732

commit v3 on v2

v3 whole, which is shorter than its diff:
```python
import functools
import math

import jax
import jax.numpy as jnp
from jax import lax
from jax.experimental import pallas as pl
from jax.experimental.pallas import tpu as pltpu
from jax.sharding import PartitionSpec as P

HALO = 128
BLK = 128
ALPHA = 0.95
DELTA = 0.05
SPACE = ("zhi", "x", "y", "core")
QMAX = 32000.0
VPAD = 128
VROWS = 112
VUSE = 104
TILE = 256
GELU_C = math.sqrt(2.0 / math.pi)
MIB = 1 << 20
BIG = 56
MID = 24
F32 = jnp.float32
BF16 = jnp.bfloat16


def dot(a, b):
    return jnp.dot(a, b, preferred_element_type=F32)


def dot_nt(a, b):
    return lax.dot_general(a, b, (((1,), (1,)), ((), ())), preferred_element_type=F32)


def smem(count):
    return [pl.BlockSpec(memory_space=pltpu.SMEM)] * count


def cost(flops, nbytes):
    return pl.CostEstimate(flops=flops, bytes_accessed=nbytes, transcendentals=0)


def params(mib):
    return pltpu.CompilerParams(vmem_limit_bytes=mib * MIB)


def whole(*arrays):
    return [
        pl.BlockSpec(a.shape, functools.partial(lambda n, j: (0,) * n, len(a.shape)))
        for a in arrays
    ]


def hbm(count):
    return [pl.BlockSpec(memory_space=pltpu.HBM)] * count


def vmem(count):
    return [pl.BlockSpec(memory_space=pltpu.VMEM)] * count


def start_copy(src, dst, sem):
    copy = pltpu.make_async_copy(src, dst, sem)
    copy.start()
    return copy


def pair_factor(members):
    fair_eps = (1.0 - ALPHA) / members
    return (1.0 - fair_eps) / (2.0 * members * (members - 1))


def smooth_abs(distance):
    square = distance * distance + DELTA * DELTA
    return square * lax.rsqrt(square)


def signum(distance):
    return distance * lax.rsqrt(distance * distance + DELTA * DELTA)


def prepare_kernel(
    where_ref, count_hbm, src_hbm, dst_hbm, wt_hbm, lat_hbm, clat_hbm, w_hbm,
    cf_hbm, cft_hbm, cfo_ref, part_ref,
    count_ref, src_ref, dst_ref, wt_ref, x_ref, w_ref, cf_ref, cft_ref, in_sem, out_sem,
):
    edges = [
        start_copy(src, dst, in_sem.at[k])
        for k, (src, dst) in enumerate(
            ((count_hbm, count_ref), (src_hbm, src_ref), (dst_hbm, dst_ref), (wt_hbm, wt_ref))
        )
    ]
    local = lat_hbm.shape[0]
    inputs = []
    for m in range(local):
        for k, ref in enumerate((lat_hbm, clat_hbm)):
            inputs.append(
                start_copy(
                    ref.at[m],
                    x_ref.at[pl.ds((2 * m + k) * HALO, HALO)],
                    in_sem.at[4 + 2 * m + k],
                )
            )
    inputs.append(start_copy(w_hbm, w_ref, in_sem.at[4 + 2 * local]))
    core = where_ref[0]
    slots = src_ref.shape[1]
    window = cf_ref.shape[1] // 2
    points = cf_ref.shape[0]
    for copy in edges:
        copy.wait()
    for b in range(src_ref.shape[0]):
        src = src_ref[b : b + 1, :]
        slot = lax.broadcasted_iota(jnp.int32, (1, slots), 1)
        wt = jnp.where(slot < count_ref[b], wt_ref[b : b + 1, :], 0.0)
        left = 2 * HALO - HALO * core
        right = HALO + HALO * core
        place = jnp.where(
            src < HALO,
            src + left,
            jnp.where(src < 2 * HALO, src - HALO, src - 2 * HALO + right),
        )
        rows = lax.broadcasted_iota(jnp.int32, (window, slots), 0)
        hot = jnp.where(rows == place, 1.0, 0.0).astype(BF16)
        pts = lax.broadcasted_iota(jnp.int32, (BLK, slots), 0)
        mat = jnp.where(pts == dst_ref[b : b + 1, :], wt, 0.0).astype(BF16)
        coef = dot_nt(mat, hot)
        high = coef.astype(BF16)
        low = (coef - high.astype(F32)).astype(BF16)
        at = slice(b * BLK, (b + 1) * BLK)
        cf_ref[at, :window] = high
        cf_ref[at, window:] = low
        cfo_ref[at, :HALO] = high[:, 2 * HALO :]
        cfo_ref[at, HALO:] = low[:, 2 * HALO :]
        coef_t = dot_nt(hot, mat)
        high_t = coef_t.astype(BF16)
        cft_ref[:, b * BLK : (b + 1) * BLK] = high_t
        cft_ref[:, points + b * BLK : points + (b + 1) * BLK] = (
            coef_t - high_t.astype(F32)
        ).astype(BF16)
    outs = [
        start_copy(cf_ref, cf_hbm, out_sem.at[0]),
        start_copy(cft_ref, cft_hbm, out_sem.at[1]),
    ]
    for copy in inputs:
        copy.wait()
    x = x_ref[...]
    high = cf_ref[:, : 2 * HALO]
    low = cf_ref[:, window : window + 2 * HALO]
    for j in range(w_ref.shape[1] // TILE):
        at = slice(j * TILE, (j + 1) * TILE)
        p = dot(x, w_ref[:, at]).astype(BF16)
        for m in range(local):
            pm = p[2 * m * HALO : (2 * m + 2) * HALO]
            part_ref[m, :, at] = dot(high, pm) + dot(low, pm)
    for copy in outs:
        copy.wait()


def forward_kernel(
    odd_ref, w_ref, cfo_ref, part_ref, dpt_ref, summed_hbm, hidden_hbm, coded_hbm,
    summed_ref, hidden_ref, code_ref, out_sem,
):
    local, points, depth = part_ref.shape
    steps = depth // TILE
    forecast = [jnp.zeros((VPAD, points), F32) for _ in range(local)]
    outs = []
    for j in range(steps):
        at = slice(j * TILE, (j + 1) * TILE)
        p = dot(odd_ref[...], w_ref[:, at]).astype(BF16)
        for m in range(local):
            pm = p[m * HALO : (m + 1) * HALO]
            s = part_ref[m, :, at] + dot(cfo_ref[...], jnp.concatenate([pm, pm], axis=0))
            summed_ref[m, :, at] = s
            t = jnp.tanh(GELU_C * (s + 0.044715 * (s * s * s)))
            h = (0.5 * s * (1.0 + t)).astype(BF16)
            hidden_ref[m, :, at] = h
            forecast[m] = forecast[m] + dot_nt(dpt_ref[:, at], h)
        cols = pl.ds(j * TILE, TILE)
        for k, (src, dst) in enumerate(((summed_ref, summed_hbm), (hidden_ref, hidden_hbm))):
            outs.append(
                start_copy(src.at[:, :, cols], dst.at[:, :, cols], out_sem.at[k, j])
            )
    for m in range(local):
        f = forecast[m]
        largest = jnp.maximum(jnp.max(jnp.abs(f), axis=1, keepdims=True), 1e-30)
        power = jnp.ceil(jnp.log(largest) * (1.0 / math.log(2.0)) + 1e-3)
        power = jnp.broadcast_to(power, (VPAD, VPAD))
        q = f * (jnp.exp2(-power[:, :1]) * QMAX)
        q = jnp.where(q >= 0.0, q + 0.5, q - 0.5)
        row = jnp.concatenate([power.T[:8], jnp.zeros((8, points - VPAD), F32)], axis=1)
        row = jnp.where(row >= 0.0, row + 0.5, row - 0.5)
        code = jnp.concatenate([q[:VUSE], row], axis=0)
        code_ref[m] = code.astype(jnp.int32).astype(jnp.int16)
    for e in range(coded_hbm.shape[0]):
        outs.append(start_copy(code_ref, coded_hbm.at[e], out_sem.at[2, e]))
    for copy in outs:
        copy.wait()


def factors_kernel(
    where_ref, lat_ref, clat_ref, olat_ref, cf_ref, summed_ref, hidden_ref,
    aggt_ref, hidt_ref, slope_ref, x_ref,
):
    core = where_ref[0]
    j = pl.program_id(0)
    window = cf_ref.shape[1] // 2
    half = aggt_ref.shape[0] // 2
    local = lat_ref.shape[0]
    points = cf_ref.shape[0]
    high = cf_ref[:, :window]
    low = cf_ref[:, window:]
    for m in range(local):
        x_ref[:HALO] = lat_ref[m]
        x_ref[HALO : 2 * HALO] = clat_ref[m]
        x_ref[2 * HALO :] = olat_ref[m * HALO : (m + 1) * HALO]
        cols = slice(m * points, (m + 1) * points)
        x = x_ref[...]
        agg = (dot(high, x) + dot(low, x)).T.astype(BF16)
        hid = hidden_ref[m].astype(F32).T.astype(BF16)
        for k in range(TILE // 16):
            xy = lax.rem(j, 2) * (TILE // 32) + k // 2
            to = lax.bitwise_xor(core, k % 2) * half + xy * 32 + lax.div(j, 2) * 16
            to = pl.ds(pl.multiple_of(to, 16), 16)
            aggt_ref[to, cols] = agg[k * 16 : (k + 1) * 16]
            hidt_ref[to, cols] = hid[k * 16 : (k + 1) * 16]
        s = summed_ref[m]
        t = jnp.tanh(GELU_C * (s + 0.044715 * (s * s * s)))
        slope_ref[m] = 0.5 * (1.0 + t) + (0.5 * GELU_C) * s * (1.0 - t * t) * (
            1.0 + 3.0 * 0.044715 * (s * s)
        )


def decode(code_ref, index):
    code = code_ref[index].astype(jnp.int32).astype(F32)
    power = jnp.broadcast_to(code[VUSE : VUSE + 1, :VPAD], (VPAD, VPAD)).T
    return code[:VUSE] * (jnp.exp2(power[:VUSE, :1]) * (1.0 / QMAX))


def score_kernel(code_ref, truth_ref, score_ref):
    members = code_ref.shape[0]
    nvar = truth_ref.shape[0]
    collected = [decode(code_ref, m)[:nvar] for m in range(members)]
    truth = truth_ref[...]
    skill = sum(smooth_abs(f - truth) for f in collected)
    spread = jnp.zeros_like(skill)
    for m in range(members):
        for o in range(m + 1, members):
            spread = spread + smooth_abs(collected[m] - collected[o])
    score_ref[...] = skill * (1.0 / members) - (pair_factor(members) * 2.0) * spread


def backward_kernel(
    where_ref, code_hbm, truth_hbm, var_hbm, area_hbm, dpt_hbm, aggt_hbm, hidt_hbm, slope_hbm,
    mine_hbm, theirs_hbm, sg_hbm,
    code_ref, truth_ref, var_ref, area_ref, dpt_ref, aggt_ref, hidt_ref, slope_ref,
    f_ref, part_ref, out_ref, sg_ref, in_sem, out_sem,
):
    members = code_ref.shape[0]
    local, points, depth = slope_ref.shape
    half = depth // 2
    steps = depth // TILE
    pairs = (
        (code_hbm, code_ref), (truth_hbm, truth_ref), (var_hbm, var_ref), (area_hbm, area_ref),
        (dpt_hbm, dpt_ref), (hidt_hbm, hidt_ref), (slope_hbm, slope_ref), (aggt_hbm, aggt_ref),
    )
    copies = [start_copy(src, dst, in_sem.at[k]) for k, (src, dst) in enumerate(pairs)]
    for copy in copies[:5]:
        copy.wait()
    for m in range(members):
        f_ref[m] = decode(code_ref, m)
    first = where_ref[1] * local
    truth = truth_ref[...]
    multiplier = var_ref[...] * area_ref[...]
    grads = []
    for m in range(local):
        own = f_ref[first + m]
        mutual = sum(signum(own - f_ref[o]) for o in range(members))
        g = multiplier * (
            signum(own - truth) * (1.0 / members) - (2.0 * pair_factor(members)) * mutual
        )
        g = jnp.concatenate([g, jnp.zeros((VPAD - VUSE, points), F32)], axis=0)
        grads.append(g.T.astype(BF16))
    grad = jnp.concatenate(grads, axis=0)
    outs = []
    copies[5].wait()
    out_ref[...] = dot(hidt_ref[...], grad).astype(BF16)
    cols = pl.ds(depth, VPAD)
    for k, hbm_ref in enumerate((mine_hbm, theirs_hbm)):
        src = out_ref.at[pl.ds(k * half, half)]
        outs.append(start_copy(src, hbm_ref.at[:, cols], out_sem.at[k, steps]))
    copies[6].wait()
    copies[7].wait()
    for j in range(steps):
        at = slice(j * TILE, (j + 1) * TILE)
        cols = pl.ds(j * TILE, TILE)
        hg = dot(grad, dpt_ref[:, at])
        for m in range(local):
            rows = slice(m * points, (m + 1) * points)
            sg_ref[j, rows, :] = (hg[rows] * slope_ref[m, :, at]).astype(BF16)
        part_ref[j] = dot(aggt_ref[...], sg_ref[j]).astype(BF16)
        outs.append(start_copy(sg_ref.at[j], sg_hbm.at[:, cols], out_sem.at[2, j]))
        for k, hbm_ref in enumerate((mine_hbm, theirs_hbm)):
            src = part_ref.at[j, pl.ds(k * half, half)]
            outs.append(start_copy(src, hbm_ref.at[:, cols], out_sem.at[k, j]))
    for copy in outs:
        copy.wait()


def merge_kernel(mine_ref, theirs_ref, out_hbm, out_ref, out_sem):
    rows = mine_ref.shape[0] // 4
    outs = []
    for k in range(4):
        at = slice(k * rows, (k + 1) * rows)
        out_ref[at] = (mine_ref[at].astype(F32) + theirs_ref[at].astype(F32)).astype(BF16)
        cut = pl.ds(k * rows, rows)
        outs.append(start_copy(out_ref.at[cut], out_hbm.at[cut], out_sem.at[k]))
    for copy in outs:
        copy.wait()


def rows_kernel(
    cft_hbm, sg_hbm, core_hbm, odd_hbm, cft_ref, sg_ref, core_ref, odd_ref, in_sem, out_sem
):
    local = core_ref.shape[0]
    points = cft_ref.shape[1] // 2
    cft_copy = start_copy(cft_hbm.at[pl.ds(HALO, 2 * HALO)], cft_ref, in_sem.at[local])
    copies = [
        start_copy(sg_hbm.at[pl.ds(m * points, points)], sg_ref.at[m], in_sem.at[m])
        for m in range(local)
    ]
    cft_copy.wait()
    high = cft_ref[:, :points]
    low = cft_ref[:, points:]
    outs = []
    for m in range(local):
        copies[m].wait()
        for j in range(sg_ref.shape[2] // TILE):
            at = slice(j * TILE, (j + 1) * TILE)
            s = sg_ref[m, :, at]
            g = (dot(high, s) + dot(low, s)).astype(BF16)
            core_ref[m, :, at] = g[:HALO]
            odd_ref[m, :, at] = g[HALO:]
        outs.append(start_copy(odd_ref.at[m], odd_hbm.at[m], out_sem.at[0, m]))
        outs.append(start_copy(core_ref.at[m], core_hbm.at[m], out_sem.at[1, m]))
    for copy in outs:
        copy.wait()


def plane_kernel(got_ref, out_hbm, out_ref, out_sem):
    per = out_hbm.shape[2]
    outs = []
    for z in range(out_hbm.shape[0]):
        at = slice(z * per, (z + 1) * per)
        total = got_ref[0, at].astype(F32)
        for k in range(1, got_ref.shape[0]):
            total = total + got_ref[k, at].astype(F32)
        out_ref[z] = total.astype(BF16)
        for e in range(out_hbm.shape[1]):
            outs.append(start_copy(out_ref.at[z], out_hbm.at[z, e], out_sem.at[z, e]))
    for copy in outs:
        copy.wait()


def final_kernel(got_ref, src_ref, out_ref, *, scaling):
    total = got_ref[0].astype(F32)
    for k in range(1, got_ref.shape[0]):
        total = total + got_ref[k].astype(F32)
    total = total * scaling
    depth = src_ref.shape[1]
    src_ref[...] = total[:, :depth]
    out_ref[...] = total[:, depth : depth + out_ref.shape[1]]


def latent_kernel(cft_ref, sg_ref, core_ref, odd_ref, w_ref, out_ref, g_ref):
    local = core_ref.shape[0]
    points = cft_ref.shape[1] // 2

    @pl.when(pl.program_id(0) == 0)
    def _():
        high = cft_ref[:, :points]
        low = cft_ref[:, points:]
        for m in range(local):
            s = sg_ref[m * points : (m + 1) * points]
            g = dot(high, s) + dot(low, s)
            g = g + core_ref[m].astype(F32) + odd_ref[m].astype(F32)
            g_ref[m * HALO : (m + 1) * HALO] = g.astype(BF16)

    r = dot_nt(g_ref[...], w_ref[...]).astype(BF16)
    for m in range(local):
        out_ref[m] = r[m * HALO : (m + 1) * HALO]


def shape(dims, dtype):
    return jax.ShapeDtypeStruct(dims, dtype)


def call_prepare(where, edge_count, edge_src, edge_dst, edge_weight, latent, core_lat, weight):
    local, rows, depth = latent.shape
    window = rows + 2 * HALO
    points = edge_src.shape[0] * BLK
    edges = edge_src.shape
    return pl.pallas_call(
        prepare_kernel,
        out_shape=(
            shape((points, 2 * window), BF16),
            shape((window, 2 * points), BF16),
            shape((points, 2 * HALO), BF16),
            shape((local, points, depth), F32),
        ),
        in_specs=smem(1) + hbm(7),
        out_specs=tuple(hbm(2) + vmem(2)),
        scratch_shapes=[
            pltpu.SMEM(edge_count.shape, jnp.int32),
            pltpu.VMEM(edges, jnp.int32),
            pltpu.VMEM(edges, jnp.int32),
            pltpu.VMEM(edges, F32),
            pltpu.VMEM((local * 2 * HALO, depth), BF16),
            pltpu.VMEM(weight.shape, BF16),
            pltpu.VMEM((points, 2 * window), BF16),
            pltpu.VMEM((window, 2 * points), BF16),
            pltpu.SemaphoreType.DMA((5 + 2 * local,)),
            pltpu.SemaphoreType.DMA((2,)),
        ],
        compiler_params=params(BIG),
        cost_estimate=cost(3 * 10**9, 6 * 10**6),
        name="prepare",
    )(where, edge_count, edge_src, edge_dst, edge_weight, latent, core_lat, weight)


def call_forward(odd_lat, weight, cfo, part, dpt, ens):
    local, points, depth = part.shape
    steps = depth // TILE
    return pl.pallas_call(
        forward_kernel,
        out_shape=(
            shape((local, points, depth), F32),
            shape((local, points, depth), BF16),
            shape((ens, local, VROWS, points), jnp.int16),
        ),
        in_specs=vmem(5),
        out_specs=tuple(hbm(3)),
        scratch_shapes=[
            pltpu.VMEM((local, points, depth), F32),
            pltpu.VMEM((local, points, depth), BF16),
            pltpu.VMEM((local, VROWS, points), jnp.int16),
            pltpu.SemaphoreType.DMA((3, max(steps, ens))),
        ],
        compiler_params=params(BIG),
        cost_estimate=cost(2 * 10**9, 8 * 10**6),
        name="forward",
    )(odd_lat, weight, cfo, part, dpt)


def call_factors(where, latent, core_lat, odd_lat, cf, summed, hidden):
    local, points, depth = summed.shape
    rows = latent.shape[1]
    lat_spec = pl.BlockSpec((local, rows, TILE), lambda j: (0, 0, j))
    sliced = pl.BlockSpec((local, points, TILE), lambda j: (0, 0, j))
    out_shape = (
        shape((depth, local * points), BF16),
        shape((depth, local * points), BF16),
        shape((local, points, depth), F32),
    )
    return pl.pallas_call(
        factors_kernel,
        grid=(depth // TILE,),
        out_shape=out_shape,
        in_specs=smem(1)
        + [
            lat_spec,
            lat_spec,
            pl.BlockSpec((local * rows, TILE), lambda j: (0, j)),
            *whole(cf),
            sliced,
            sliced,
        ],
        out_specs=(*whole(*out_shape[:2]), sliced),
        scratch_shapes=[pltpu.VMEM((cf.shape[1] // 2, TILE), BF16)],
        compiler_params=params(BIG),
        cost_estimate=cost(3 * 10**9, 10 * 10**6),
        name="factors",
    )(where, latent, core_lat, odd_lat, cf, summed, hidden)


def call_backward(where, everyone, truth, var_col, area, dpt, aggt, hidt, slope):
    members = everyone.shape[0]
    local, points, depth = slope.shape
    cols = depth + VPAD
    steps = depth // TILE
    operands = (everyone, truth, var_col, area, dpt, aggt, hidt, slope)
    return pl.pallas_call(
        backward_kernel,
        out_shape=(
            shape((depth // 2, cols), BF16),
            shape((depth // 2, cols), BF16),
            shape((local * points, depth), BF16),
        ),
        in_specs=smem(1) + hbm(len(operands)),
        out_specs=tuple(hbm(3)),
        scratch_shapes=[pltpu.VMEM(a.shape, a.dtype) for a in operands]
        + [
            pltpu.VMEM((members, VUSE, points), F32),
            pltpu.VMEM((steps, depth, TILE), BF16),
            pltpu.VMEM((depth, VPAD), BF16),
            pltpu.VMEM((steps, local * points, TILE), BF16),
            pltpu.SemaphoreType.DMA((len(operands),)),
            pltpu.SemaphoreType.DMA((3, steps + 1)),
        ],
        compiler_params=params(BIG),
        cost_estimate=cost(2 * 10**9, 8 * 10**6),
        name="backward",
    )(where, *operands)


def call_merge(mine, theirs):
    return pl.pallas_call(
        merge_kernel,
        out_shape=shape(mine.shape, BF16),
        in_specs=vmem(2),
        out_specs=hbm(1)[0],
        scratch_shapes=[pltpu.VMEM(mine.shape, BF16), pltpu.SemaphoreType.DMA((4,))],
        compiler_params=params(MID),
        cost_estimate=cost(10**6, 4 * 10**6),
        name="merge",
    )(mine, theirs)


def call_rows(cft, summed_grad, local):
    depth = summed_grad.shape[1]
    points = summed_grad.shape[0] // local
    send = shape((local, HALO, depth), BF16)
    return pl.pallas_call(
        rows_kernel,
        out_shape=(send, send),
        in_specs=hbm(2),
        out_specs=tuple(hbm(2)),
        scratch_shapes=[
            pltpu.VMEM((2 * HALO, cft.shape[1]), BF16),
            pltpu.VMEM((local, points, depth), BF16),
            pltpu.VMEM(send.shape, BF16),
            pltpu.VMEM(send.shape, BF16),
            pltpu.SemaphoreType.DMA((local + 1,)),
            pltpu.SemaphoreType.DMA((2, local)),
        ],
        compiler_params=params(BIG),
        cost_estimate=cost(10**9, 4 * 10**6),
        name="rows",
    )(cft, summed_grad)


def call_plane(got, ens):
    out_shape = shape((2, ens, got.shape[1] // 2, got.shape[2]), BF16)
    return pl.pallas_call(
        plane_kernel,
        out_shape=out_shape,
        in_specs=vmem(1),
        out_specs=hbm(1)[0],
        scratch_shapes=[
            pltpu.VMEM((2,) + out_shape.shape[2:], BF16),
            pltpu.SemaphoreType.DMA((2, ens)),
        ],
        compiler_params=params(MID),
        cost_estimate=cost(10**6, 2 * 10**6),
        name="plane",
    )(got)


def call_score(everyone, truth):
    return pl.pallas_call(
        score_kernel,
        grid=(1,),
        out_shape=shape(truth.shape, F32),
        in_specs=whole(everyone, truth),
        out_specs=whole(truth)[0],
        compiler_params=params(MID),
        cost_estimate=cost(10**7, 10**6),
        name="score",
    )(everyone, truth)


def call_latent(cft, summed_grad, core_grad, odd_grad, weight):
    local, rows, depth = core_grad.shape
    return pl.pallas_call(
        latent_kernel,
        grid=(depth // TILE,),
        out_shape=shape(core_grad.shape, BF16),
        in_specs=[
            pl.BlockSpec((HALO, cft.shape[1]), lambda j: (0, 0)),
            *whole(summed_grad, core_grad, odd_grad),
            pl.BlockSpec((TILE, depth), lambda j: (j, 0)),
        ],
        out_specs=pl.BlockSpec((local, rows, TILE), lambda j: (0, 0, j)),
        scratch_shapes=[pltpu.VMEM((local * rows, depth), BF16)],
        compiler_params=params(BIG),
        cost_estimate=cost(10**9, 5 * 10**6),
        name="latent",
    )(cft, summed_grad, core_grad, odd_grad, weight)


def call_final(got, nvar, scaling):
    per = got.shape[1]
    return pl.pallas_call(
        functools.partial(final_kernel, scaling=scaling),
        out_shape=(shape((per, got.shape[2] - VPAD), F32), shape((per, nvar), F32)),
        in_specs=vmem(1),
        out_specs=tuple(vmem(2)),
        compiler_params=params(MID),
        cost_estimate=cost(10**5, 4 * 10**5),
        name="final",
    )(got)


def make_body(count):
    odd_pairs = [(i, (i + 1) % count if i % 2 else (i - 1) % count) for i in range(count)]
    swap = [(0, 1), (1, 0)]

    def body(
        latent, src_weight, decoder_projection, truth, area_weight, var_weight,
        edge_src, edge_dst, edge_weight, edge_count,
    ):
        local, rows, depth = latent.shape
        ens = lax.axis_size("ens")
        members = local * ens
        nvar = decoder_projection.shape[1]
        points = truth.shape[1]
        per = depth // count
        cols = depth + VPAD
        where = jnp.stack([lax.axis_index("core"), lax.axis_index("ens")]).astype(jnp.int32)

        odd_lat = lax.ppermute(latent, SPACE, odd_pairs).reshape(local * rows, depth)
        core_lat = lax.ppermute(latent, "core", swap)
        dpt = jnp.pad(decoder_projection.T, ((0, VPAD - nvar), (0, 0)))
        cf, cft, cfo, part = call_prepare(
            where, edge_count, edge_src, edge_dst, edge_weight, latent, core_lat, src_weight
        )
        summed, hidden, coded = call_forward(odd_lat, src_weight, cfo, part, dpt, ens)
        everyone = lax.all_to_all(coded, "ens", 0, 0, tiled=True)
        everyone = everyone.reshape(members, VROWS, points)
        aggt, hidt, slope = call_factors(
            where, latent, core_lat, odd_lat, cf, summed, hidden
        )
        tall = jnp.pad(truth, ((0, VUSE - nvar), (0, 0)))
        var_col = jnp.pad(var_weight, (0, VUSE - nvar)).reshape(VUSE, 1)
        mine, theirs, summed_grad = call_backward(
            where, everyone, tall, var_col, area_weight.reshape(1, points), dpt,
            aggt, hidt, slope,
        )

        theirs = lax.ppermute(theirs, "core", swap)
        half = call_merge(mine, theirs).reshape(16, 2 * per, cols)
        got = lax.all_to_all(half, ("x", "y"), 0, 0, tiled=True)
        core_send, odd_send = call_rows(cft, summed_grad, local)
        odd_grad = lax.ppermute(odd_send, SPACE, odd_pairs)
        core_grad = lax.ppermute(core_send, "core", swap)
        plane = call_plane(got, ens)
        got = lax.all_to_all(plane.reshape(2 * ens, per, cols), ("zhi", "ens"), 0, 0, tiled=True)
        score = call_score(everyone, truth)
        grad_latent = call_latent(cft, summed_grad, core_grad, odd_grad, src_weight)
        grad_src, grad_out = call_final(got, nvar, 1.0 / math.sqrt(members * points * count))
        return score, grad_latent, grad_src, grad_out

    return body


def solution(mesh):
    fine = jax.sharding.Mesh(
        mesh.devices.reshape(mesh.devices.shape[0], 2, 4, 4, 2), ("ens",) + SPACE
    )
    return jax.shard_map(
        make_body(mesh.devices.shape[1]),
        mesh=fine,
        in_specs=(
            P("ens", SPACE, None), P(), P(), P(None, SPACE), P(SPACE), P(),
            P(SPACE, None), P(SPACE, None), P(SPACE, None), P(SPACE),
        ),
        out_specs=(P(None, SPACE), P("ens", SPACE, None), P(SPACE, None), P(SPACE, None)),
        check_vma=False,
    )
```

time: 111 us -> 108 us (0.973)
  local copies, waits for them, and re-layouts: 29.7 us -> 8.28 us
  waiting for transfers between devices: 16 us -> 31.3 us
  Pallas kernels: 27.4 us -> 40.2 us
  starting transfers between devices: 34.3 us -> 26 us
    unnamed x68 -> x18, local copies, waits for them, and re-layouts: 28.7 us -> 5.24 us
    pallas_call x9 -> x10, Pallas kernels: 27.4 us -> 40.2 us  [the longest x1 7.66 us: call_prepare(): pl.pallas_call(prepare_kernel, out_shape=(shape((points, 2 * window), BF1...]
    all_to_all x1, waiting for transfers between devices: 9.91 us -> 19.9 us  [body(): got = lax.all_to_all(half, ('x', 'y'), 0, 0, tiled=True)]
    all_to_all x1, waiting for transfers between devices: 0.59 us -> 5.8 us  [body(): everyone = lax.all_to_all(coded, 'ens', 0, 0, tiled=True)]
    ppermute x2 -> x1, starting transfers between devices: 3.56 us -> 0.21 us  [body(): odd_grad = lax.ppermute(odd_send, SPACE, odd_pairs)]
    all_to_all x1, starting transfers between devices: 13.2 us -> 10.2 us  [body(): got = lax.all_to_all(half, ('x', 'y'), 0, 0, tiled=True)]
    all_to_all x1, starting transfers between devices: 10.5 us -> 8.65 us  [body(): lax.all_to_all(plane.reshape(2 * ens, per, cols), ('zhi', 'ens'), 0, 0, t...]
    convert_element_type x1 -> x0, other arithmetic: 1.35 us -> none  [body(): (mine.astype(F32) + theirs.astype(F32)).astype(BF16)]
  transfers between devices with their start and end apart: 9 -> 8, of which waited for: 4 -> 4; matrix products, arithmetic and copies ran while one was open for 1% -> 3% of each run, Pallas kernels for 15% -> 24%
where the time goes in v3:
time: 108 us; the launch traced here: 107 us
  Pallas kernels  40.2 us (37%)
  waiting for transfers between devices  31.3 us (29%)
  starting transfers between devices  26 us (24%)
  local copies, waits for them, and re-layouts  8.28 us (8%)
    all_to_all x1, waiting for transfers between devices, body(): got = lax.all_to_all(half, ('x', 'y'), 0, 0, tiled=True)  19.9 us
    all_to_all x1, starting transfers between devices, body(): got = lax.all_to_all(half, ('x', 'y'), 0, 0, tiled=True)  10.2 us
    all_to_all x1, starting transfers between devices, body(): lax.all_to_all(plane.reshape(2 * ens, per, cols), ('zhi', 'ens'), 0, 0, t...  8.65 us
    pallas_call x1, Pallas kernels, call_prepare(): pl.pallas_call(prepare_kernel, out_shape=(shape((points, 2 * window), BF1...  7.66 us
    pallas_call x1, Pallas kernels, call_factors(): pl.pallas_call(factors_kernel, grid=(depth // TILE,), out_shape=out_shape...  7.29 us
    pallas_call x1, Pallas kernels, call_backward(): pl.pallas_call(backward_kernel, out_shape=(shape((depth // 2, cols), BF16...  6.49 us
    pallas_call x1, Pallas kernels, call_forward(): pl.pallas_call(forward_kernel, out_shape=(shape((local, points, depth), F...  6.18 us
    all_to_all x1, waiting for transfers between devices, body(): everyone = lax.all_to_all(coded, 'ens', 0, 0, tiled=True)  5.8 us
  transfers between devices with their start and end apart: 8, of which 4 were waited for; matrix products, arithmetic and copies ran while one was open for 3% of the time, Pallas kernels for 24%

profile of v3, /device:TPU:8, one launch (start us, length us, event | category | flops | bytes accessed | tf_op | source)
XLA Modules:
  0.0 107.2 jit_solution(13266084189766158213)
XLA Ops:
  0.6 0.1 collective-permute-start.1
  0.7 2.3 %collective-permute-start = (bf16[2,128,1024]{2,1,0:T(8,128)(2,1)}, bf16[2,128,1024]{2,1,0:T(8,128)(2,1)S(1)}, u32[]{:S(2)}, u32[]{:S(2)}) collective-permute-start(bf16[2,128,1024]{2,1,0:T(8,128)(2,1)} %lat_ref.1), channel_id=1, source_target_pairs={{0,63},{1,2},{2,1},{3,4},{4,3},{5,6},{6,5},{7,8},{8,7},{9,10},{10,... | collective-permute-start | bytes 1572872 | tf_op jit(solution)/shard_map/ppermute | solution.py:632
  3.0 1.7 %pad.12.dpt_ref.dpt_hbm = bf16[128,1024]{1,0:T(8,128)(2,1)} pad(bf16[100,1024]{1,0:T(8,128)(2,1)} %bitcast.12, bf16[]{:T(256)} %constant.13.clone.1), padding=0_28x0_0 | pad | bytes 466946 | tf_op jit(solution)/shard_map/jit(_pad)/pad | solution.py:634
  4.7 0.6 pad_add_fusion.where_ref
  5.3 0.0 collective-permute-done.1.clat_hbm.clat_ref
  5.3 0.0 copy-start.6
  5.3 0.8 copy-done.6
  6.1 7.7 %prepare.1 = (bf16[256,768]{1,0:T(8,128)(2,1)}, bf16[384,512]{1,0:T(8,128)(2,1)}, bf16[256,256]{1,0:T(8,128)(2,1)}, f32[2,256,1024]{2,1,0:T(8,128)}) custom-call(s32[2]{0:T(128)} %pad_add_fusion.where_ref, s32[2]{0:T(128)} %count_hbm.1, s32[2,512]{1,0:T(2,128)} %src_hbm.1, s32[2,512]{1,0:T(2,128)} %dst_hbm.1, f32[2,512]{1,0:T(2,128)} %wt_hbm.1, ...), custom_call_target="tpu_custom_call" | custom-call | flops 3000000000 | bytes 6000000 | tf_op jit(solution)/shard_map/prepare/pallas_call | solution.py:404
  13.8 0.0 collective-permute-done
  13.8 0.0 copy-start.7
  13.8 0.8 copy-done.7
  14.6 0.0 copy-start.8
  14.6 0.0 copy-start.3
  14.6 6.2 %forward.1 = (f32[2,256,1024]{2,1,0:T(8,128)}, bf16[2,256,1024]{2,1,0:T(8,128)(2,1)}, s16[4,2,112,256]{3,2,1,0:T(8,128)(2,1)}) custom-call(bf16[256,1024]{1,0:T(8,128)(2,1)} %bitcast.13, bf16[1024,1024]{1,0:T(8,128)(2,1)} %w_ref.3, bf16[256,256]{1,0:T(8,128)(2,1)} %get-tuple-element.21.cfo_ref, f32[2,256,1024]{2,1,0:T(8,128)} %get-tuple-element.22.part_ref, ...), custom_call_target="tpu_custom_call" | custom-call | flops 2000000000 | bytes 8000000 | tf_op jit(solution)/shard_map/forward/pallas_call | solution.py:435
  20.8 4.2 %all-to-all-start = ((s16[4,2,112,256]{3,2,1,0:T(8,128)(2,1)}), s16[4,2,112,256]{3,2,1,0:T(8,128)(2,1)S(1)}, u32[]{:S(2)}, u32[]{:S(2)}) async-start(s16[4,2,112,256]{3,2,1,0:T(8,128)(2,1)} %get-tuple-element.23), calls=%async_computation | async-start | bytes 917504 | tf_op jit(solution)/shard_map/all_to_all | solution.py:639
  24.9 0.0 copy-done.8
  24.9 0.7 copy.14.var_hbm
  25.7 0.0 copy-done.3
  25.7 0.7 pad.13.truth_hbm
  26.3 7.3 %factors.1 = (bf16[1024,512]{1,0:T(8,128)(2,1)}, bf16[1024,512]{1,0:T(8,128)(2,1)}, f32[2,256,1024]{2,1,0:T(8,128)}) custom-call(s32[2]{0:T(128)} %pad_add_fusion.where_ref, bf16[2,128,1024]{2,1,0:T(8,128)(2,1)} %lat_ref.1, bf16[2,128,1024]{2,1,0:T(8,128)(2,1)} %copy-done.6, bf16[256,1024]{1,0:T(8,128)(2,1)} %bitcast.14, ...), custom_call_target="tpu_custom_call" | custom-call | flops 3000000000 | bytes 10000000 | tf_op jit(solution)/shard_map/factors/pallas_call | solution.py:466
  33.6 5.8 %all-to-all-done = s16[4,2,112,256]{3,2,1,0:T(8,128)(2,1)S(1)} async-done(((s16[4,2,112,256]{3,2,1,0:T(8,128)(2,1)}), s16[4,2,112,256]{3,2,1,0:T(8,128)(2,1)S(1)}, u32[]{:S(2)}, u32[]{:S(2)}) %all-to-all-start) | async-done | bytes 458784 | tf_op jit(solution)/shard_map/all_to_all | solution.py:639
  39.4 0.0 copy-start
  39.4 0.8 copy-done
  40.2 6.5 %backward.1 = (bf16[512,1152]{1,0:T(8,128)(2,1)}, bf16[512,1152]{1,0:T(8,128)(2,1)}, bf16[512,1024]{1,0:T(8,128)(2,1)}) custom-call(s32[2]{0:T(128)} %pad_add_fusion.where_ref, s16[8,112,256]{2,1,0:T(8,128)(2,1)} %bitcast.10, f32[104,256]{1,0:T(8,128)} %pad.13.truth_hbm, f32[104,1]{1,0:T(8,128)} %copy.14.var_hbm, f32[1,256]{1,0:T(1,128)} %bitcast.15, ...), custom_call_target="tpu_custom_call" | custom-call | flops 2000000000 | bytes 8000000 | tf_op jit(solution)/shard_map/backward/pallas_call | solution.py:493
  46.7 0.2 collective-permute-start.4
  46.9 3.0 %collective-permute-done.4.theirs_ref = bf16[512,1152]{1,0:T(8,128)(2,1)S(1)} collective-permute-done((bf16[512,1152]{1,0:T(8,128)(2,1)}, bf16[512,1152]{1,0:T(8,128)(2,1)S(1)}, u32[]{:S(2)}, u32[]{:S(2)}) %collective-permute-start.4) | collective-permute-done | bytes 1179680 | tf_op jit(solution)/shard_map/ppermute | solution.py:651
  49.8 0.0 copy-start.2
  49.8 1.3 %copy-done.2 = bf16[512,1152]{1,0:T(8,128)(2,1)S(1)} copy-done((bf16[512,1152]{1,0:T(8,128)(2,1)S(1)}, bf16[512,1152]{1,0:T(8,128)(2,1)}, u32[]{:S(2)}) %copy-start.2) | copy-done | bytes 1179672
  51.1 1.1 %merge.1 = bf16[512,1152]{1,0:T(8,128)(2,1)} custom-call(bf16[512,1152]{1,0:T(8,128)(2,1)S(1)} %copy-done.2, bf16[512,1152]{1,0:T(8,128)(2,1)S(1)} %collective-permute-done.4.theirs_ref), custom_call_target="tpu_custom_call" | custom-call | flops 1000000 | bytes 4000000 | tf_op jit(solution)/shard_map/merge/pallas_call | solution.py:518
  52.2 10.2 %all-to-all-start.1 = ((bf16[16,32,1152]{2,1,0:T(8,128)(2,1)}), bf16[16,32,1152]{2,1,0:T(8,128)(2,1)S(1)}, u32[]{:S(2)}, u32[]{:S(2)}) async-start(bf16[16,32,1152]{2,1,0:T(8,128)(2,1)} %bitcast.7), calls=%async_computation.1 | async-start | bytes 2359296 | tf_op jit(solution)/shard_map/all_to_all | solution.py:653
  62.4 2.9 %rows.1 = (bf16[2,128,1024]{2,1,0:T(8,128)(2,1)}, bf16[2,128,1024]{2,1,0:T(8,128)(2,1)}) custom-call(bf16[384,512]{1,0:T(8,128)(2,1)} %get-tuple-element.24.cft_hbm.cft_ref, bf16[512,1024]{1,0:T(8,128)(2,1)} %get-tuple-element.31.sg_hbm.sg_ref), custom_call_target="tpu_custom_call" | custom-call | flops 1000000000 | bytes 4000000 | tf_op jit(solution)/shard_map/rows/pallas_call | solution.py:534
  65.3 0.0 copy-start.1
  65.3 0.3 collective-permute-start.2
  65.5 0.2 collective-permute-start.3
  65.8 19.9 %all-to-all-done.1.got_ref = bf16[16,32,1152]{2,1,0:T(8,128)(2,1)S(1)} async-done(((bf16[16,32,1152]{2,1,0:T(8,128)(2,1)}), bf16[16,32,1152]{2,1,0:T(8,128)(2,1)S(1)}, u32[]{:S(2)}, u32[]{:S(2)}) %all-to-all-start.1) | async-done | bytes 1179680 | tf_op jit(solution)/shard_map/all_to_all | solution.py:653
  85.7 0.9 plane.1
  86.6 8.7 %all-to-all-start.2 = ((bf16[8,16,1152]{2,1,0:T(8,128)(2,1)}), bf16[8,16,1152]{2,1,0:T(8,128)(2,1)S(1)}, u32[]{:S(2)}, u32[]{:S(2)}) async-start(bf16[8,16,1152]{2,1,0:T(8,128)(2,1)} %bitcast.8), calls=%async_computation.2 | async-start | bytes 589824 | tf_op jit(solution)/shard_map/all_to_all | solution.py:658
  95.2 0.0 copy-done.1
  95.2 1.8 %score.1 = f32[100,256]{1,0:T(8,128)} custom-call(s16[8,112,256]{2,1,0:T(8,128)(2,1)S(1)} %bitcast.11, f32[100,256]{1,0:T(8,128)S(1)} %copy-done.3), custom_call_target="tpu_custom_call" | custom-call | flops 10000000 | bytes 1000000 | tf_op jit(solution)/shard_map/score/pallas_call | solution.py:571
  97.1 0.0 collective-permute-done.2.core_ref
  97.1 0.0 copy-start.4
  97.1 0.0 collective-permute-done.3.odd_ref
  97.1 0.8 copy-done.4
  97.9 0.0 copy-start.5
  97.9 0.8 copy-done.5
  98.7 5.2 %latent.1 = bf16[2,128,1024]{2,1,0:T(8,128)(2,1)} custom-call(bf16[384,512]{1,0:T(8,128)(2,1)} %get-tuple-element.24.cft_hbm.cft_ref, bf16[512,1024]{1,0:T(8,128)(2,1)} %get-tuple-element.31.sg_hbm.sg_ref, bf16[2,128,1024]{2,1,0:T(8,128)(2,1)} %copy-done.4, bf16[2,128,1024]{2,1,0:T(8,128)(2,1)} %copy-done.5, bf16[1024,1024]{1,0:T(8,128)(2,1)} %w_ref.3), custom_call_target="tpu_custom_call" | custom-call | flops 1000000000 | bytes 5000000 | tf_op jit(solution)/shard_map/latent/pallas_call | solution.py:585
  103.9 2.6 %all-to-all-done.2.got_ref = bf16[8,16,1152]{2,1,0:T(8,128)(2,1)S(1)} async-done(((bf16[8,16,1152]{2,1,0:T(8,128)(2,1)}), bf16[8,16,1152]{2,1,0:T(8,128)(2,1)S(1)}, u32[]{:S(2)}, u32[]{:S(2)}) %all-to-all-start.2) | async-done | bytes 294944 | tf_op jit(solution)/shard_map/all_to_all | solution.py:658
  106.5 0.7 final.1
  (1 shorter events, 0.0 us)
Async XLA Ops:
  0.6 4.7 %collective-permute-start.1 = (bf16[2,128,1024]{2,1,0:T(8,128)(2,1)}, bf16[2,128,1024]{2,1,0:T(8,128)(2,1)S(1)}, u32[]{:S(2)}, u32[]{:S(2)}) collective-permute-start(bf16[2,128,1024]{2,1,0:T(8,128)(2,1)} %lat_ref.1), channel_id=1, source_target_pairs={{0,1},{1,0},{2,3},{3,2},{4,5},{5,4},{6,7},{7,6},{8,9},{9,8},{10,11... | collective-permute-start | bytes 1572872 | tf_op jit(solution)/shard_map/ppermute | solution.py:633
  0.7 13.0 %collective-permute-start = (bf16[2,128,1024]{2,1,0:T(8,128)(2,1)}, bf16[2,128,1024]{2,1,0:T(8,128)(2,1)S(1)}, u32[]{:S(2)}, u32[]{:S(2)}) collective-permute-start(bf16[2,128,1024]{2,1,0:T(8,128)(2,1)} %lat_ref.1), channel_id=1, source_target_pairs={{0,63},{1,2},{2,1},{3,4},{4,3},{5,6},{6,5},{7,8},{8,7},{9,10},{10,... | collective-permute-start | bytes 1572872 | tf_op jit(solution)/shard_map/ppermute | solution.py:632
  5.3 0.8 copy-start.6
  13.8 0.8 copy-start.7
  14.6 10.4 %copy-start.8 = (f32[100]{0:T(128)S(1)}, f32[100]{0:T(128)}, u32[]{:S(2)}) copy-start(f32[100]{0:T(128)} %param.15) | copy-start | bytes 1204
  14.6 11.1 %copy-start.3 = (f32[100,256]{1,0:T(8,128)S(1)}, f32[100,256]{1,0:T(8,128)}, u32[]{:S(2)}) copy-start(f32[100,256]{1,0:T(8,128)} %truth_ref.1) | copy-start | bytes 307204
  20.8 18.7 %all-to-all-start = ((s16[4,2,112,256]{3,2,1,0:T(8,128)(2,1)}), s16[4,2,112,256]{3,2,1,0:T(8,128)(2,1)S(1)}, u32[]{:S(2)}, u32[]{:S(2)}) async-start(s16[4,2,112,256]{3,2,1,0:T(8,128)(2,1)} %get-tuple-element.23), calls=%async_computation | async-start | bytes 917504 | tf_op jit(solution)/shard_map/all_to_all | solution.py:639
  39.4 0.8 copy-start
  46.7 3.1 %collective-permute-start.4 = (bf16[512,1152]{1,0:T(8,128)(2,1)}, bf16[512,1152]{1,0:T(8,128)(2,1)S(1)}, u32[]{:S(2)}, u32[]{:S(2)}) collective-permute-start(bf16[512,1152]{1,0:T(8,128)(2,1)} %get-tuple-element.35), channel_id=1, source_target_pairs={{0,1},{1,0},{2,3},{3,2},{4,5},{5,4},{6,7},{7,6},{8,9},{9,8},{10,11... | collective-permute-start | bytes 3538952 | tf_op jit(solution)/shard_map/ppermute | solution.py:651
  49.8 1.3 %copy-start.2 = (bf16[512,1152]{1,0:T(8,128)(2,1)S(1)}, bf16[512,1152]{1,0:T(8,128)(2,1)}, u32[]{:S(2)}) copy-start(bf16[512,1152]{1,0:T(8,128)(2,1)} %get-tuple-element.34.mine_ref) | copy-start | bytes 3538948
  52.2 33.5 %all-to-all-start.1 = ((bf16[16,32,1152]{2,1,0:T(8,128)(2,1)}), bf16[16,32,1152]{2,1,0:T(8,128)(2,1)S(1)}, u32[]{:S(2)}, u32[]{:S(2)}) async-start(bf16[16,32,1152]{2,1,0:T(8,128)(2,1)} %bitcast.7), calls=%async_computation.1 | async-start | bytes 2359296 | tf_op jit(solution)/shard_map/all_to_all | solution.py:653
  65.3 30.0 %copy-start.1 = (s16[4,2,112,256]{3,2,1,0:T(8,128)(2,1)S(1)}, s16[4,2,112,256]{3,2,1,0:T(8,128)(2,1)}, u32[]{:S(2)}) copy-start(s16[4,2,112,256]{3,2,1,0:T(8,128)(2,1)} %copy-done) | copy-start | bytes 1376260
  65.3 31.8 %collective-permute-start.2 = (bf16[2,128,1024]{2,1,0:T(8,128)(2,1)}, bf16[2,128,1024]{2,1,0:T(8,128)(2,1)S(1)}, u32[]{:S(2)}, u32[]{:S(2)}) collective-permute-start(bf16[2,128,1024]{2,1,0:T(8,128)(2,1)} %get-tuple-element.32), channel_id=1, source_target_pairs={{0,1},{1,0},{2,3},{3,2},{4,5},{5,4},{6,7},{7,6},{8,9},{9,8},{10,11... | collective-permute-start | bytes 1572872 | tf_op jit(solution)/shard_map/ppermute | solution.py:656
  65.5 31.5 %collective-permute-start.3 = (bf16[2,128,1024]{2,1,0:T(8,128)(2,1)}, bf16[2,128,1024]{2,1,0:T(8,128)(2,1)S(1)}, u32[]{:S(2)}, u32[]{:S(2)}) collective-permute-start(bf16[2,128,1024]{2,1,0:T(8,128)(2,1)} %get-tuple-element.33), channel_id=1, source_target_pairs={{0,63},{1,2},{2,1},{3,4},{4,3},{5,6},{6,5},{7,8},{8,7},{9,10},{10,... | collective-permute-start | bytes 1572872 | tf_op jit(solution)/shard_map/ppermute | solution.py:655
  86.6 20.0 %all-to-all-start.2 = ((bf16[8,16,1152]{2,1,0:T(8,128)(2,1)}), bf16[8,16,1152]{2,1,0:T(8,128)(2,1)S(1)}, u32[]{:S(2)}, u32[]{:S(2)}) async-start(bf16[8,16,1152]{2,1,0:T(8,128)(2,1)} %bitcast.8), calls=%async_computation.2 | async-start | bytes 589824 | tf_op jit(solution)/shard_map/all_to_all | solution.py:658
  97.1 0.8 copy-start.4
  97.9 0.8 copy-start.5

commit v4 on v3

v4 whole, which is shorter than its diff:
```python
import functools
import math

import jax
import jax.numpy as jnp
from jax import lax
from jax.experimental import pallas as pl
from jax.experimental.pallas import tpu as pltpu
from jax.sharding import PartitionSpec as P

HALO = 128
BLK = 128
ALPHA = 0.95
DELTA = 0.05
SPACE = ("zhi", "x", "y", "core")
QMAX = 32000.0
VPAD = 128
VROWS = 112
VUSE = 104
TILE = 256
GELU_C = math.sqrt(2.0 / math.pi)
MIB = 1 << 20
LIMIT = 24
PREP = 53
F32 = jnp.float32
BF16 = jnp.bfloat16


def dot(a, b):
    return jnp.dot(a, b, preferred_element_type=F32)


def dot_nt(a, b):
    return lax.dot_general(a, b, (((1,), (1,)), ((), ())), preferred_element_type=F32)


def smem(count):
    return [pl.BlockSpec(memory_space=pltpu.SMEM)] * count


def cost(flops, nbytes):
    return pl.CostEstimate(flops=flops, bytes_accessed=nbytes, transcendentals=0)


def params(mib):
    return pltpu.CompilerParams(vmem_limit_bytes=mib * MIB)


def hbm(count):
    return [pl.BlockSpec(memory_space=pltpu.HBM)] * count


def vmem(count):
    return [pl.BlockSpec(memory_space=pltpu.VMEM)] * count


def anywhere(count):
    return [pl.BlockSpec(memory_space=pl.ANY)] * count


def start_copy(src, dst, sem):
    copy = pltpu.make_async_copy(src, dst, sem)
    copy.start()
    return copy


def pair_factor(members):
    fair_eps = (1.0 - ALPHA) / members
    return (1.0 - fair_eps) / (2.0 * members * (members - 1))


def smooth_abs(distance):
    square = distance * distance + DELTA * DELTA
    return square * lax.rsqrt(square)


def signum(distance):
    return distance * lax.rsqrt(distance * distance + DELTA * DELTA)


def prepare_kernel(
    where_ref, count_hbm, src_hbm, dst_hbm, wt_hbm, lat_hbm, clat_hbm, w_hbm,
    cf_ref, cft_hbm, cfo_ref, part_ref,
    count_ref, src_ref, dst_ref, wt_ref, x_ref, w_ref, cft_ref, in_sem, out_sem,
):
    edges = [
        start_copy(src, dst, in_sem.at[k])
        for k, (src, dst) in enumerate(
            ((count_hbm, count_ref), (src_hbm, src_ref), (dst_hbm, dst_ref), (wt_hbm, wt_ref))
        )
    ]
    local = lat_hbm.shape[0]
    inputs = []
    for m in range(local):
        for k, ref in enumerate((lat_hbm, clat_hbm)):
            inputs.append(
                start_copy(
                    ref.at[m],
                    x_ref.at[pl.ds((2 * m + k) * HALO, HALO)],
                    in_sem.at[4 + 2 * m + k],
                )
            )
    inputs.append(start_copy(w_hbm, w_ref, in_sem.at[4 + 2 * local]))
    core = where_ref[0]
    slots = src_ref.shape[1]
    window = cf_ref.shape[1] // 2
    points = cf_ref.shape[0]
    for copy in edges:
        copy.wait()
    for b in range(src_ref.shape[0]):
        src = src_ref[b : b + 1, :]
        slot = lax.broadcasted_iota(jnp.int32, (1, slots), 1)
        wt = jnp.where(slot < count_ref[b], wt_ref[b : b + 1, :], 0.0)
        left = 2 * HALO - HALO * core
        right = HALO + HALO * core
        place = jnp.where(
            src < HALO,
            src + left,
            jnp.where(src < 2 * HALO, src - HALO, src - 2 * HALO + right),
        )
        rows = lax.broadcasted_iota(jnp.int32, (window, slots), 0)
        hot = jnp.where(rows == place, 1.0, 0.0).astype(BF16)
        pts = lax.broadcasted_iota(jnp.int32, (BLK, slots), 0)
        mat = jnp.where(pts == dst_ref[b : b + 1, :], wt, 0.0).astype(BF16)
        coef = dot_nt(mat, hot)
        high = coef.astype(BF16)
        low = (coef - high.astype(F32)).astype(BF16)
        at = slice(b * BLK, (b + 1) * BLK)
        cf_ref[at, :window] = high
        cf_ref[at, window:] = low
        cfo_ref[at, :HALO] = high[:, 2 * HALO :]
        cfo_ref[at, HALO:] = low[:, 2 * HALO :]
        coef_t = dot_nt(hot, mat)
        high_t = coef_t.astype(BF16)
        cft_ref[:, b * BLK : (b + 1) * BLK] = high_t
        cft_ref[:, points + b * BLK : points + (b + 1) * BLK] = (
            coef_t - high_t.astype(F32)
        ).astype(BF16)
    out = start_copy(cft_ref, cft_hbm, out_sem)
    for copy in inputs:
        copy.wait()
    x = x_ref[...]
    high = cf_ref[:, : 2 * HALO]
    low = cf_ref[:, window : window + 2 * HALO]
    for j in range(w_ref.shape[1] // TILE):
        at = slice(j * TILE, (j + 1) * TILE)
        p = dot(x, w_ref[:, at]).astype(BF16)
        for m in range(local):
            pm = p[2 * m * HALO : (2 * m + 2) * HALO]
            part_ref[m, :, at] = dot(high, pm) + dot(low, pm)
    out.wait()


def forward_kernel(
    odd_ref, w_ref, cfo_ref, part_ref, dpt_ref, summed_ref, hidden_ref, code_ref
):
    local, points, depth = part_ref.shape
    forecast = [jnp.zeros((VPAD, points), F32) for _ in range(local)]
    for j in range(depth // TILE):
        at = slice(j * TILE, (j + 1) * TILE)
        p = dot(odd_ref[...], w_ref[:, at]).astype(BF16)
        for m in range(local):
            pm = p[m * HALO : (m + 1) * HALO]
            s = part_ref[m, :, at] + dot(cfo_ref[...], jnp.concatenate([pm, pm], axis=0))
            summed_ref[m, :, at] = s
            t = jnp.tanh(s * (GELU_C + (GELU_C * 0.044715) * (s * s)))
            h = (0.5 * s * (1.0 + t)).astype(BF16)
            hidden_ref[m, :, at] = h
            forecast[m] = forecast[m] + dot_nt(dpt_ref[:, at], h)
    for m in range(local):
        f = forecast[m]
        largest = jnp.maximum(jnp.max(jnp.abs(f), axis=1, keepdims=True), 1e-30)
        power = jnp.ceil(jnp.log(largest) * (1.0 / math.log(2.0)) + 1e-3)
        power = jnp.broadcast_to(power, (VPAD, VPAD))
        q = f * (jnp.exp2(-power[:, :1]) * QMAX)
        q = jnp.where(q >= 0.0, q + 0.5, q - 0.5)
        row = jnp.concatenate([power.T[:8], jnp.zeros((8, points - VPAD), F32)], axis=1)
        row = jnp.where(row >= 0.0, row + 0.5, row - 0.5)
        code = jnp.concatenate([q[:VUSE], row], axis=0)
        code_ref[m] = code.astype(jnp.int32).astype(jnp.int16)


def factors_kernel(
    where_ref, lat_ref, clat_ref, olat_ref, cf_ref, summed_ref, hidden_ref,
    aggt_ref, hidt_ref, slope_ref, x_ref,
):
    core = where_ref[0]
    window = cf_ref.shape[1] // 2
    local, points, depth = summed_ref.shape
    high = cf_ref[:, :window]
    low = cf_ref[:, window:]
    for m in range(local):
        x_ref[:HALO] = lat_ref[m]
        x_ref[HALO : 2 * HALO] = clat_ref[m]
        x_ref[2 * HALO :] = olat_ref[m * HALO : (m + 1) * HALO]
        cols = slice(m * points, (m + 1) * points)
        for j in range(depth // TILE):
            at = slice(j * TILE, (j + 1) * TILE)
            x = x_ref[:, at]
            agg = (dot(high, x) + dot(low, x)).T.astype(BF16)
            hid = hidden_ref[m, :, at].astype(F32).T.astype(BF16)
            for k in range(TILE // 16):
                block = j * (TILE // 16) + k
                zhi, rest = divmod(block, 32)
                xy, c = divmod(rest, 2)
                to = lax.bitwise_xor(core, c) * (depth // 2) + (xy * 32 + zhi * 16)
                to = pl.ds(pl.multiple_of(to, 16), 16)
                aggt_ref[to, cols] = agg[k * 16 : (k + 1) * 16]
                hidt_ref[to, cols] = hid[k * 16 : (k + 1) * 16]
            s = summed_ref[m, :, at]
            t = jnp.tanh(s * (GELU_C + (GELU_C * 0.044715) * (s * s)))
            slope_ref[m, :, at] = 0.5 * (1.0 + t) + (0.5 * GELU_C) * s * (1.0 - t * t) * (
                1.0 + 3.0 * 0.044715 * (s * s)
            )


def decode(where_ref, code_refs, f_ref):
    local = code_refs[0].shape[0]
    rows = [
        ref[m, VROWS - 8 :, :].astype(jnp.int32).astype(F32)[:1, :VPAD]
        for ref in code_refs
        for m in range(local)
    ]
    rows.append(jnp.zeros((VPAD - len(rows), VPAD), F32))
    power = (jnp.exp2(jnp.concatenate(rows, axis=0)) * (1.0 / QMAX)).T
    for k, ref in enumerate(code_refs):
        first = lax.bitwise_xor(where_ref[1], k) * local
        for m in range(local):
            code = ref[m].astype(jnp.int32).astype(F32)[:VUSE]
            at = k * local + m
            f_ref[first + m] = code * power[:VUSE, at : at + 1]


def score_kernel(where_ref, c0_ref, c1_ref, c2_ref, c3_ref, truth_ref, score_ref, f_ref):
    members = f_ref.shape[0]
    nvar = truth_ref.shape[0]
    decode(where_ref, (c0_ref, c1_ref, c2_ref, c3_ref), f_ref)
    collected = [f_ref[m][:nvar] for m in range(members)]
    truth = truth_ref[...]
    skill = sum(smooth_abs(f - truth) for f in collected)
    spread = jnp.zeros_like(skill)
    for m in range(members):
        for o in range(m + 1, members):
            spread = spread + smooth_abs(collected[m] - collected[o])
    score_ref[...] = skill * (1.0 / members) - (pair_factor(members) * 2.0) * spread


def backward_kernel(
    where_ref, c0_ref, c1_ref, c2_ref, c3_ref, truth_ref, var_ref, area_ref, dpt_ref,
    aggt_ref, hidt_ref, slope_ref, mine_ref, theirs_ref, sg_ref, f_ref, g_ref,
):
    members = f_ref.shape[0]
    nvar = truth_ref.shape[0]
    local, points, depth = slope_ref.shape
    half = depth // 2
    decode(where_ref, (c0_ref, c1_ref, c2_ref, c3_ref), f_ref)
    first = where_ref[1] * local
    truth = truth_ref[...]
    g_ref[96:] = jnp.zeros((VPAD - 96, points), F32)
    grads = []
    for m in range(local):
        own = f_ref[first + m][:nvar]
        mutual = sum(signum(own - f_ref[o][:nvar]) for o in range(members))
        g_ref[:nvar] = area_ref[...] * (
            signum(own - truth) * (1.0 / members) - (2.0 * pair_factor(members)) * mutual
        )
        grads.append((g_ref[...].T * var_ref[...]).astype(BF16))
    grad = jnp.concatenate(grads, axis=0)
    out = dot(hidt_ref[...], grad).astype(BF16)
    mine_ref[:, depth:] = out[:half]
    theirs_ref[:, depth:] = out[half:]
    for j in range(depth // TILE):
        at = slice(j * TILE, (j + 1) * TILE)
        hg = dot(grad, dpt_ref[:, at])
        for m in range(local):
            rows = slice(m * points, (m + 1) * points)
            sg_ref[rows, at] = (hg[rows] * slope_ref[m, :, at]).astype(BF16)
        part = dot(aggt_ref[...], sg_ref[:, at]).astype(BF16)
        mine_ref[:, at] = part[:half]
        theirs_ref[:, at] = part[half:]


def merge_kernel(mine_ref, theirs_ref, out_hbm, out_ref, out_sem):
    rows = mine_ref.shape[0] // 4
    outs = []
    for k in range(4):
        at = slice(k * rows, (k + 1) * rows)
        out_ref[at] = (mine_ref[at].astype(F32) + theirs_ref[at].astype(F32)).astype(BF16)
        cut = pl.ds(k * rows, rows)
        outs.append(start_copy(out_ref.at[cut], out_hbm.at[cut], out_sem.at[k]))
    for copy in outs:
        copy.wait()


def rows_kernel(cft_ref, sg_ref, core_hbm, odd_hbm, core_ref, odd_ref, out_sem):
    local, _, depth = core_ref.shape
    points = cft_ref.shape[1] // 2
    high = cft_ref[HALO:, :points]
    low = cft_ref[HALO:, points:]
    outs = []
    for m in range(local):
        for j in range(depth // TILE):
            at = slice(j * TILE, (j + 1) * TILE)
            s = sg_ref[m * points : (m + 1) * points, at]
            g = (dot(high, s) + dot(low, s)).astype(BF16)
            core_ref[m, :, at] = g[:HALO]
            odd_ref[m, :, at] = g[HALO:]
        outs.append(start_copy(odd_ref.at[m], odd_hbm.at[m], out_sem.at[0, m]))
        outs.append(start_copy(core_ref.at[m], core_hbm.at[m], out_sem.at[1, m]))
    for copy in outs:
        copy.wait()


def plane_kernel(got_ref, out_hbm, out_ref, out_sem):
    per = out_hbm.shape[2]
    outs = []
    for z in range(out_hbm.shape[0]):
        at = slice(z * per, (z + 1) * per)
        total = got_ref[0, at].astype(F32)
        for k in range(1, got_ref.shape[0]):
            total = total + got_ref[k, at].astype(F32)
        out_ref[z] = total.astype(BF16)
        for e in range(out_hbm.shape[1]):
            outs.append(start_copy(out_ref.at[z], out_hbm.at[z, e], out_sem.at[z, e]))
    for copy in outs:
        copy.wait()


def final_kernel(got_ref, src_ref, out_ref, *, scaling):
    total = got_ref[0].astype(F32)
    for k in range(1, got_ref.shape[0]):
        total = total + got_ref[k].astype(F32)
    total = total * scaling
    depth = src_ref.shape[1]
    src_ref[...] = total[:, :depth]
    out_ref[...] = total[:, depth : depth + out_ref.shape[1]]


def latent_kernel(
    cft_ref, sg_ref, w_ref, core_ref, odd_ref, out_hbm, g_ref, out_ref, out_sem
):
    local, rows, depth = core_ref.shape
    points = cft_ref.shape[1] // 2
    steps = depth // TILE
    high = cft_ref[:HALO, :points]
    low = cft_ref[:HALO, points:]
    for m in range(local):
        for j in range(steps):
            at = slice(j * TILE, (j + 1) * TILE)
            s = sg_ref[m * points : (m + 1) * points, at]
            g = dot(high, s) + dot(low, s)
            g = g + core_ref[m, :, at].astype(F32) + odd_ref[m, :, at].astype(F32)
            g_ref[m * HALO : (m + 1) * HALO, at] = g.astype(BF16)
    outs = []
    for j in range(steps):
        at = slice(j * TILE, (j + 1) * TILE)
        r = dot_nt(g_ref[...], w_ref[at, :]).astype(BF16)
        for m in range(local):
            out_ref[m, :, at] = r[m * HALO : (m + 1) * HALO]
        cols = pl.ds(j * TILE, TILE)
        outs.append(start_copy(out_ref.at[:, :, cols], out_hbm.at[:, :, cols], out_sem.at[j]))
    for copy in outs:
        copy.wait()


def shape(dims, dtype):
    return jax.ShapeDtypeStruct(dims, dtype)


def scratch(*arrays):
    return [pltpu.VMEM(a.shape, a.dtype) for a in arrays]


def sems(*dims):
    return pltpu.SemaphoreType.DMA(dims)


def call(
    kernel, name, out_shape, in_specs, out_specs, scratch_shapes, work, operands, limit=LIMIT
):
    return pl.pallas_call(
        kernel,
        out_shape=out_shape,
        in_specs=in_specs,
        out_specs=out_specs,
        scratch_shapes=scratch_shapes,
        compiler_params=params(limit),
        cost_estimate=cost(*work),
        name=name,
    )(*operands)


def call_prepare(where, edge_count, edge_src, edge_dst, edge_weight, latent, core_lat, weight):
    local, rows, depth = latent.shape
    window = rows + 2 * HALO
    points = edge_src.shape[0] * BLK
    cf = shape((points, 2 * window), BF16)
    cft = shape((window, 2 * points), BF16)
    return call(
        prepare_kernel,
        "prepare",
        (cf, cft, shape((points, 2 * HALO), BF16), shape((local, points, depth), F32)),
        smem(1) + hbm(5) + anywhere(1) + hbm(1),
        tuple(vmem(1) + hbm(1) + vmem(2)),
        [pltpu.SMEM(edge_count.shape, jnp.int32)]
        + scratch(edge_src, edge_dst, edge_weight)
        + [pltpu.VMEM((local * 2 * HALO, depth), BF16)]
        + scratch(weight, cft)
        + [sems(5 + 2 * local), pltpu.SemaphoreType.DMA],
        (3 * 10**9, 6 * 10**6),
        (where, edge_count, edge_src, edge_dst, edge_weight, latent, core_lat, weight),
        PREP,
    )


def call_forward(odd_lat, weight, cfo, part, dpt):
    local, points, depth = part.shape
    return call(
        forward_kernel,
        "forward",
        (
            shape(part.shape, F32),
            shape(part.shape, BF16),
            shape((local, VROWS, points), jnp.int16),
        ),
        vmem(5),
        tuple(vmem(3)),
        [],
        (2 * 10**9, 8 * 10**6),
        (odd_lat, weight, cfo, part, dpt),
    )


def call_factors(where, latent, core_lat, odd_lat, cf, summed, hidden):
    local, points, depth = summed.shape
    left = shape((depth, local * points), BF16)
    return call(
        factors_kernel,
        "factors",
        (left, left, shape(summed.shape, F32)),
        smem(1) + vmem(6),
        tuple(vmem(3)),
        [pltpu.VMEM((cf.shape[1] // 2, depth), BF16)],
        (3 * 10**9, 10 * 10**6),
        (where, latent, core_lat, odd_lat, cf, summed, hidden),
    )


def call_backward(where, codes, truth, var_row, area_row, dpt, aggt, hidt, slope):
    local, points, depth = slope.shape
    part = shape((depth // 2, depth + VPAD), BF16)
    return call(
        backward_kernel,
        "backward",
        (part, part, shape((local * points, depth), BF16)),
        smem(1) + vmem(len(codes) + 7),
        tuple(vmem(3)),
        [
            pltpu.VMEM((local * len(codes), VUSE, points), F32),
            pltpu.VMEM((VPAD, points), F32),
        ],
        (2 * 10**9, 5 * 10**6),
        (where, *codes, truth, var_row, area_row, dpt, aggt, hidt, slope),
    )


def call_merge(mine, theirs):
    return call(
        merge_kernel,
        "merge",
        shape(mine.shape, BF16),
        vmem(2),
        hbm(1)[0],
        scratch(mine) + [sems(4)],
        (10**6, 4 * 10**6),
        (mine, theirs),
    )


def call_rows(cft, summed_grad, local):
    send = shape((local, HALO, summed_grad.shape[1]), BF16)
    return call(
        rows_kernel,
        "rows",
        (send, send),
        vmem(2),
        tuple(hbm(2)),
        scratch(send, send) + [sems(2, local)],
        (10**9, 3 * 10**6),
        (cft, summed_grad),
    )


def call_plane(got, ens):
    out_shape = shape((2, ens, got.shape[1] // 2, got.shape[2]), BF16)
    return call(
        plane_kernel,
        "plane",
        out_shape,
        vmem(1),
        hbm(1)[0],
        [pltpu.VMEM((2,) + out_shape.shape[2:], BF16), sems(2, ens)],
        (10**6, 10**6),
        (got,),
    )


def call_score(where, codes, truth):
    local, _, points = codes[0].shape
    return call(
        score_kernel,
        "score",
        shape(truth.shape, F32),
        smem(1) + vmem(len(codes) + 1),
        vmem(1)[0],
        [pltpu.VMEM((local * len(codes), VUSE, points), F32)],
        (10**7, 10**6),
        (where, *codes, truth),
    )


def call_latent(cft, summed_grad, weight, core_grad, odd_grad):
    local, rows, depth = core_grad.shape
    return call(
        latent_kernel,
        "latent",
        shape(core_grad.shape, BF16),
        vmem(5),
        hbm(1)[0],
        [pltpu.VMEM((local * rows, depth), BF16)]
        + scratch(core_grad)
        + [sems(depth // TILE)],
        (10**9, 5 * 10**6),
        (cft, summed_grad, weight, core_grad, odd_grad),
    )


def call_final(got, nvar, scaling):
    per = got.shape[1]
    return call(
        functools.partial(final_kernel, scaling=scaling),
        "final",
        (shape((per, got.shape[2] - VPAD), F32), shape((per, nvar), F32)),
        vmem(1),
        tuple(vmem(2)),
        [],
        (10**5, 4 * 10**5),
        (got,),
    )


def make_body(count):
    odd_pairs = [(i, (i + 1) % count if i % 2 else (i - 1) % count) for i in range(count)]
    swap = [(0, 1), (1, 0)]

    def body(
        latent, src_weight, decoder_projection, truth, area_weight, var_weight,
        edge_src, edge_dst, edge_weight, edge_count,
    ):
        local, rows, depth = latent.shape
        ens = lax.axis_size("ens")
        members = local * ens
        nvar = decoder_projection.shape[1]
        points = truth.shape[1]
        per = depth // count
        where = jnp.stack([lax.axis_index("core"), lax.axis_index("ens")]).astype(jnp.int32)

        odd_lat = lax.ppermute(latent, SPACE, odd_pairs).reshape(local * rows, depth)
        core_lat = lax.ppermute(latent, "core", swap)
        dpt = jnp.pad(decoder_projection.T, ((0, VPAD - nvar), (0, 0)))
        cf, cft, cfo, part = call_prepare(
            where, edge_count, edge_src, edge_dst, edge_weight, latent, core_lat, src_weight
        )
        var_row = jnp.pad(var_weight, (0, VPAD - nvar)).reshape(1, VPAD)
        area_row = area_weight.reshape(1, points)
        summed, hidden, coded = call_forward(odd_lat, src_weight, cfo, part, dpt)
        codes = [coded] + [
            lax.ppermute(coded, "ens", [(e, e ^ k) for e in range(ens)]) for k in range(1, ens)
        ]
        aggt, hidt, slope = call_factors(
            where, latent, core_lat, odd_lat, cf, summed, hidden
        )
        mine, theirs, summed_grad = call_backward(
            where, codes, truth, var_row, area_row, dpt, aggt, hidt, slope
        )
        theirs = lax.ppermute(theirs, "core", swap)
        part = call_merge(mine, theirs)
        core_send, odd_send = call_rows(cft, summed_grad, local)
        part = part.reshape(16, 2 * per, part.shape[1])
        got = lax.all_to_all(part, ("x", "y"), 0, 0, tiled=True)
        odd_grad = lax.ppermute(odd_send, SPACE, odd_pairs)
        core_grad = lax.ppermute(core_send, "core", swap)
        plane = call_plane(got, ens).reshape(2 * ens, per, got.shape[2])
        got = lax.all_to_all(plane, ("zhi", "ens"), 0, 0, tiled=True)
        score = call_score(where, codes, truth)
        grad_latent = call_latent(cft, summed_grad, src_weight, core_grad, odd_grad)
        scaling = 1.0 / math.sqrt(members * points * count)
        grad_src, grad_out = call_final(got, nvar, scaling)
        return score, grad_latent, grad_src, grad_out

    return body


def solution(mesh):
    fine = jax.sharding.Mesh(
        mesh.devices.reshape(mesh.devices.shape[0], 2, 4, 4, 2), ("ens",) + SPACE
    )
    return jax.shard_map(
        make_body(mesh.devices.shape[1]),
        mesh=fine,
        in_specs=(
            P("ens", SPACE, None), P(), P(), P(None, SPACE), P(SPACE), P(),
            P(SPACE, None), P(SPACE, None), P(SPACE, None), P(SPACE),
        ),
        out_specs=(P(None, SPACE), P("ens", SPACE, None), P(SPACE, None), P(SPACE, None)),
        check_vma=False,
    )
```

time: 108 us -> 99.1 us (0.918)
  Pallas kernels: 40.2 us -> 28.2 us
  local copies, waits for them, and re-layouts: 8.28 us -> 15.1 us
  waiting for transfers between devices: 31.3 us -> 25.6 us
  starting transfers between devices: 26 us -> 28.6 us
    pallas_call x10, Pallas kernels: 40.2 us -> 28.2 us  [call(): pl.pallas_call(kernel, out_shape=out_shape, in_specs=in_specs, out_specs=...]
    all_to_all x3 -> x2, waiting for transfers between devices: 28.4 us -> 19.3 us  [the longest x1 19.2 us: body(): got = lax.all_to_all(part, ('x', 'y'), 0, 0, tiled=True)]
    unnamed x18 -> x54, local copies, waits for them, and re-layouts: 5.24 us -> 13.5 us
    ppermute x0 -> x3, starting transfers between devices: none -> 4.45 us  [body(): lax.ppermute(coded, 'ens', [(e, e ^ k) for e in range(ens)])]
    ppermute x0 -> x3, waiting for transfers between devices: none -> 3.7 us  [body(): lax.ppermute(coded, 'ens', [(e, e ^ k) for e in range(ens)])]
    all_to_all x3 -> x2, starting transfers between devices: 23 us -> 20.9 us  [the longest x1 12.2 us: body(): got = lax.all_to_all(part, ('x', 'y'), 0, 0, tiled=True)]
  transfers between devices with their start and end apart: 8 -> 10, of which waited for: 4 -> 4; matrix products, arithmetic and copies ran while one was open for 3% -> 2% of each run, Pallas kernels for 24% -> 20%
where the time goes in v4:
time: 99.1 us; the launch traced here: 98.3 us
  starting transfers between devices  28.6 us (29%)
  Pallas kernels  28.2 us (28%)
  waiting for transfers between devices  25.6 us (26%)
  local copies, waits for them, and re-layouts  15.1 us (15%)
    pallas_call x10, Pallas kernels, call(): pl.pallas_call(kernel, out_shape=out_shape, in_specs=in_specs, out_specs=...  28.2 us
    all_to_all x1, waiting for transfers between devices, body(): got = lax.all_to_all(part, ('x', 'y'), 0, 0, tiled=True)  19.2 us
    unnamed x54, local copies, waits for them, and re-layouts  13.5 us
    all_to_all x1, starting transfers between devices, body(): got = lax.all_to_all(part, ('x', 'y'), 0, 0, tiled=True)  12.2 us
    all_to_all x1, starting transfers between devices, body(): got = lax.all_to_all(plane, ('zhi', 'ens'), 0, 0, tiled=True)  8.72 us
    ppermute x3, starting transfers between devices, body(): lax.ppermute(coded, 'ens', [(e, e ^ k) for e in range(ens)])  4.45 us
    ppermute x3, waiting for transfers between devices, body(): lax.ppermute(coded, 'ens', [(e, e ^ k) for e in range(ens)])  3.7 us
    ppermute x1, waiting for transfers between devices, body(): theirs = lax.ppermute(theirs, 'core', swap)  2.52 us
  transfers between devices with their start and end apart: 10, of which 4 were waited for; matrix products, arithmetic and copies ran while one was open for 2% of the time, Pallas kernels for 20%

profile of v4, /device:TPU:8, one launch (start us, length us, event | category | flops | bytes accessed | tf_op | source)
XLA Modules:
  0.0 98.3 jit_solution(3989133823631398856)
XLA Ops:
  0.6 0.1 collective-permute-start.1
  0.7 2.3 %collective-permute-start = (bf16[2,128,1024]{2,1,0:T(8,128)(2,1)}, bf16[2,128,1024]{2,1,0:T(8,128)(2,1)}, u32[]{:S(2)}, u32[]{:S(2)}) collective-permute-start(bf16[2,128,1024]{2,1,0:T(8,128)(2,1)} %lat_ref.1), channel_id=1, source_target_pairs={{0,63},{1,2},{2,1},{3,4},{4,3},{5,6},{6,5},{7,8},{8,7},{9,10},{10,... | collective-permute-start | bytes 1572872 | tf_op jit(solution)/shard_map/ppermute | solution.py:568
  3.0 1.0 pad.8.dpt_ref
  4.0 0.7 pad_bitcast_fusion.var_ref
  4.6 0.1 pad_add_fusion.where_ref
  4.7 0.0 collective-permute-done.1.clat_hbm.clat_ref
  4.7 0.8 copy-done.19
  5.5 0.7 copy-done.21
  6.2 0.7 copy-done.22
  6.9 0.7 copy-done.23
  7.6 0.7 copy-done.25
  8.3 7.5 %prepare.1 = (bf16[256,768]{1,0:T(8,128)(2,1)S(1)}, bf16[384,512]{1,0:T(8,128)(2,1)S(1)}, bf16[256,256]{1,0:T(8,128)(2,1)S(1)}, f32[2,256,1024]{2,1,0:T(8,128)}) custom-call(s32[2]{0:T(128)S(1)} %pad_add_fusion.where_ref, s32[2]{0:T(128)S(1)} %copy-done.25, s32[2,512]{1,0:T(2,128)S(1)} %copy-done.21, s32[2,512]{1,0:T(2,128)S(1)} %copy-done.22, ...), custom_call_target="tpu_custom_call" | custom-call | flops 3000000000 | bytes 6000000 | tf_op jit(solution)/shard_map/prepare/pallas_call | solution.py:381
  15.8 0.0 collective-permute-done
  15.8 1.7 %copy-done.26 = f32[2,256,1024]{2,1,0:T(8,128)S(1)} copy-done((f32[2,256,1024]{2,1,0:T(8,128)S(1)}, f32[2,256,1024]{2,1,0:T(8,128)}, u32[]{:S(2)}) %copy-start.26) | copy-done | bytes 2097176
  17.5 3.9 %forward.1 = (f32[2,256,1024]{2,1,0:T(8,128)S(1)}, bf16[2,256,1024]{2,1,0:T(8,128)(2,1)S(1)}, s16[2,112,256]{2,1,0:T(8,128)(2,1)S(1)}) custom-call(bf16[256,1024]{1,0:T(8,128)(2,1)} %bitcast.2.odd_ref.olat_ref, bf16[1024,1024]{1,0:T(8,128)(2,1)S(1)} %copy-done, bf16[256,256]{1,0:T(8,128)(2,1)S(1)} %get-tuple-element.21.cfo_ref, ...), custom_call_target="tpu_custom_call" | custom-call | flops 2000000000 | bytes 8000000 | tf_op jit(solution)/shard_map/forward/pallas_call | solution.py:381
  21.4 0.2 collective-permute-start.2
  21.7 3.3 %collective-permute-start.3 = (s16[2,112,256]{2,1,0:T(8,128)(2,1)S(1)}, s16[2,112,256]{2,1,0:T(8,128)(2,1)S(1)}, u32[]{:S(2)}, u32[]{:S(2)}) collective-permute-start(s16[2,112,256]{2,1,0:T(8,128)(2,1)S(1)} %get-tuple-element.23.c0_ref), channel_id=1, source_target_pairs={{0,128},{64,192},{128,0},{192,64},{1,129},{65,193},{129,1},{193,65... | collective-permute-start | bytes 344072 | tf_op jit(solution)/shard_map/ppermute | solution.py:578
  25.0 0.9 collective-permute-start.4
  25.9 4.0 %factors.1 = (bf16[1024,512]{1,0:T(8,128)(2,1)S(1)}, bf16[1024,512]{1,0:T(8,128)(2,1)S(1)}, f32[2,256,1024]{2,1,0:T(8,128)S(1)}) custom-call(s32[2]{0:T(128)S(1)} %pad_add_fusion.where_ref, bf16[2,128,1024]{2,1,0:T(8,128)(2,1)S(1)} %copy-done.18, bf16[2,128,1024]{2,1,0:T(8,128)(2,1)S(1)} %copy-done.20, bf16[256,1024]{1,0:T(8,128)(2,1)} %bitcast.2.odd_ref.olat_ref, ...), custom_call_target="tpu_custom_call" | custom-call | flops 3000000000 | bytes 10000000 | tf_op jit(solution)/shard_map/factors/pallas_call | solution.py:381
  29.9 0.0 collective-permute-done.2.c1_ref
  29.9 3.7 %collective-permute-done.3.c2_ref = s16[2,112,256]{2,1,0:T(8,128)(2,1)S(1)} collective-permute-done((s16[2,112,256]{2,1,0:T(8,128)(2,1)S(1)}, s16[2,112,256]{2,1,0:T(8,128)(2,1)S(1)}, u32[]{:S(2)}, u32[]{:S(2)}) %collective-permute-start.3) | collective-permute-done | bytes 114720 | tf_op jit(solution)/shard_map/ppermute | solution.py:578
  33.6 0.0 collective-permute-done.4.c3_ref
  33.6 3.3 %backward.1 = (bf16[512,1152]{1,0:T(8,128)(2,1)S(1)}, bf16[512,1152]{1,0:T(8,128)(2,1)S(1)}, bf16[512,1024]{1,0:T(8,128)(2,1)S(1)}) custom-call(s32[2]{0:T(128)S(1)} %pad_add_fusion.where_ref, s16[2,112,256]{2,1,0:T(8,128)(2,1)S(1)} %get-tuple-element.23.c0_ref, s16[2,112,256]{2,1,0:T(8,128)(2,1)S(1)} %collective-permute-done.2.c1_ref, ...), custom_call_target="tpu_custom_call" | custom-call | flops 2000000000 | bytes 5000000 | tf_op jit(solution)/shard_map/backward/pallas_call | solution.py:381
  37.0 0.4 collective-permute-start.7
  37.4 2.5 %collective-permute-done.7.theirs_ref = bf16[512,1152]{1,0:T(8,128)(2,1)S(1)} collective-permute-done((bf16[512,1152]{1,0:T(8,128)(2,1)S(1)}, bf16[512,1152]{1,0:T(8,128)(2,1)S(1)}, u32[]{:S(2)}, u32[]{:S(2)}) %collective-permute-start.7) | collective-permute-done | bytes 1179680 | tf_op jit(solution)/shard_map/ppermute | solution.py:586
  39.9 1.1 %merge.1 = bf16[512,1152]{1,0:T(8,128)(2,1)} custom-call(bf16[512,1152]{1,0:T(8,128)(2,1)S(1)} %get-tuple-element.34.mine_ref, bf16[512,1152]{1,0:T(8,128)(2,1)S(1)} %collective-permute-done.7.theirs_ref), custom_call_target="tpu_custom_call" | custom-call | flops 1000000 | bytes 4000000 | tf_op jit(solution)/shard_map/merge/pallas_call | solution.py:381
  41.1 12.2 %all-to-all-start = ((bf16[16,32,1152]{2,1,0:T(8,128)(2,1)}), bf16[16,32,1152]{2,1,0:T(8,128)(2,1)S(1)}, u32[]{:S(2)}, u32[]{:S(2)}) async-start(bf16[16,32,1152]{2,1,0:T(8,128)(2,1)} %bitcast.6), calls=%async_computation | async-start | bytes 2359296 | tf_op jit(solution)/shard_map/all_to_all | solution.py:590
  53.3 1.2 %copy-done.3 = bf16[512,1024]{1,0:T(8,128)(2,1)S(1)} copy-done((bf16[512,1024]{1,0:T(8,128)(2,1)S(1)}, bf16[512,1024]{1,0:T(8,128)(2,1)}, u32[]{:S(2)}) %copy-start.3) | copy-done | bytes 1048600
  54.5 1.0 %copy-done.6 = bf16[384,512]{1,0:T(8,128)(2,1)S(1)} copy-done((bf16[384,512]{1,0:T(8,128)(2,1)S(1)}, bf16[384,512]{1,0:T(8,128)(2,1)}, u32[]{:S(2)}) %copy-start.6) | copy-done | bytes 393240
  55.5 1.5 %rows.1 = (bf16[2,128,1024]{2,1,0:T(8,128)(2,1)}, bf16[2,128,1024]{2,1,0:T(8,128)(2,1)}) custom-call(bf16[384,512]{1,0:T(8,128)(2,1)S(1)} %copy-done.6, bf16[512,1024]{1,0:T(8,128)(2,1)S(1)} %copy-done.3), custom_call_target="tpu_custom_call" | custom-call | flops 1000000000 | bytes 3000000 | tf_op jit(solution)/shard_map/rows/pallas_call | solution.py:381
  57.1 0.1 collective-permute-start.5
  57.2 0.3 collective-permute-start.6
  57.5 19.2 %all-to-all-done.got_ref = bf16[16,32,1152]{2,1,0:T(8,128)(2,1)S(1)} async-done(((bf16[16,32,1152]{2,1,0:T(8,128)(2,1)}), bf16[16,32,1152]{2,1,0:T(8,128)(2,1)S(1)}, u32[]{:S(2)}, u32[]{:S(2)}) %all-to-all-start) | async-done | bytes 1179680 | tf_op jit(solution)/shard_map/all_to_all | solution.py:590
  76.7 0.6 plane.1
  77.4 0.7 copy-done.1
  78.1 8.7 %all-to-all-start.1 = ((bf16[8,16,1152]{2,1,0:T(8,128)(2,1)}), bf16[8,16,1152]{2,1,0:T(8,128)(2,1)S(1)}, u32[]{:S(2)}, u32[]{:S(2)}) async-start(bf16[8,16,1152]{2,1,0:T(8,128)(2,1)} %bitcast.9), calls=%async_computation.1 | async-start | bytes 589824 | tf_op jit(solution)/shard_map/all_to_all | solution.py:594
  86.8 0.9 copy-done.9
  87.7 0.9 copy-done.11
  88.6 0.9 copy-done.13
  89.5 0.9 copy-done.15
  90.4 0.7 copy-done.17
  91.1 2.5 %score.1 = f32[100,256]{1,0:T(8,128)} custom-call(s32[2]{0:T(128)S(1)} %copy-done.17, s16[2,112,256]{2,1,0:T(8,128)(2,1)S(1)} %get-tuple-element.23.c0_ref, s16[2,112,256]{2,1,0:T(8,128)(2,1)S(1)} %copy-done.9, s16[2,112,256]{2,1,0:T(8,128)(2,1)S(1)} %copy-done.11, s16[2,112,256]{2,1,0:T(8,128)(2,1)S(1)} %copy-done.13, f32[100,256]{1,0:T(8,128)S(1)} %copy-done.15), custom_call_target="tpu_custom_call" | custom-call | flops 10000000 | bytes 1000000 | tf_op jit(solution)/shard_map/score/pallas_call | solution.py:381
  93.5 0.0 collective-permute-done.5.core_ref
  93.5 0.0 collective-permute-done.6.odd_ref
  93.6 1.0 %copy-done.7 = bf16[384,512]{1,0:T(8,128)(2,1)S(1)} copy-done((bf16[384,512]{1,0:T(8,128)(2,1)S(1)}, bf16[384,512]{1,0:T(8,128)(2,1)}, u32[]{:S(2)}) %copy-start.7) | copy-done | bytes 393240
  94.6 3.0 %latent.1 = bf16[2,128,1024]{2,1,0:T(8,128)(2,1)} custom-call(bf16[384,512]{1,0:T(8,128)(2,1)S(1)} %copy-done.7, bf16[512,1024]{1,0:T(8,128)(2,1)S(1)} %copy-done.4, bf16[1024,1024]{1,0:T(8,128)(2,1)S(1)} %copy-done, bf16[2,128,1024]{2,1,0:T(8,128)(2,1)} %collective-permute-done.5.core_ref, bf16[2,128,1024]{2,1,0:T(8,128)(2,1)} %collective-permute-done.6.odd_ref), custom_call_target="tpu_custom_call" | custom-call | flops 1000000000 | bytes 5000000 | tf_op jit(solution)/shard_map/latent/pallas_call | solution.py:381
  97.6 0.1 all-to-all-done.1.got_ref
  97.7 0.7 final.1
  (39 shorter events, 0.1 us)
Async XLA Ops:
  0.6 4.1 %collective-permute-start.1 = (bf16[2,128,1024]{2,1,0:T(8,128)(2,1)}, bf16[2,128,1024]{2,1,0:T(8,128)(2,1)S(1)}, u32[]{:S(2)}, u32[]{:S(2)}) collective-permute-start(bf16[2,128,1024]{2,1,0:T(8,128)(2,1)} %lat_ref.1), channel_id=1, source_target_pairs={{0,1},{1,0},{2,3},{3,2},{4,5},{5,4},{6,7},{7,6},{8,9},{9,8},{10,11... | collective-permute-start | bytes 1572872 | tf_op jit(solution)/shard_map/ppermute | solution.py:569
  0.7 15.1 %collective-permute-start = (bf16[2,128,1024]{2,1,0:T(8,128)(2,1)}, bf16[2,128,1024]{2,1,0:T(8,128)(2,1)}, u32[]{:S(2)}, u32[]{:S(2)}) collective-permute-start(bf16[2,128,1024]{2,1,0:T(8,128)(2,1)} %lat_ref.1), channel_id=1, source_target_pairs={{0,63},{1,2},{2,1},{3,4},{4,3},{5,6},{6,5},{7,8},{8,7},{9,10},{10,... | collective-permute-start | bytes 1572872 | tf_op jit(solution)/shard_map/ppermute | solution.py:568
  4.7 28.9 %copy-start.16 = (s32[2]{0:T(128)}, s32[2]{0:T(128)S(1)}, u32[]{:S(2)}) copy-start(s32[2]{0:T(128)S(1)} %pad_add_fusion.where_ref) | copy-start | bytes 28
  4.7 11.1 %copy-start = (bf16[1024,1024]{1,0:T(8,128)(2,1)S(1)}, bf16[1024,1024]{1,0:T(8,128)(2,1)}, u32[]{:S(2)}) copy-start(bf16[1024,1024]{1,0:T(8,128)(2,1)} %w_ref.3) | copy-start | bytes 6291460
  4.7 0.8 copy-start.19
  5.5 0.7 copy-start.21
  6.2 0.7 copy-start.22
  6.9 0.7 copy-start.23
  7.6 0.7 copy-start.25
  15.8 5.7 %copy-start.5 = (bf16[384,512]{1,0:T(8,128)(2,1)}, bf16[384,512]{1,0:T(8,128)(2,1)S(1)}, u32[]{:S(2)}) copy-start(bf16[384,512]{1,0:T(8,128)(2,1)S(1)} %get-tuple-element.24.cft_ref) | copy-start | bytes 1179652
  15.8 1.7 %copy-start.26 = (f32[2,256,1024]{2,1,0:T(8,128)S(1)}, f32[2,256,1024]{2,1,0:T(8,128)}, u32[]{:S(2)}) copy-start(f32[2,256,1024]{2,1,0:T(8,128)} %get-tuple-element.22.part_ref) | copy-start | bytes 6291460
  17.5 8.4 %copy-start.18 = (bf16[2,128,1024]{2,1,0:T(8,128)(2,1)S(1)}, bf16[2,128,1024]{2,1,0:T(8,128)(2,1)}, u32[]{:S(2)}) copy-start(bf16[2,128,1024]{2,1,0:T(8,128)(2,1)} %lat_ref.1) | copy-start | bytes 1572868
  17.5 8.4 %copy-start.20 = (bf16[2,128,1024]{2,1,0:T(8,128)(2,1)S(1)}, bf16[2,128,1024]{2,1,0:T(8,128)(2,1)}, u32[]{:S(2)}) copy-start(bf16[2,128,1024]{2,1,0:T(8,128)(2,1)} %copy-done.19) | copy-start | bytes 1572868
  21.4 8.5 %collective-permute-start.2 = (s16[2,112,256]{2,1,0:T(8,128)(2,1)S(1)}, s16[2,112,256]{2,1,0:T(8,128)(2,1)S(1)}, u32[]{:S(2)}, u32[]{:S(2)}) collective-permute-start(s16[2,112,256]{2,1,0:T(8,128)(2,1)S(1)} %get-tuple-element.23.c0_ref), channel_id=1, source_target_pairs={{0,64},{64,0},{128,192},{192,128},{1,65},{65,1},{129,193},{193,129... | collective-permute-start | bytes 344072 | tf_op jit(solution)/shard_map/ppermute | solution.py:578
  21.7 11.9 %collective-permute-start.3 = (s16[2,112,256]{2,1,0:T(8,128)(2,1)S(1)}, s16[2,112,256]{2,1,0:T(8,128)(2,1)S(1)}, u32[]{:S(2)}, u32[]{:S(2)}) collective-permute-start(s16[2,112,256]{2,1,0:T(8,128)(2,1)S(1)} %get-tuple-element.23.c0_ref), channel_id=1, source_target_pairs={{0,128},{64,192},{128,0},{192,64},{1,129},{65,193},{129,1},{193,65... | collective-permute-start | bytes 344072 | tf_op jit(solution)/shard_map/ppermute | solution.py:578
  25.0 8.7 %collective-permute-start.4 = (s16[2,112,256]{2,1,0:T(8,128)(2,1)S(1)}, s16[2,112,256]{2,1,0:T(8,128)(2,1)S(1)}, u32[]{:S(2)}, u32[]{:S(2)}) collective-permute-start(s16[2,112,256]{2,1,0:T(8,128)(2,1)S(1)} %get-tuple-element.23.c0_ref), channel_id=1, source_target_pairs={{0,192},{64,128},{128,64},{192,0},{1,193},{65,129},{129,65},{193,1... | collective-permute-start | bytes 344072 | tf_op jit(solution)/shard_map/ppermute | solution.py:578
  25.9 7.7 %copy-start.14 = (f32[100,256]{1,0:T(8,128)S(1)}, f32[100,256]{1,0:T(8,128)}, u32[]{:S(2)}) copy-start(f32[100,256]{1,0:T(8,128)} %truth_ref.3) | copy-start | bytes 307204
  25.9 7.7 %copy-start.24 = (f32[256]{0:T(256)S(1)}, f32[256]{0:T(256)}, u32[]{:S(2)}) copy-start(f32[256]{0:T(256)} %param.14) | copy-start | bytes 3076
  29.9 7.0 %copy-start.8 = (s16[2,112,256]{2,1,0:T(8,128)(2,1)}, s16[2,112,256]{2,1,0:T(8,128)(2,1)S(1)}, u32[]{:S(2)}) copy-start(s16[2,112,256]{2,1,0:T(8,128)(2,1)S(1)} %collective-permute-done.2.c1_ref) | copy-start | bytes 344068
  33.6 3.3 %copy-start.10 = (s16[2,112,256]{2,1,0:T(8,128)(2,1)}, s16[2,112,256]{2,1,0:T(8,128)(2,1)S(1)}, u32[]{:S(2)}) copy-start(s16[2,112,256]{2,1,0:T(8,128)(2,1)S(1)} %collective-permute-done.3.c2_ref) | copy-start | bytes 344068
  33.6 3.3 %copy-start.12 = (s16[2,112,256]{2,1,0:T(8,128)(2,1)}, s16[2,112,256]{2,1,0:T(8,128)(2,1)S(1)}, u32[]{:S(2)}) copy-start(s16[2,112,256]{2,1,0:T(8,128)(2,1)S(1)} %collective-permute-done.4.c3_ref) | copy-start | bytes 344068
  37.0 4.1 %copy-start.2 = (bf16[512,1024]{1,0:T(8,128)(2,1)}, bf16[512,1024]{1,0:T(8,128)(2,1)S(1)}, u32[]{:S(2)}) copy-start(bf16[512,1024]{1,0:T(8,128)(2,1)S(1)} %get-tuple-element.31.sg_ref) | copy-start | bytes 3145732
  37.0 2.9 %collective-permute-start.7 = (bf16[512,1152]{1,0:T(8,128)(2,1)S(1)}, bf16[512,1152]{1,0:T(8,128)(2,1)S(1)}, u32[]{:S(2)}, u32[]{:S(2)}) collective-permute-start(bf16[512,1152]{1,0:T(8,128)(2,1)S(1)} %get-tuple-element.35), channel_id=1, source_target_pairs={{0,1},{1,0},{2,3},{3,2},{4,5},{5,4},{6,7},{7,6},{8,9},{9,8},{10,11... | collective-permute-start | bytes 3538952 | tf_op jit(solution)/shard_map/ppermute | solution.py:586
  41.1 35.6 %all-to-all-start = ((bf16[16,32,1152]{2,1,0:T(8,128)(2,1)}), bf16[16,32,1152]{2,1,0:T(8,128)(2,1)S(1)}, u32[]{:S(2)}, u32[]{:S(2)}) async-start(bf16[16,32,1152]{2,1,0:T(8,128)(2,1)} %bitcast.6), calls=%async_computation | async-start | bytes 2359296 | tf_op jit(solution)/shard_map/all_to_all | solution.py:590
  53.3 1.2 %copy-start.3 = (bf16[512,1024]{1,0:T(8,128)(2,1)S(1)}, bf16[512,1024]{1,0:T(8,128)(2,1)}, u32[]{:S(2)}) copy-start(bf16[512,1024]{1,0:T(8,128)(2,1)} %copy-done.2) | copy-start | bytes 3145732
  54.5 1.0 %copy-start.6 = (bf16[384,512]{1,0:T(8,128)(2,1)S(1)}, bf16[384,512]{1,0:T(8,128)(2,1)}, u32[]{:S(2)}) copy-start(bf16[384,512]{1,0:T(8,128)(2,1)} %copy-done.5) | copy-start | bytes 1179652
  57.1 36.5 %collective-permute-start.5 = (bf16[2,128,1024]{2,1,0:T(8,128)(2,1)}, bf16[2,128,1024]{2,1,0:T(8,128)(2,1)}, u32[]{:S(2)}, u32[]{:S(2)}) collective-permute-start(bf16[2,128,1024]{2,1,0:T(8,128)(2,1)} %get-tuple-element.32), channel_id=1, source_target_pairs={{0,1},{1,0},{2,3},{3,2},{4,5},{5,4},{6,7},{7,6},{8,9},{9,8},{10,11... | collective-permute-start | bytes 1572872 | tf_op jit(solution)/shard_map/ppermute | solution.py:592
  57.2 36.4 %collective-permute-start.6 = (bf16[2,128,1024]{2,1,0:T(8,128)(2,1)}, bf16[2,128,1024]{2,1,0:T(8,128)(2,1)}, u32[]{:S(2)}, u32[]{:S(2)}) collective-permute-start(bf16[2,128,1024]{2,1,0:T(8,128)(2,1)} %get-tuple-element.33), channel_id=1, source_target_pairs={{0,63},{1,2},{2,1},{3,4},{4,3},{5,6},{6,5},{7,8},{8,7},{9,10},{10,... | collective-permute-start | bytes 1572872 | tf_op jit(solution)/shard_map/ppermute | solution.py:591
  77.4 0.7 copy-start.1
  78.1 15.5 %copy-start.4 = (bf16[512,1024]{1,0:T(8,128)(2,1)S(1)}, bf16[512,1024]{1,0:T(8,128)(2,1)}, u32[]{:S(2)}) copy-start(bf16[512,1024]{1,0:T(8,128)(2,1)} %copy-done.2) | copy-start | bytes 3145732
  78.1 19.6 %all-to-all-start.1 = ((bf16[8,16,1152]{2,1,0:T(8,128)(2,1)}), bf16[8,16,1152]{2,1,0:T(8,128)(2,1)S(1)}, u32[]{:S(2)}, u32[]{:S(2)}) async-start(bf16[8,16,1152]{2,1,0:T(8,128)(2,1)} %bitcast.9), calls=%async_computation.1 | async-start | bytes 589824 | tf_op jit(solution)/shard_map/all_to_all | solution.py:594
  86.8 0.9 copy-start.9
  87.7 0.9 copy-start.11
  88.6 0.9 copy-start.13
  89.5 0.9 copy-start.15
  90.4 0.7 copy-start.17
  93.6 1.0 %copy-start.7 = (bf16[384,512]{1,0:T(8,128)(2,1)S(1)}, bf16[384,512]{1,0:T(8,128)(2,1)}, u32[]{:S(2)}) copy-start(bf16[384,512]{1,0:T(8,128)(2,1)} %copy-done.5) | copy-start | bytes 1179652

commit v5 on v4

--- a/solution.py
+++ b/solution.py
@@ -21,7 +21,8 @@
 GELU_C = math.sqrt(2.0 / math.pi)
 MIB = 1 << 20
 LIMIT = 24
-PREP = 53
+PREP = 50
+LARGE = 56
 F32 = jnp.float32
 BF16 = jnp.bfloat16
 
@@ -231,10 +232,18 @@
             f_ref[first + m] = code * power[:VUSE, at : at + 1]
 
 
-def score_kernel(where_ref, c0_ref, c1_ref, c2_ref, c3_ref, truth_ref, score_ref, f_ref):
+def score_kernel(
+    where_ref, c0_any, c1_any, c2_any, c3_any, truth_hbm, score_ref,
+    c_ref, truth_ref, f_ref, in_sem,
+):
     members = f_ref.shape[0]
     nvar = truth_ref.shape[0]
-    decode(where_ref, (c0_ref, c1_ref, c2_ref, c3_ref), f_ref)
+    codes = [c_ref.at[k] for k in range(4)]
+    pairs = list(zip((c0_any, c1_any, c2_any, c3_any), codes)) + [(truth_hbm, truth_ref)]
+    copies = [start_copy(src, dst, in_sem.at[k]) for k, (src, dst) in enumerate(pairs)]
+    for copy in copies:
+        copy.wait()
+    decode(where_ref, codes, f_ref)
     collected = [f_ref[m][:nvar] for m in range(members)]
     truth = truth_ref[...]
     skill = sum(smooth_abs(f - truth) for f in collected)
@@ -280,7 +289,7 @@
         theirs_ref[:, at] = part[half:]
 
 
-def merge_kernel(mine_ref, theirs_ref, out_hbm, out_ref, out_sem):
+def merge_kernel(mine_ref, theirs_ref, after_any, out_hbm, out_ref, out_sem):
     rows = mine_ref.shape[0] // 4
     outs = []
     for k in range(4):
@@ -337,20 +346,30 @@
 
 
 def latent_kernel(
-    cft_ref, sg_ref, w_ref, core_ref, odd_ref, out_hbm, g_ref, out_ref, out_sem
+    cft_hbm, sg_hbm, w_hbm, core_any, far_any, near_any, out_hbm,
+    cft_ref, sg_ref, w_ref, core_ref, far_ref, near_ref, g_ref, out_ref, in_sem, out_sem,
 ):
     local, rows, depth = core_ref.shape
     points = cft_ref.shape[1] // 2
     steps = depth // TILE
-    high = cft_ref[:HALO, :points]
-    low = cft_ref[:HALO, points:]
+    pairs = (
+        (cft_hbm.at[pl.ds(0, HALO)], cft_ref), (sg_hbm, sg_ref), (core_any, core_ref),
+        (far_any, far_ref), (near_any, near_ref), (w_hbm, w_ref),
+    )
+    copies = [start_copy(src, dst, in_sem.at[k]) for k, (src, dst) in enumerate(pairs)]
+    for copy in copies[:5]:
+        copy.wait()
+    high = cft_ref[:, :points]
+    low = cft_ref[:, points:]
     for m in range(local):
         for j in range(steps):
             at = slice(j * TILE, (j + 1) * TILE)
             s = sg_ref[m * points : (m + 1) * points, at]
             g = dot(high, s) + dot(low, s)
-            g = g + core_ref[m, :, at].astype(F32) + odd_ref[m, :, at].astype(F32)
+            for ref in (core_ref, far_ref, near_ref):
+                g = g + ref[m, :, at].astype(F32)
             g_ref[m * HALO : (m + 1) * HALO, at] = g.astype(BF16)
+    copies[5].wait()
     outs = []
     for j in range(steps):
         at = slice(j * TILE, (j + 1) * TILE)
@@ -464,16 +483,16 @@
     )
 
 
-def call_merge(mine, theirs):
+def call_merge(mine, theirs, after):
     return call(
         merge_kernel,
         "merge",
         shape(mine.shape, BF16),
-        vmem(2),
+        vmem(2) + anywhere(1),
         hbm(1)[0],
         scratch(mine) + [sems(4)],
         (10**6, 4 * 10**6),
-        (mine, theirs),
+        (mine, theirs, after),
     )
 
 
@@ -511,27 +530,33 @@
         score_kernel,
         "score",
         shape(truth.shape, F32),
-        smem(1) + vmem(len(codes) + 1),
+        smem(1) + anywhere(len(codes)) + hbm(1),
         vmem(1)[0],
-        [pltpu.VMEM((local * len(codes), VUSE, points), F32)],
+        [pltpu.VMEM((len(codes),) + codes[0].shape, jnp.int16)]
+        + scratch(truth)
+        + [pltpu.VMEM((local * len(codes), VUSE, points), F32), sems(len(codes) + 1)],
         (10**7, 10**6),
         (where, *codes, truth),
-    )
-
-
-def call_latent(cft, summed_grad, weight, core_grad, odd_grad):
+        LARGE,
+    )
+
+
+def call_latent(cft, summed_grad, weight, core_grad, far_grad, near_grad):
     local, rows, depth = core_grad.shape
     return call(
         latent_kernel,
         "latent",
         shape(core_grad.shape, BF16),
-        vmem(5),
+        hbm(3) + anywhere(3),
         hbm(1)[0],
-        [pltpu.VMEM((local * rows, depth), BF16)]
+        [pltpu.VMEM((HALO, cft.shape[1]), BF16)]
+        + scratch(summed_grad, weight, core_grad, far_grad, near_grad)
+        + [pltpu.VMEM((local * rows, depth), BF16)]
         + scratch(core_grad)
-        + [sems(depth // TILE)],
+        + [sems(6), sems(depth // TILE)],
         (10**9, 5 * 10**6),
-        (cft, summed_grad, weight, core_grad, odd_grad),
+        (cft, summed_grad, weight, core_grad, far_grad, near_grad),
+        LARGE,
     )
 
 
@@ -551,6 +576,8 @@
 
 def make_body(count):
     odd_pairs = [(i, (i + 1) % count if i % 2 else (i - 1) % count) for i in range(count)]
+    far = [p for p in odd_pairs if abs(p[0] - p[1]) > 1 or p[0] // 32 != p[1] // 32]
+    near = [p for p in odd_pairs if p not in far]
     swap = [(0, 1), (1, 0)]
 
     def body(
@@ -584,16 +611,18 @@
             where, codes, truth, var_row, area_row, dpt, aggt, hidt, slope
         )
         theirs = lax.ppermute(theirs, "core", swap)
-        part = call_merge(mine, theirs)
         core_send, odd_send = call_rows(cft, summed_grad, local)
+        near_grad = lax.ppermute(odd_send, SPACE, near)
+        part = call_merge(mine, theirs, odd_send)
+        part, odd_send, core_send = lax.optimization_barrier((part, odd_send, core_send))
         part = part.reshape(16, 2 * per, part.shape[1])
         got = lax.all_to_all(part, ("x", "y"), 0, 0, tiled=True)
-        odd_grad = lax.ppermute(odd_send, SPACE, odd_pairs)
+        far_grad = lax.ppermute(odd_send, SPACE, far)
         core_grad = lax.ppermute(core_send, "core", swap)
         plane = call_plane(got, ens).reshape(2 * ens, per, got.shape[2])
         got = lax.all_to_all(plane, ("zhi", "ens"), 0, 0, tiled=True)
         score = call_score(where, codes, truth)
-        grad_latent = call_latent(cft, summed_grad, src_weight, core_grad, odd_grad)
+        grad_latent = call_latent(cft, summed_grad, src_weight, core_grad, far_grad, near_grad)
         scaling = 1.0 / math.sqrt(members * points * count)
         grad_src, grad_out = call_final(got, nvar, scaling)
         return score, grad_latent, grad_src, grad_out

time: 99.1 us -> 96 us (0.969)
  local copies, waits for them, and re-layouts: 15.1 us -> 6.51 us
  starting transfers between devices: 28.6 us -> 35 us
  Pallas kernels: 28.2 us -> 26.9 us
    unnamed x54 -> x34, local copies, waits for them, and re-layouts: 13.5 us -> 4.9 us
    ppermute x1 -> x2, starting transfers between devices: 0.32 us -> 3.37 us  [the longest x1 1.91 us: body(): near_grad = lax.ppermute(odd_send, SPACE, near)]
    all_to_all x1, starting transfers between devices: 12.2 us -> 15 us  [body(): got = lax.all_to_all(part, ('x', 'y'), 0, 0, tiled=True)]
    all_to_all x1, waiting for transfers between devices: 0.07 us -> 2.03 us  [body(): got = lax.all_to_all(plane, ('zhi', 'ens'), 0, 0, tiled=True)]
    ppermute x1, starting transfers between devices: 0.09 us -> 1.66 us  [body(): core_grad = lax.ppermute(core_send, 'core', swap)]
    pallas_call x10, Pallas kernels: 28.2 us -> 26.9 us  [call(): pl.pallas_call(kernel, out_shape=out_shape, in_specs=in_specs, out_specs=...]
    ppermute x1, waiting for transfers between devices: 2.52 us -> 1.48 us  [body(): theirs = lax.ppermute(theirs, 'core', swap)]
    all_to_all x1, starting transfers between devices: 8.72 us -> 7.69 us  [body(): got = lax.all_to_all(plane, ('zhi', 'ens'), 0, 0, tiled=True)]
  transfers between devices with their start and end apart: 10 -> 11, of which waited for: 4 -> 4; matrix products, arithmetic and copies ran while one was open for 2% -> 2% of each run, Pallas kernels for 20% -> 20%
where the time goes in v5:
time: 96 us; the launch traced here: 95.5 us
  starting transfers between devices  35 us (36%)
  Pallas kernels  26.9 us (28%)
  waiting for transfers between devices  26.1 us (27%)
  local copies, waits for them, and re-layouts  6.51 us (7%)
    pallas_call x10, Pallas kernels, call(): pl.pallas_call(kernel, out_shape=out_shape, in_specs=in_specs, out_specs=...  26.9 us
    all_to_all x1, waiting for transfers between devices, body(): got = lax.all_to_all(part, ('x', 'y'), 0, 0, tiled=True)  18.4 us
    all_to_all x1, starting transfers between devices, body(): got = lax.all_to_all(part, ('x', 'y'), 0, 0, tiled=True)  15 us
    all_to_all x1, starting transfers between devices, body(): got = lax.all_to_all(plane, ('zhi', 'ens'), 0, 0, tiled=True)  7.69 us
    unnamed x34, local copies, waits for them, and re-layouts  4.9 us
    ppermute x3, starting transfers between devices, body(): lax.ppermute(coded, 'ens', [(e, e ^ k) for e in range(ens)])  4.45 us
    ppermute x3, waiting for transfers between devices, body(): lax.ppermute(coded, 'ens', [(e, e ^ k) for e in range(ens)])  4.23 us
    ppermute x1, starting transfers between devices, body(): lax.ppermute(latent, SPACE, odd_pairs).reshape(local * rows, depth)  2.28 us
  transfers between devices with their start and end apart: 11, of which 4 were waited for; matrix products, arithmetic and copies ran while one was open for 2% of the time, Pallas kernels for 20%

profile of v5, /device:TPU:8, one launch (start us, length us, event | category | flops | bytes accessed | tf_op | source)
XLA Modules:
  0.0 95.5 jit_solution(14877343802296503004)
XLA Ops:
  0.6 0.1 collective-permute-start.1
  0.7 2.3 %collective-permute-start = (bf16[2,128,1024]{2,1,0:T(8,128)(2,1)}, bf16[2,128,1024]{2,1,0:T(8,128)(2,1)S(1)}, u32[]{:S(2)}, u32[]{:S(2)}) collective-permute-start(bf16[2,128,1024]{2,1,0:T(8,128)(2,1)} %lat_ref.1), channel_id=1, source_target_pairs={{0,63},{1,2},{2,1},{3,4},{4,3},{5,6},{6,5},{7,8},{8,7},{9,10},{10,... | collective-permute-start | bytes 1572872 | tf_op jit(solution)/shard_map/ppermute | solution.py:595
  3.0 1.0 pad.8.dpt_ref
  4.0 0.7 pad_bitcast_fusion.var_ref
  4.6 0.1 pad_add_fusion.where_ref
  4.7 0.0 collective-permute-done.1.clat_hbm.clat_ref
  4.7 1.2 %copy-done.9 = bf16[2,128,1024]{2,1,0:T(8,128)(2,1)S(1)} copy-done((bf16[2,128,1024]{2,1,0:T(8,128)(2,1)S(1)}, bf16[2,128,1024]{2,1,0:T(8,128)(2,1)}, u32[]{:S(2)}) %copy-start.9) | copy-done | bytes 524312
  5.9 0.7 copy-done.10
  6.6 0.7 copy-done.11
  7.3 0.7 copy-done.12
  8.0 0.7 copy-done.14
  8.6 5.9 %prepare.1 = (bf16[256,768]{1,0:T(8,128)(2,1)S(1)}, bf16[384,512]{1,0:T(8,128)(2,1)S(1)}, bf16[256,256]{1,0:T(8,128)(2,1)S(1)}, f32[2,256,1024]{2,1,0:T(8,128)S(1)}) custom-call(s32[2]{0:T(128)S(1)} %pad_add_fusion.where_ref, s32[2]{0:T(128)S(1)} %copy-done.14, s32[2,512]{1,0:T(2,128)S(1)} %copy-done.10, s32[2,512]{1,0:T(2,128)S(1)} %copy-done.11, ...), custom_call_target="tpu_custom_call" | custom-call | flops 3000000000 | bytes 6000000 | tf_op jit(solution)/shard_map/prepare/pallas_call | solution.py:400
  14.5 0.0 copy-start.2
  14.5 0.0 collective-permute-done
  14.6 0.0 copy-done
  14.6 2.8 %forward.1 = (f32[2,256,1024]{2,1,0:T(8,128)S(1)}, bf16[2,256,1024]{2,1,0:T(8,128)(2,1)S(1)}, s16[2,112,256]{2,1,0:T(8,128)(2,1)S(1)}) custom-call(bf16[256,1024]{1,0:T(8,128)(2,1)S(1)} %bitcast.9, bf16[1024,1024]{1,0:T(8,128)(2,1)S(1)} %copy-done, bf16[256,256]{1,0:T(8,128)(2,1)S(1)} %get-tuple-element.24.cfo_ref, ...), custom_call_target="tpu_custom_call" | custom-call | flops 2000000000 | bytes 8000000 | tf_op jit(solution)/shard_map/forward/pallas_call | solution.py:400
  17.3 0.2 collective-permute-start.2
  17.6 3.3 %collective-permute-start.3 = (s16[2,112,256]{2,1,0:T(8,128)(2,1)S(1)}, s16[2,112,256]{2,1,0:T(8,128)(2,1)S(1)}, u32[]{:S(2)}, u32[]{:S(2)}) collective-permute-start(s16[2,112,256]{2,1,0:T(8,128)(2,1)S(1)} %get-tuple-element.26.c0_any.c0_ref), channel_id=1, source_target_pairs={{0,128},{64,192},{128,0},{192,64},{1,129},{65,193},{129,1},{193,65... | collective-permute-start | bytes 344072 | tf_op jit(solution)/shard_map/ppermute | solution.py:605
  20.9 0.9 collective-permute-start.4
  21.8 3.5 %factors.1 = (bf16[1024,512]{1,0:T(8,128)(2,1)S(1)}, bf16[1024,512]{1,0:T(8,128)(2,1)S(1)}, f32[2,256,1024]{2,1,0:T(8,128)S(1)}) custom-call(s32[2]{0:T(128)S(1)} %pad_add_fusion.where_ref, bf16[2,128,1024]{2,1,0:T(8,128)(2,1)S(1)} %copy-done.9, bf16[2,128,1024]{2,1,0:T(8,128)(2,1)S(1)} %collective-permute-done.1.clat_hbm.clat_ref, ...), custom_call_target="tpu_custom_call" | custom-call | flops 3000000000 | bytes 10000000 | tf_op jit(solution)/shard_map/factors/pallas_call | solution.py:400
  25.3 0.0 collective-permute-done.2.c1_any.c1_ref
  25.3 0.0 copy-start.4
  25.3 4.2 %collective-permute-done.3.c2_any.c2_ref = s16[2,112,256]{2,1,0:T(8,128)(2,1)S(1)} collective-permute-done((s16[2,112,256]{2,1,0:T(8,128)(2,1)S(1)}, s16[2,112,256]{2,1,0:T(8,128)(2,1)S(1)}, u32[]{:S(2)}, u32[]{:S(2)}) %collective-permute-start.3) | collective-permute-done | bytes 114720 | tf_op jit(solution)/shard_map/ppermute | solution.py:605
  29.5 0.0 collective-permute-done.4.c3_any.c3_ref
  29.5 0.0 copy-done.8
  29.5 0.0 copy-done.3
  29.6 3.3 %backward.1 = (bf16[512,1152]{1,0:T(8,128)(2,1)S(1)}, bf16[512,1152]{1,0:T(8,128)(2,1)S(1)}, bf16[512,1024]{1,0:T(8,128)(2,1)S(1)}) custom-call(s32[2]{0:T(128)S(1)} %pad_add_fusion.where_ref, s16[2,112,256]{2,1,0:T(8,128)(2,1)S(1)} %get-tuple-element.26.c0_any.c0_ref, s16[2,112,256]{2,1,0:T(8,128)(2,1)S(1)} %collective-permute-done.2.c1_any.c1_ref, ...), custom_call_target="tpu_custom_call" | custom-call | flops 2000000000 | bytes 5000000 | tf_op jit(solution)/shard_map/backward/pallas_call | solution.py:400
  32.9 0.4 collective-permute-start.5
  33.3 1.0 %rows.1 = (bf16[2,128,1024]{2,1,0:T(8,128)(2,1)S(1)}, bf16[2,128,1024]{2,1,0:T(8,128)(2,1)S(1)}) custom-call(bf16[384,512]{1,0:T(8,128)(2,1)S(1)} %get-tuple-element.27.cft_ref.cft_hbm, bf16[512,1024]{1,0:T(8,128)(2,1)S(1)} %get-tuple-element.34.sg_ref.sg_hbm), custom_call_target="tpu_custom_call" | custom-call | flops 1000000000 | bytes 3000000 | tf_op jit(solution)/shard_map/rows/pallas_call | solution.py:400
  34.3 1.5 %collective-permute-done.5.theirs_ref = bf16[512,1152]{1,0:T(8,128)(2,1)S(1)} collective-permute-done((bf16[512,1152]{1,0:T(8,128)(2,1)S(1)}, bf16[512,1152]{1,0:T(8,128)(2,1)S(1)}, u32[]{:S(2)}, u32[]{:S(2)}) %collective-permute-start.5) | collective-permute-done | bytes 1179680 | tf_op jit(solution)/shard_map/ppermute | solution.py:613
  35.8 1.1 %merge.1 = bf16[512,1152]{1,0:T(8,128)(2,1)} custom-call(bf16[512,1152]{1,0:T(8,128)(2,1)S(1)} %get-tuple-element.35.mine_ref, bf16[512,1152]{1,0:T(8,128)(2,1)S(1)} %collective-permute-done.5.theirs_ref, bf16[2,128,1024]{2,1,0:T(8,128)(2,1)S(1)} %get-tuple-element.40.after_any), custom_call_target="tpu_custom_call" | custom-call | flops 1000000 | bytes 4000000 | tf_op jit(solution)/shard_map/merge/pallas_call | solution.py:400
  37.0 15.0 %all-to-all-start = ((bf16[16,32,1152]{2,1,0:T(8,128)(2,1)}), bf16[16,32,1152]{2,1,0:T(8,128)(2,1)S(1)}, u32[]{:S(2)}, u32[]{:S(2)}) async-start(bf16[16,32,1152]{2,1,0:T(8,128)(2,1)} %bitcast.6), calls=%async_computation | async-start | bytes 2359296 | tf_op jit(solution)/shard_map/all_to_all | solution.py:619
  51.9 1.9 %collective-permute-start.8 = (bf16[2,128,1024]{2,1,0:T(8,128)(2,1)S(1)}, bf16[2,128,1024]{2,1,0:T(8,128)(2,1)S(1)}, u32[]{:S(2)}, u32[]{:S(2)}) collective-permute-start(bf16[2,128,1024]{2,1,0:T(8,128)(2,1)S(1)} %get-tuple-element.40.after_any), channel_id=1, source_target_pairs={{1,2},{2,1},{3,4},{4,3},{5,6},{6,5},{7,8},{8,7},{9,10},{10,9},{11,... | collective-permute-start | bytes 1572872 | tf_op jit(solution)/shard_map/ppermute | solution.py:615
  53.9 1.7 %collective-permute-start.6 = (bf16[2,128,1024]{2,1,0:T(8,128)(2,1)S(1)}, bf16[2,128,1024]{2,1,0:T(8,128)(2,1)S(1)}, u32[]{:S(2)}, u32[]{:S(2)}) collective-permute-start(bf16[2,128,1024]{2,1,0:T(8,128)(2,1)S(1)} %get-tuple-element.39), channel_id=1, source_target_pairs={{0,1},{1,0},{2,3},{3,2},{4,5},{5,4},{6,7},{7,6},{8,9},{9,8},{10,11... | collective-permute-start | bytes 1572872 | tf_op jit(solution)/shard_map/ppermute | solution.py:621
  55.5 1.5 %collective-permute-start.7 = (bf16[2,128,1024]{2,1,0:T(8,128)(2,1)S(1)}, bf16[2,128,1024]{2,1,0:T(8,128)(2,1)}, u32[]{:S(2)}, u32[]{:S(2)}) collective-permute-start(bf16[2,128,1024]{2,1,0:T(8,128)(2,1)S(1)} %get-tuple-element.40.after_any), channel_id=1, source_target_pairs={{0,63},{31,32},{32,31},{63,0},{64,127},{95,96},{96,95},{127,64},{1... | collective-permute-start | bytes 1572872 | tf_op jit(solution)/shard_map/ppermute | solution.py:620
  57.0 18.4 %all-to-all-done.got_ref = bf16[16,32,1152]{2,1,0:T(8,128)(2,1)S(1)} async-done(((bf16[16,32,1152]{2,1,0:T(8,128)(2,1)}), bf16[16,32,1152]{2,1,0:T(8,128)(2,1)S(1)}, u32[]{:S(2)}, u32[]{:S(2)}) %all-to-all-start) | async-done | bytes 1179680 | tf_op jit(solution)/shard_map/all_to_all | solution.py:619
  75.4 0.9 plane.1
  76.3 7.7 %all-to-all-start.1 = ((bf16[8,16,1152]{2,1,0:T(8,128)(2,1)}), bf16[8,16,1152]{2,1,0:T(8,128)(2,1)S(1)}, u32[]{:S(2)}, u32[]{:S(2)}) async-start(bf16[8,16,1152]{2,1,0:T(8,128)(2,1)} %bitcast.7), calls=%async_computation.1 | async-start | bytes 589824 | tf_op jit(solution)/shard_map/all_to_all | solution.py:623
  83.9 3.8 %score.1 = f32[100,256]{1,0:T(8,128)} custom-call(s32[2]{0:T(128)} %copy-done.8, s16[2,112,256]{2,1,0:T(8,128)(2,1)} %copy-done.3, s16[2,112,256]{2,1,0:T(8,128)(2,1)} %copy-done.4, s16[2,112,256]{2,1,0:T(8,128)(2,1)} %copy-done.5, s16[2,112,256]{2,1,0:T(8,128)(2,1)} %copy-done.6, f32[100,256]{1,0:T(8,128)} %truth_ref.1), custom_call_target="tpu_custom_call" | custom-call | flops 10000000 | bytes 1000000 | tf_op jit(solution)/shard_map/score/pallas_call | solution.py:400
  87.7 0.0 collective-permute-done.8.near_any
  87.7 0.0 collective-permute-done.6.core_any
  87.8 0.0 copy-start.16
  87.8 0.0 collective-permute-done.7.far_any
  87.8 0.8 copy-done.15
  88.5 0.2 copy-done.16
  88.7 4.0 %latent.1 = bf16[2,128,1024]{2,1,0:T(8,128)(2,1)} custom-call(bf16[384,512]{1,0:T(8,128)(2,1)} %copy-done.2, bf16[512,1024]{1,0:T(8,128)(2,1)} %copy-done.1, bf16[1024,1024]{1,0:T(8,128)(2,1)} %w_hbm.3, bf16[2,128,1024]{2,1,0:T(8,128)(2,1)} %copy-done.16, bf16[2,128,1024]{2,1,0:T(8,128)(2,1)} %collective-permute-done.7.far_any, bf16[2,128,1024]{2,1,0:T(8,128)(2,1)} %copy-done.15), custom_call_target="tpu_custom_call" | custom-call | flops 1000000000 | bytes 5000000 | tf_op jit(solution)/shard_map/latent/pallas_call | solution.py:400
  92.7 2.0 %all-to-all-done.1.got_ref = bf16[8,16,1152]{2,1,0:T(8,128)(2,1)S(1)} async-done(((bf16[8,16,1152]{2,1,0:T(8,128)(2,1)}), bf16[8,16,1152]{2,1,0:T(8,128)(2,1)S(1)}, u32[]{:S(2)}, u32[]{:S(2)}) %all-to-all-start.1) | async-done | bytes 294944 | tf_op jit(solution)/shard_map/all_to_all | solution.py:623
  94.8 0.7 final.1
  (21 shorter events, 0.0 us)
Async XLA Ops:
  0.6 4.1 %collective-permute-start.1 = (bf16[2,128,1024]{2,1,0:T(8,128)(2,1)}, bf16[2,128,1024]{2,1,0:T(8,128)(2,1)S(1)}, u32[]{:S(2)}, u32[]{:S(2)}) collective-permute-start(bf16[2,128,1024]{2,1,0:T(8,128)(2,1)} %lat_ref.1), channel_id=1, source_target_pairs={{0,1},{1,0},{2,3},{3,2},{4,5},{5,4},{6,7},{7,6},{8,9},{9,8},{10,11... | collective-permute-start | bytes 1572872 | tf_op jit(solution)/shard_map/ppermute | solution.py:596
  0.7 13.8 %collective-permute-start = (bf16[2,128,1024]{2,1,0:T(8,128)(2,1)}, bf16[2,128,1024]{2,1,0:T(8,128)(2,1)S(1)}, u32[]{:S(2)}, u32[]{:S(2)}) collective-permute-start(bf16[2,128,1024]{2,1,0:T(8,128)(2,1)} %lat_ref.1), channel_id=1, source_target_pairs={{0,63},{1,2},{2,1},{3,4},{4,3},{5,6},{6,5},{7,8},{8,7},{9,10},{10,... | collective-permute-start | bytes 1572872 | tf_op jit(solution)/shard_map/ppermute | solution.py:595
  4.7 24.8 %copy-start.8 = (s32[2]{0:T(128)}, s32[2]{0:T(128)S(1)}, u32[]{:S(2)}) copy-start(s32[2]{0:T(128)S(1)} %pad_add_fusion.where_ref) | copy-start | bytes 28
  4.7 9.8 %copy-start = (bf16[1024,1024]{1,0:T(8,128)(2,1)S(1)}, bf16[1024,1024]{1,0:T(8,128)(2,1)}, u32[]{:S(2)}) copy-start(bf16[1024,1024]{1,0:T(8,128)(2,1)} %w_hbm.3) | copy-start | bytes 6291460
  4.7 1.2 %copy-start.9 = (bf16[2,128,1024]{2,1,0:T(8,128)(2,1)S(1)}, bf16[2,128,1024]{2,1,0:T(8,128)(2,1)}, u32[]{:S(2)}) copy-start(bf16[2,128,1024]{2,1,0:T(8,128)(2,1)} %lat_ref.1) | copy-start | bytes 1572868
  5.9 0.7 copy-start.10
  6.6 0.7 copy-start.11
  7.3 0.7 copy-start.12
  8.0 0.7 copy-start.14
  14.5 18.8 %copy-start.2 = (bf16[384,512]{1,0:T(8,128)(2,1)}, bf16[384,512]{1,0:T(8,128)(2,1)S(1)}, u32[]{:S(2)}) copy-start(bf16[384,512]{1,0:T(8,128)(2,1)S(1)} %get-tuple-element.27.cft_ref.cft_hbm) | copy-start | bytes 1179652
  17.3 12.2 %copy-start.3 = (s16[2,112,256]{2,1,0:T(8,128)(2,1)}, s16[2,112,256]{2,1,0:T(8,128)(2,1)S(1)}, u32[]{:S(2)}) copy-start(s16[2,112,256]{2,1,0:T(8,128)(2,1)S(1)} %get-tuple-element.26.c0_any.c0_ref) | copy-start | bytes 344068
  17.3 7.9 %collective-permute-start.2 = (s16[2,112,256]{2,1,0:T(8,128)(2,1)S(1)}, s16[2,112,256]{2,1,0:T(8,128)(2,1)S(1)}, u32[]{:S(2)}, u32[]{:S(2)}) collective-permute-start(s16[2,112,256]{2,1,0:T(8,128)(2,1)S(1)} %get-tuple-element.26.c0_any.c0_ref), channel_id=1, source_target_pairs={{0,64},{64,0},{128,192},{192,128},{1,65},{65,1},{129,193},{193,129... | collective-permute-start | bytes 344072 | tf_op jit(solution)/shard_map/ppermute | solution.py:605
  17.6 11.9 %collective-permute-start.3 = (s16[2,112,256]{2,1,0:T(8,128)(2,1)S(1)}, s16[2,112,256]{2,1,0:T(8,128)(2,1)S(1)}, u32[]{:S(2)}, u32[]{:S(2)}) collective-permute-start(s16[2,112,256]{2,1,0:T(8,128)(2,1)S(1)} %get-tuple-element.26.c0_any.c0_ref), channel_id=1, source_target_pairs={{0,128},{64,192},{128,0},{192,64},{1,129},{65,193},{129,1},{193,65... | collective-permute-start | bytes 344072 | tf_op jit(solution)/shard_map/ppermute | solution.py:605
  20.9 8.7 %collective-permute-start.4 = (s16[2,112,256]{2,1,0:T(8,128)(2,1)S(1)}, s16[2,112,256]{2,1,0:T(8,128)(2,1)S(1)}, u32[]{:S(2)}, u32[]{:S(2)}) collective-permute-start(s16[2,112,256]{2,1,0:T(8,128)(2,1)S(1)} %get-tuple-element.26.c0_any.c0_ref), channel_id=1, source_target_pairs={{0,192},{64,128},{128,64},{192,0},{1,193},{65,129},{129,65},{193,1... | collective-permute-start | bytes 344072 | tf_op jit(solution)/shard_map/ppermute | solution.py:605
  21.8 7.7 %copy-start.7 = (f32[100,256]{1,0:T(8,128)S(1)}, f32[100,256]{1,0:T(8,128)}, u32[]{:S(2)}) copy-start(f32[100,256]{1,0:T(8,128)} %truth_ref.1) | copy-start | bytes 307204
  21.8 7.7 %copy-start.13 = (f32[256]{0:T(256)S(1)}, f32[256]{0:T(256)}, u32[]{:S(2)}) copy-start(f32[256]{0:T(256)} %param.14) | copy-start | bytes 3076
  25.3 7.6 %copy-start.4 = (s16[2,112,256]{2,1,0:T(8,128)(2,1)}, s16[2,112,256]{2,1,0:T(8,128)(2,1)S(1)}, u32[]{:S(2)}) copy-start(s16[2,112,256]{2,1,0:T(8,128)(2,1)S(1)} %collective-permute-done.2.c1_any.c1_ref) | copy-start | bytes 344068
  29.5 3.4 %copy-start.5 = (s16[2,112,256]{2,1,0:T(8,128)(2,1)}, s16[2,112,256]{2,1,0:T(8,128)(2,1)S(1)}, u32[]{:S(2)}) copy-start(s16[2,112,256]{2,1,0:T(8,128)(2,1)S(1)} %collective-permute-done.3.c2_any.c2_ref) | copy-start | bytes 344068
  29.5 3.4 %copy-start.6 = (s16[2,112,256]{2,1,0:T(8,128)(2,1)}, s16[2,112,256]{2,1,0:T(8,128)(2,1)S(1)}, u32[]{:S(2)}) copy-start(s16[2,112,256]{2,1,0:T(8,128)(2,1)S(1)} %collective-permute-done.4.c3_any.c3_ref) | copy-start | bytes 344068
  32.9 1.5 %copy-start.1 = (bf16[512,1024]{1,0:T(8,128)(2,1)}, bf16[512,1024]{1,0:T(8,128)(2,1)S(1)}, u32[]{:S(2)}) copy-start(bf16[512,1024]{1,0:T(8,128)(2,1)S(1)} %get-tuple-element.34.sg_ref.sg_hbm) | copy-start | bytes 3145732
  32.9 2.9 %collective-permute-start.5 = (bf16[512,1152]{1,0:T(8,128)(2,1)S(1)}, bf16[512,1152]{1,0:T(8,128)(2,1)S(1)}, u32[]{:S(2)}, u32[]{:S(2)}) collective-permute-start(bf16[512,1152]{1,0:T(8,128)(2,1)S(1)} %get-tuple-element.36), channel_id=1, source_target_pairs={{0,1},{1,0},{2,3},{3,2},{4,5},{5,4},{6,7},{7,6},{8,9},{9,8},{10,11... | collective-permute-start | bytes 3538952 | tf_op jit(solution)/shard_map/ppermute | solution.py:613
  37.0 38.4 %all-to-all-start = ((bf16[16,32,1152]{2,1,0:T(8,128)(2,1)}), bf16[16,32,1152]{2,1,0:T(8,128)(2,1)S(1)}, u32[]{:S(2)}, u32[]{:S(2)}) async-start(bf16[16,32,1152]{2,1,0:T(8,128)(2,1)} %bitcast.6), calls=%async_computation | async-start | bytes 2359296 | tf_op jit(solution)/shard_map/all_to_all | solution.py:619
  51.9 35.8 %collective-permute-start.8 = (bf16[2,128,1024]{2,1,0:T(8,128)(2,1)S(1)}, bf16[2,128,1024]{2,1,0:T(8,128)(2,1)S(1)}, u32[]{:S(2)}, u32[]{:S(2)}) collective-permute-start(bf16[2,128,1024]{2,1,0:T(8,128)(2,1)S(1)} %get-tuple-element.40.after_any), channel_id=1, source_target_pairs={{1,2},{2,1},{3,4},{4,3},{5,6},{6,5},{7,8},{8,7},{9,10},{10,9},{11,... | collective-permute-start | bytes 1572872 | tf_op jit(solution)/shard_map/ppermute | solution.py:615
  53.9 33.9 %collective-permute-start.6 = (bf16[2,128,1024]{2,1,0:T(8,128)(2,1)S(1)}, bf16[2,128,1024]{2,1,0:T(8,128)(2,1)S(1)}, u32[]{:S(2)}, u32[]{:S(2)}) collective-permute-start(bf16[2,128,1024]{2,1,0:T(8,128)(2,1)S(1)} %get-tuple-element.39), channel_id=1, source_target_pairs={{0,1},{1,0},{2,3},{3,2},{4,5},{5,4},{6,7},{7,6},{8,9},{9,8},{10,11... | collective-permute-start | bytes 1572872 | tf_op jit(solution)/shard_map/ppermute | solution.py:621
  55.5 32.3 %collective-permute-start.7 = (bf16[2,128,1024]{2,1,0:T(8,128)(2,1)S(1)}, bf16[2,128,1024]{2,1,0:T(8,128)(2,1)}, u32[]{:S(2)}, u32[]{:S(2)}) collective-permute-start(bf16[2,128,1024]{2,1,0:T(8,128)(2,1)S(1)} %get-tuple-element.40.after_any), channel_id=1, source_target_pairs={{0,63},{31,32},{32,31},{63,0},{64,127},{95,96},{96,95},{127,64},{1... | collective-permute-start | bytes 1572872 | tf_op jit(solution)/shard_map/ppermute | solution.py:620
  76.3 18.5 %all-to-all-start.1 = ((bf16[8,16,1152]{2,1,0:T(8,128)(2,1)}), bf16[8,16,1152]{2,1,0:T(8,128)(2,1)S(1)}, u32[]{:S(2)}, u32[]{:S(2)}) async-start(bf16[8,16,1152]{2,1,0:T(8,128)(2,1)} %bitcast.7), calls=%async_computation.1 | async-start | bytes 589824 | tf_op jit(solution)/shard_map/all_to_all | solution.py:623
  87.7 0.8 copy-start.15
  87.8 1.0 %copy-start.16 = (bf16[2,128,1024]{2,1,0:T(8,128)(2,1)}, bf16[2,128,1024]{2,1,0:T(8,128)(2,1)S(1)}, u32[]{:S(2)}) copy-start(bf16[2,128,1024]{2,1,0:T(8,128)(2,1)S(1)} %collective-permute-done.6.core_any) | copy-start | bytes 1572868

commit v6 on v5

--- a/solution.py
+++ b/solution.py
@@ -256,7 +256,7 @@
 
 def backward_kernel(
     where_ref, c0_ref, c1_ref, c2_ref, c3_ref, truth_ref, var_ref, area_ref, dpt_ref,
-    aggt_ref, hidt_ref, slope_ref, mine_ref, theirs_ref, sg_ref, f_ref, g_ref,
+    aggt_ref, hidt_ref, slope_ref, theirs_ref, sg_ref, grad_ref, f_ref, g_ref,
 ):
     members = f_ref.shape[0]
     nvar = truth_ref.shape[0]
@@ -275,18 +275,24 @@
         )
         grads.append((g_ref[...].T * var_ref[...]).astype(BF16))
     grad = jnp.concatenate(grads, axis=0)
-    out = dot(hidt_ref[...], grad).astype(BF16)
-    mine_ref[:, depth:] = out[:half]
-    theirs_ref[:, depth:] = out[half:]
+    grad_ref[...] = grad
+    theirs_ref[:, depth:] = dot(hidt_ref[half:], grad).astype(BF16)
     for j in range(depth // TILE):
         at = slice(j * TILE, (j + 1) * TILE)
         hg = dot(grad, dpt_ref[:, at])
         for m in range(local):
             rows = slice(m * points, (m + 1) * points)
             sg_ref[rows, at] = (hg[rows] * slope_ref[m, :, at]).astype(BF16)
-        part = dot(aggt_ref[...], sg_ref[:, at]).astype(BF16)
-        mine_ref[:, at] = part[:half]
-        theirs_ref[:, at] = part[half:]
+        theirs_ref[:, at] = dot(aggt_ref[half:], sg_ref[:, at]).astype(BF16)
+
+
+def mine_kernel(grad_ref, sg_ref, aggt_ref, hidt_ref, mine_ref):
+    half, cols = mine_ref.shape
+    depth = sg_ref.shape[1]
+    mine_ref[:, depth:] = dot(hidt_ref[:half], grad_ref[...]).astype(BF16)
+    for j in range(depth // TILE):
+        at = slice(j * TILE, (j + 1) * TILE)
+        mine_ref[:, at] = dot(aggt_ref[:half], sg_ref[:, at]).astype(BF16)
 
 
 def merge_kernel(mine_ref, theirs_ref, after_any, out_hbm, out_ref, out_sem):
@@ -471,7 +477,7 @@
     return call(
         backward_kernel,
         "backward",
-        (part, part, shape((local * points, depth), BF16)),
+        (part, shape((local * points, depth), BF16), shape((local * points, VPAD), BF16)),
         smem(1) + vmem(len(codes) + 7),
         tuple(vmem(3)),
         [
@@ -480,6 +486,19 @@
         ],
         (2 * 10**9, 5 * 10**6),
         (where, *codes, truth, var_row, area_row, dpt, aggt, hidt, slope),
+    )
+
+
+def call_mine(grad, summed_grad, aggt, hidt):
+    return call(
+        mine_kernel,
+        "mine",
+        shape((aggt.shape[0] // 2, summed_grad.shape[1] + VPAD), BF16),
+        vmem(4),
+        vmem(1)[0],
+        [],
+        (10**9, 4 * 10**6),
+        (grad, summed_grad, aggt, hidt),
     )
 
 
@@ -607,10 +626,11 @@
         aggt, hidt, slope = call_factors(
             where, latent, core_lat, odd_lat, cf, summed, hidden
         )
-        mine, theirs, summed_grad = call_backward(
+        theirs, summed_grad, grad = call_backward(
             where, codes, truth, var_row, area_row, dpt, aggt, hidt, slope
         )
         theirs = lax.ppermute(theirs, "core", swap)
+        mine = call_mine(grad, summed_grad, aggt, hidt)
         core_send, odd_send = call_rows(cft, summed_grad, local)
         near_grad = lax.ppermute(odd_send, SPACE, near)
         part = call_merge(mine, theirs, odd_send)

time: 96 us -> 95.5 us (level)
    pallas_call x10 -> x11, Pallas kernels: 26.9 us -> 27.1 us  [call(): pl.pallas_call(kernel, out_shape=out_shape, in_specs=in_specs, out_specs=...]
    unnamed x34 -> x38, local copies, waits for them, and re-layouts: 4.9 us -> 4.89 us
  transfers between devices with their start and end apart: 11 -> 11, of which waited for: 4 -> 4; matrix products, arithmetic and copies ran while one was open for 2% -> 2% of each run, Pallas kernels for 20% -> 21%
where the time goes in v6:
time: 95.5 us; the launch traced here: 94.9 us
  starting transfers between devices  35.1 us (37%)
  Pallas kernels  27.1 us (28%)
  waiting for transfers between devices  25.3 us (26%)
  local copies, waits for them, and re-layouts  6.5 us (7%)
    pallas_call x11, Pallas kernels, call(): pl.pallas_call(kernel, out_shape=out_shape, in_specs=in_specs, out_specs=...  27.1 us
    all_to_all x1, waiting for transfers between devices, body(): got = lax.all_to_all(part, ('x', 'y'), 0, 0, tiled=True)  18.4 us
    all_to_all x1, starting transfers between devices, body(): got = lax.all_to_all(part, ('x', 'y'), 0, 0, tiled=True)  15.1 us
    all_to_all x1, starting transfers between devices, body(): got = lax.all_to_all(plane, ('zhi', 'ens'), 0, 0, tiled=True)  7.69 us
    unnamed x38, local copies, waits for them, and re-layouts  4.89 us
    ppermute x3, starting transfers between devices, body(): lax.ppermute(coded, 'ens', [(e, e ^ k) for e in range(ens)])  4.45 us
    ppermute x3, waiting for transfers between devices, body(): lax.ppermute(coded, 'ens', [(e, e ^ k) for e in range(ens)])  4.23 us
    ppermute x1, starting transfers between devices, body(): lax.ppermute(latent, SPACE, odd_pairs).reshape(local * rows, depth)  2.28 us
  transfers between devices with their start and end apart: 11, of which 4 were waited for; matrix products, arithmetic and copies ran while one was open for 2% of the time, Pallas kernels for 21%

profile of v6, /device:TPU:8, one launch (start us, length us, event | category | flops | bytes accessed | tf_op | source)
XLA Modules:
  0.0 94.9 jit_solution(11271004778801986741)
XLA Ops:
  0.6 0.1 collective-permute-start.1
  0.7 2.3 %collective-permute-start = (bf16[2,128,1024]{2,1,0:T(8,128)(2,1)}, bf16[2,128,1024]{2,1,0:T(8,128)(2,1)S(1)}, u32[]{:S(2)}, u32[]{:S(2)}) collective-permute-start(bf16[2,128,1024]{2,1,0:T(8,128)(2,1)} %lat_ref.1), channel_id=1, source_target_pairs={{0,63},{1,2},{2,1},{3,4},{4,3},{5,6},{6,5},{7,8},{8,7},{9,10},{10,... | collective-permute-start | bytes 1572872 | tf_op jit(solution)/shard_map/ppermute | solution.py:614
  3.0 1.0 %pad.8.dpt_ref = bf16[128,1024]{1,0:T(8,128)(2,1)S(1)} pad(bf16[100,1024]{1,0:T(8,128)(2,1)} %bitcast.12, bf16[]{:T(256)} %constant.13.clone.1), padding=0_28x0_0 | pad | bytes 466946 | tf_op jit(solution)/shard_map/jit(_pad)/pad | solution.py:616
  4.0 0.7 pad_bitcast_fusion.var_ref
  4.6 0.1 pad_add_fusion.where_ref
  4.7 0.0 collective-permute-done.1.clat_hbm.clat_ref
  4.7 1.2 %copy-done.9 = bf16[2,128,1024]{2,1,0:T(8,128)(2,1)S(1)} copy-done((bf16[2,128,1024]{2,1,0:T(8,128)(2,1)S(1)}, bf16[2,128,1024]{2,1,0:T(8,128)(2,1)}, u32[]{:S(2)}) %copy-start.9) | copy-done | bytes 524312
  5.9 0.7 copy-done.12
  6.6 0.7 copy-done.13
  7.3 0.7 copy-done.14
  8.0 0.7 copy-done.16
  8.6 5.9 %prepare.1 = (bf16[256,768]{1,0:T(8,128)(2,1)S(1)}, bf16[384,512]{1,0:T(8,128)(2,1)S(1)}, bf16[256,256]{1,0:T(8,128)(2,1)S(1)}, f32[2,256,1024]{2,1,0:T(8,128)S(1)}) custom-call(s32[2]{0:T(128)S(1)} %pad_add_fusion.where_ref, s32[2]{0:T(128)S(1)} %copy-done.16, s32[2,512]{1,0:T(2,128)S(1)} %copy-done.12, s32[2,512]{1,0:T(2,128)S(1)} %copy-done.13, ...), custom_call_target="tpu_custom_call" | custom-call | flops 3000000000 | bytes 6000000 | tf_op jit(solution)/shard_map/prepare/pallas_call | solution.py:406
  14.5 0.0 copy-start.2
  14.5 0.0 collective-permute-done
  14.6 2.8 %forward.1 = (f32[2,256,1024]{2,1,0:T(8,128)S(1)}, bf16[2,256,1024]{2,1,0:T(8,128)(2,1)S(1)}, s16[2,112,256]{2,1,0:T(8,128)(2,1)S(1)}) custom-call(bf16[256,1024]{1,0:T(8,128)(2,1)S(1)} %bitcast.9, bf16[1024,1024]{1,0:T(8,128)(2,1)S(1)} %copy-done.1, bf16[256,256]{1,0:T(8,128)(2,1)S(1)} %get-tuple-element.24.cfo_ref, ...), custom_call_target="tpu_custom_call" | custom-call | flops 2000000000 | bytes 8000000 | tf_op jit(solution)/shard_map/forward/pallas_call | solution.py:406
  17.4 0.2 collective-permute-start.2
  17.6 3.3 %collective-permute-start.3 = (s16[2,112,256]{2,1,0:T(8,128)(2,1)S(1)}, s16[2,112,256]{2,1,0:T(8,128)(2,1)S(1)}, u32[]{:S(2)}, u32[]{:S(2)}) collective-permute-start(s16[2,112,256]{2,1,0:T(8,128)(2,1)S(1)} %get-tuple-element.26.c0_any.c0_ref), channel_id=1, source_target_pairs={{0,128},{64,192},{128,0},{192,64},{1,129},{65,193},{129,1},{193,65... | collective-permute-start | bytes 344072 | tf_op jit(solution)/shard_map/ppermute | solution.py:624
  20.9 0.9 collective-permute-start.4
  21.8 3.5 %factors.1 = (bf16[1024,512]{1,0:T(8,128)(2,1)S(1)}, bf16[1024,512]{1,0:T(8,128)(2,1)S(1)}, f32[2,256,1024]{2,1,0:T(8,128)S(1)}) custom-call(s32[2]{0:T(128)S(1)} %pad_add_fusion.where_ref, bf16[2,128,1024]{2,1,0:T(8,128)(2,1)S(1)} %copy-done.9, bf16[2,128,1024]{2,1,0:T(8,128)(2,1)S(1)} %collective-permute-done.1.clat_hbm.clat_ref, ...), custom_call_target="tpu_custom_call" | custom-call | flops 3000000000 | bytes 10000000 | tf_op jit(solution)/shard_map/factors/pallas_call | solution.py:406
  25.3 0.0 collective-permute-done.2.c1_any.c1_ref
  25.3 4.2 %collective-permute-done.3.c2_any.c2_ref = s16[2,112,256]{2,1,0:T(8,128)(2,1)S(1)} collective-permute-done((s16[2,112,256]{2,1,0:T(8,128)(2,1)S(1)}, s16[2,112,256]{2,1,0:T(8,128)(2,1)S(1)}, u32[]{:S(2)}, u32[]{:S(2)}) %collective-permute-start.3) | collective-permute-done | bytes 114720 | tf_op jit(solution)/shard_map/ppermute | solution.py:624
  29.5 0.0 collective-permute-done.4.c3_any.c3_ref
  29.6 2.6 %backward.1 = (bf16[512,1152]{1,0:T(8,128)(2,1)S(1)}, bf16[512,1024]{1,0:T(8,128)(2,1)S(1)}, bf16[512,128]{1,0:T(8,128)(2,1)S(1)}) custom-call(s32[2]{0:T(128)S(1)} %pad_add_fusion.where_ref, s16[2,112,256]{2,1,0:T(8,128)(2,1)S(1)} %get-tuple-element.26.c0_any.c0_ref, s16[2,112,256]{2,1,0:T(8,128)(2,1)S(1)} %collective-permute-done.2.c1_any.c1_ref, ...), custom_call_target="tpu_custom_call" | custom-call | flops 2000000000 | bytes 5000000 | tf_op jit(solution)/shard_map/backward/pallas_call | solution.py:406
  32.2 0.4 collective-permute-start.5
  32.6 1.0 %rows.1 = (bf16[2,128,1024]{2,1,0:T(8,128)(2,1)S(1)}, bf16[2,128,1024]{2,1,0:T(8,128)(2,1)S(1)}) custom-call(bf16[384,512]{1,0:T(8,128)(2,1)S(1)} %get-tuple-element.27.cft_ref.cft_hbm, bf16[512,1024]{1,0:T(8,128)(2,1)S(1)} %get-tuple-element.34.sg_ref.sg_hbm), custom_call_target="tpu_custom_call" | custom-call | flops 1000000000 | bytes 3000000 | tf_op jit(solution)/shard_map/rows/pallas_call | solution.py:406
  33.7 0.0 copy-start.10
  33.7 0.9 mine.1.mine_ref
  34.5 0.0 copy-done.10
  34.6 0.6 collective-permute-done.5.theirs_ref
  35.2 1.1 %merge.1 = bf16[512,1152]{1,0:T(8,128)(2,1)} custom-call(bf16[512,1152]{1,0:T(8,128)(2,1)S(1)} %mine.1.mine_ref, bf16[512,1152]{1,0:T(8,128)(2,1)S(1)} %collective-permute-done.5.theirs_ref, bf16[2,128,1024]{2,1,0:T(8,128)(2,1)S(1)} %get-tuple-element.40.after_any), custom_call_target="tpu_custom_call" | custom-call | flops 1000000 | bytes 4000000 | tf_op jit(solution)/shard_map/merge/pallas_call | solution.py:406
  36.3 0.0 copy-start.11
  36.3 15.1 %all-to-all-start = ((bf16[16,32,1152]{2,1,0:T(8,128)(2,1)}), bf16[16,32,1152]{2,1,0:T(8,128)(2,1)S(1)}, u32[]{:S(2)}, u32[]{:S(2)}) async-start(bf16[16,32,1152]{2,1,0:T(8,128)(2,1)} %bitcast.6), calls=%async_computation | async-start | bytes 2359296 | tf_op jit(solution)/shard_map/all_to_all | solution.py:639
  51.4 1.9 %collective-permute-start.8 = (bf16[2,128,1024]{2,1,0:T(8,128)(2,1)S(1)}, bf16[2,128,1024]{2,1,0:T(8,128)(2,1)S(1)}, u32[]{:S(2)}, u32[]{:S(2)}) collective-permute-start(bf16[2,128,1024]{2,1,0:T(8,128)(2,1)S(1)} %get-tuple-element.40.after_any), channel_id=1, source_target_pairs={{1,2},{2,1},{3,4},{4,3},{5,6},{6,5},{7,8},{8,7},{9,10},{10,9},{11,... | collective-permute-start | bytes 1572872 | tf_op jit(solution)/shard_map/ppermute | solution.py:635
  53.3 0.0 copy-done.11
  53.3 1.7 %collective-permute-start.6 = (bf16[2,128,1024]{2,1,0:T(8,128)(2,1)S(1)}, bf16[2,128,1024]{2,1,0:T(8,128)(2,1)S(1)}, u32[]{:S(2)}, u32[]{:S(2)}) collective-permute-start(bf16[2,128,1024]{2,1,0:T(8,128)(2,1)S(1)} %copy-done.11), channel_id=1, source_target_pairs={{0,1},{1,0},{2,3},{3,2},{4,5},{5,4},{6,7},{7,6},{8,9},{9,8},{10,11... | collective-permute-start | bytes 1572872 | tf_op jit(solution)/shard_map/ppermute | solution.py:641
  55.0 1.5 %collective-permute-start.7 = (bf16[2,128,1024]{2,1,0:T(8,128)(2,1)S(1)}, bf16[2,128,1024]{2,1,0:T(8,128)(2,1)}, u32[]{:S(2)}, u32[]{:S(2)}) collective-permute-start(bf16[2,128,1024]{2,1,0:T(8,128)(2,1)S(1)} %get-tuple-element.40.after_any), channel_id=1, source_target_pairs={{0,63},{31,32},{32,31},{63,0},{64,127},{95,96},{96,95},{127,64},{1... | collective-permute-start | bytes 1572872 | tf_op jit(solution)/shard_map/ppermute | solution.py:640
  56.5 18.4 %all-to-all-done.got_ref = bf16[16,32,1152]{2,1,0:T(8,128)(2,1)S(1)} async-done(((bf16[16,32,1152]{2,1,0:T(8,128)(2,1)}), bf16[16,32,1152]{2,1,0:T(8,128)(2,1)S(1)}, u32[]{:S(2)}, u32[]{:S(2)}) %all-to-all-start) | async-done | bytes 1179680 | tf_op jit(solution)/shard_map/all_to_all | solution.py:639
  74.8 0.9 plane.1
  75.7 7.7 %all-to-all-start.1 = ((bf16[8,16,1152]{2,1,0:T(8,128)(2,1)}), bf16[8,16,1152]{2,1,0:T(8,128)(2,1)S(1)}, u32[]{:S(2)}, u32[]{:S(2)}) async-start(bf16[8,16,1152]{2,1,0:T(8,128)(2,1)} %bitcast.7), calls=%async_computation.1 | async-start | bytes 589824 | tf_op jit(solution)/shard_map/all_to_all | solution.py:643
  83.4 3.8 %score.1 = f32[100,256]{1,0:T(8,128)} custom-call(s32[2]{0:T(128)} %copy-done.8, s16[2,112,256]{2,1,0:T(8,128)(2,1)} %copy-done.3, s16[2,112,256]{2,1,0:T(8,128)(2,1)} %copy-done.4, s16[2,112,256]{2,1,0:T(8,128)(2,1)} %copy-done.5, s16[2,112,256]{2,1,0:T(8,128)(2,1)} %copy-done.6, f32[100,256]{1,0:T(8,128)} %truth_ref.1), custom_call_target="tpu_custom_call" | custom-call | flops 10000000 | bytes 1000000 | tf_op jit(solution)/shard_map/score/pallas_call | solution.py:406
  87.2 0.0 collective-permute-done.8.near_any
  87.2 0.0 collective-permute-done.6.core_any
  87.3 0.0 collective-permute-done.7.far_any
  87.3 0.8 copy-done.17
  88.0 0.2 copy-done.18
  88.2 4.0 %latent.1 = bf16[2,128,1024]{2,1,0:T(8,128)(2,1)} custom-call(bf16[384,512]{1,0:T(8,128)(2,1)} %copy-done.2, bf16[512,1024]{1,0:T(8,128)(2,1)} %copy-done, bf16[1024,1024]{1,0:T(8,128)(2,1)} %w_hbm.3, bf16[2,128,1024]{2,1,0:T(8,128)(2,1)} %copy-done.18, bf16[2,128,1024]{2,1,0:T(8,128)(2,1)} %collective-permute-done.7.far_any, bf16[2,128,1024]{2,1,0:T(8,128)(2,1)} %copy-done.17), custom_call_target="tpu_custom_call" | custom-call | flops 1000000000 | bytes 5000000 | tf_op jit(solution)/shard_map/latent/pallas_call | solution.py:406
  92.2 2.1 %all-to-all-done.1.got_ref = bf16[8,16,1152]{2,1,0:T(8,128)(2,1)S(1)} async-done(((bf16[8,16,1152]{2,1,0:T(8,128)(2,1)}), bf16[8,16,1152]{2,1,0:T(8,128)(2,1)S(1)}, u32[]{:S(2)}, u32[]{:S(2)}) %all-to-all-start.1) | async-done | bytes 294944 | tf_op jit(solution)/shard_map/all_to_all | solution.py:643
  94.3 0.7 final.1
  (26 shorter events, 0.0 us)
Async XLA Ops:
  0.6 4.1 %collective-permute-start.1 = (bf16[2,128,1024]{2,1,0:T(8,128)(2,1)}, bf16[2,128,1024]{2,1,0:T(8,128)(2,1)S(1)}, u32[]{:S(2)}, u32[]{:S(2)}) collective-permute-start(bf16[2,128,1024]{2,1,0:T(8,128)(2,1)} %lat_ref.1), channel_id=1, source_target_pairs={{0,1},{1,0},{2,3},{3,2},{4,5},{5,4},{6,7},{7,6},{8,9},{9,8},{10,11... | collective-permute-start | bytes 1572872 | tf_op jit(solution)/shard_map/ppermute | solution.py:615
  0.7 13.8 %collective-permute-start = (bf16[2,128,1024]{2,1,0:T(8,128)(2,1)}, bf16[2,128,1024]{2,1,0:T(8,128)(2,1)S(1)}, u32[]{:S(2)}, u32[]{:S(2)}) collective-permute-start(bf16[2,128,1024]{2,1,0:T(8,128)(2,1)} %lat_ref.1), channel_id=1, source_target_pairs={{0,63},{1,2},{2,1},{3,4},{4,3},{5,6},{6,5},{7,8},{8,7},{9,10},{10,... | collective-permute-start | bytes 1572872 | tf_op jit(solution)/shard_map/ppermute | solution.py:614
  4.7 24.8 %copy-start.8 = (s32[2]{0:T(128)}, s32[2]{0:T(128)S(1)}, u32[]{:S(2)}) copy-start(s32[2]{0:T(128)S(1)} %pad_add_fusion.where_ref) | copy-start | bytes 28
  4.7 9.8 %copy-start.1 = (bf16[1024,1024]{1,0:T(8,128)(2,1)S(1)}, bf16[1024,1024]{1,0:T(8,128)(2,1)}, u32[]{:S(2)}) copy-start(bf16[1024,1024]{1,0:T(8,128)(2,1)} %w_hbm.3) | copy-start | bytes 6291460
  4.7 1.2 %copy-start.9 = (bf16[2,128,1024]{2,1,0:T(8,128)(2,1)S(1)}, bf16[2,128,1024]{2,1,0:T(8,128)(2,1)}, u32[]{:S(2)}) copy-start(bf16[2,128,1024]{2,1,0:T(8,128)(2,1)} %lat_ref.1) | copy-start | bytes 1572868
  5.9 0.7 copy-start.12
  6.6 0.7 copy-start.13
  7.3 0.7 copy-start.14
  8.0 0.7 copy-start.16
  14.5 18.1 %copy-start.2 = (bf16[384,512]{1,0:T(8,128)(2,1)}, bf16[384,512]{1,0:T(8,128)(2,1)S(1)}, u32[]{:S(2)}) copy-start(bf16[384,512]{1,0:T(8,128)(2,1)S(1)} %get-tuple-element.27.cft_ref.cft_hbm) | copy-start | bytes 1179652
  17.3 12.2 %copy-start.3 = (s16[2,112,256]{2,1,0:T(8,128)(2,1)}, s16[2,112,256]{2,1,0:T(8,128)(2,1)S(1)}, u32[]{:S(2)}) copy-start(s16[2,112,256]{2,1,0:T(8,128)(2,1)S(1)} %get-tuple-element.26.c0_any.c0_ref) | copy-start | bytes 344068
  17.4 7.9 %collective-permute-start.2 = (s16[2,112,256]{2,1,0:T(8,128)(2,1)S(1)}, s16[2,112,256]{2,1,0:T(8,128)(2,1)S(1)}, u32[]{:S(2)}, u32[]{:S(2)}) collective-permute-start(s16[2,112,256]{2,1,0:T(8,128)(2,1)S(1)} %get-tuple-element.26.c0_any.c0_ref), channel_id=1, source_target_pairs={{0,64},{64,0},{128,192},{192,128},{1,65},{65,1},{129,193},{193,129... | collective-permute-start | bytes 344072 | tf_op jit(solution)/shard_map/ppermute | solution.py:624
  17.6 11.9 %collective-permute-start.3 = (s16[2,112,256]{2,1,0:T(8,128)(2,1)S(1)}, s16[2,112,256]{2,1,0:T(8,128)(2,1)S(1)}, u32[]{:S(2)}, u32[]{:S(2)}) collective-permute-start(s16[2,112,256]{2,1,0:T(8,128)(2,1)S(1)} %get-tuple-element.26.c0_any.c0_ref), channel_id=1, source_target_pairs={{0,128},{64,192},{128,0},{192,64},{1,129},{65,193},{129,1},{193,65... | collective-permute-start | bytes 344072 | tf_op jit(solution)/shard_map/ppermute | solution.py:624
  20.9 8.7 %collective-permute-start.4 = (s16[2,112,256]{2,1,0:T(8,128)(2,1)S(1)}, s16[2,112,256]{2,1,0:T(8,128)(2,1)S(1)}, u32[]{:S(2)}, u32[]{:S(2)}) collective-permute-start(s16[2,112,256]{2,1,0:T(8,128)(2,1)S(1)} %get-tuple-element.26.c0_any.c0_ref), channel_id=1, source_target_pairs={{0,192},{64,128},{128,64},{192,0},{1,193},{65,129},{129,65},{193,1... | collective-permute-start | bytes 344072 | tf_op jit(solution)/shard_map/ppermute | solution.py:624
  21.8 7.7 %copy-start.7 = (f32[100,256]{1,0:T(8,128)S(1)}, f32[100,256]{1,0:T(8,128)}, u32[]{:S(2)}) copy-start(f32[100,256]{1,0:T(8,128)} %truth_ref.1) | copy-start | bytes 307204
  21.8 7.8 %copy-start.15 = (f32[256]{0:T(256)S(1)}, f32[256]{0:T(256)}, u32[]{:S(2)}) copy-start(f32[256]{0:T(256)} %param.14) | copy-start | bytes 3076
  25.3 6.9 %copy-start.4 = (s16[2,112,256]{2,1,0:T(8,128)(2,1)}, s16[2,112,256]{2,1,0:T(8,128)(2,1)S(1)}, u32[]{:S(2)}) copy-start(s16[2,112,256]{2,1,0:T(8,128)(2,1)S(1)} %collective-permute-done.2.c1_any.c1_ref) | copy-start | bytes 344068
  29.5 2.7 %copy-start.5 = (s16[2,112,256]{2,1,0:T(8,128)(2,1)}, s16[2,112,256]{2,1,0:T(8,128)(2,1)S(1)}, u32[]{:S(2)}) copy-start(s16[2,112,256]{2,1,0:T(8,128)(2,1)S(1)} %collective-permute-done.3.c2_any.c2_ref) | copy-start | bytes 344068
  29.5 2.7 %copy-start.6 = (s16[2,112,256]{2,1,0:T(8,128)(2,1)}, s16[2,112,256]{2,1,0:T(8,128)(2,1)S(1)}, u32[]{:S(2)}) copy-start(s16[2,112,256]{2,1,0:T(8,128)(2,1)S(1)} %collective-permute-done.4.c3_any.c3_ref) | copy-start | bytes 344068
  32.2 1.4 %copy-start = (bf16[512,1024]{1,0:T(8,128)(2,1)}, bf16[512,1024]{1,0:T(8,128)(2,1)S(1)}, u32[]{:S(2)}) copy-start(bf16[512,1024]{1,0:T(8,128)(2,1)S(1)} %get-tuple-element.34.sg_ref.sg_hbm) | copy-start | bytes 3145732
  32.2 2.9 %collective-permute-start.5 = (bf16[512,1152]{1,0:T(8,128)(2,1)S(1)}, bf16[512,1152]{1,0:T(8,128)(2,1)S(1)}, u32[]{:S(2)}, u32[]{:S(2)}) collective-permute-start(bf16[512,1152]{1,0:T(8,128)(2,1)S(1)} %get-tuple-element.36), channel_id=1, source_target_pairs={{0,1},{1,0},{2,3},{3,2},{4,5},{5,4},{6,7},{7,6},{8,9},{9,8},{10,11... | collective-permute-start | bytes 3538952 | tf_op jit(solution)/shard_map/ppermute | solution.py:632
  33.7 0.9 copy-start.10
  36.3 17.0 %copy-start.11 = (bf16[2,128,1024]{2,1,0:T(8,128)(2,1)S(1)}, bf16[2,128,1024]{2,1,0:T(8,128)(2,1)}, u32[]{:S(2)}) copy-start(bf16[2,128,1024]{2,1,0:T(8,128)(2,1)} %copy-done.10) | copy-start | bytes 1572868
  36.3 38.5 %all-to-all-start = ((bf16[16,32,1152]{2,1,0:T(8,128)(2,1)}), bf16[16,32,1152]{2,1,0:T(8,128)(2,1)S(1)}, u32[]{:S(2)}, u32[]{:S(2)}) async-start(bf16[16,32,1152]{2,1,0:T(8,128)(2,1)} %bitcast.6), calls=%async_computation | async-start | bytes 2359296 | tf_op jit(solution)/shard_map/all_to_all | solution.py:639
  51.4 35.8 %collective-permute-start.8 = (bf16[2,128,1024]{2,1,0:T(8,128)(2,1)S(1)}, bf16[2,128,1024]{2,1,0:T(8,128)(2,1)S(1)}, u32[]{:S(2)}, u32[]{:S(2)}) collective-permute-start(bf16[2,128,1024]{2,1,0:T(8,128)(2,1)S(1)} %get-tuple-element.40.after_any), channel_id=1, source_target_pairs={{1,2},{2,1},{3,4},{4,3},{5,6},{6,5},{7,8},{8,7},{9,10},{10,9},{11,... | collective-permute-start | bytes 1572872 | tf_op jit(solution)/shard_map/ppermute | solution.py:635
  53.3 33.9 %collective-permute-start.6 = (bf16[2,128,1024]{2,1,0:T(8,128)(2,1)S(1)}, bf16[2,128,1024]{2,1,0:T(8,128)(2,1)S(1)}, u32[]{:S(2)}, u32[]{:S(2)}) collective-permute-start(bf16[2,128,1024]{2,1,0:T(8,128)(2,1)S(1)} %copy-done.11), channel_id=1, source_target_pairs={{0,1},{1,0},{2,3},{3,2},{4,5},{5,4},{6,7},{7,6},{8,9},{9,8},{10,11... | collective-permute-start | bytes 1572872 | tf_op jit(solution)/shard_map/ppermute | solution.py:641
  55.0 32.2 %collective-permute-start.7 = (bf16[2,128,1024]{2,1,0:T(8,128)(2,1)S(1)}, bf16[2,128,1024]{2,1,0:T(8,128)(2,1)}, u32[]{:S(2)}, u32[]{:S(2)}) collective-permute-start(bf16[2,128,1024]{2,1,0:T(8,128)(2,1)S(1)} %get-tuple-element.40.after_any), channel_id=1, source_target_pairs={{0,63},{31,32},{32,31},{63,0},{64,127},{95,96},{96,95},{127,64},{1... | collective-permute-start | bytes 1572872 | tf_op jit(solution)/shard_map/ppermute | solution.py:640
  75.7 18.5 %all-to-all-start.1 = ((bf16[8,16,1152]{2,1,0:T(8,128)(2,1)}), bf16[8,16,1152]{2,1,0:T(8,128)(2,1)S(1)}, u32[]{:S(2)}, u32[]{:S(2)}) async-start(bf16[8,16,1152]{2,1,0:T(8,128)(2,1)} %bitcast.7), calls=%async_computation.1 | async-start | bytes 589824 | tf_op jit(solution)/shard_map/all_to_all | solution.py:643
  87.2 0.8 copy-start.17
  87.2 1.0 %copy-start.18 = (bf16[2,128,1024]{2,1,0:T(8,128)(2,1)}, bf16[2,128,1024]{2,1,0:T(8,128)(2,1)S(1)}, u32[]{:S(2)}) copy-start(bf16[2,128,1024]{2,1,0:T(8,128)(2,1)S(1)} %collective-permute-done.6.core_any) | copy-start | bytes 1572868

commit v7 on v6

--- a/solution.py
+++ b/solution.py
@@ -329,14 +329,14 @@
 def plane_kernel(got_ref, out_hbm, out_ref, out_sem):
     per = out_hbm.shape[2]
     outs = []
-    for z in range(out_hbm.shape[0]):
+    for z in range(out_hbm.shape[1]):
         at = slice(z * per, (z + 1) * per)
         total = got_ref[0, at].astype(F32)
         for k in range(1, got_ref.shape[0]):
             total = total + got_ref[k, at].astype(F32)
         out_ref[z] = total.astype(BF16)
-        for e in range(out_hbm.shape[1]):
-            outs.append(start_copy(out_ref.at[z], out_hbm.at[z, e], out_sem.at[z, e]))
+        for e in range(out_hbm.shape[0]):
+            outs.append(start_copy(out_ref.at[z], out_hbm.at[e, z], out_sem.at[z, e]))
     for copy in outs:
         copy.wait()
 
@@ -530,7 +530,7 @@
 
 
 def call_plane(got, ens):
-    out_shape = shape((2, ens, got.shape[1] // 2, got.shape[2]), BF16)
+    out_shape = shape((ens, 2, got.shape[1] // 2, got.shape[2]), BF16)
     return call(
         plane_kernel,
         "plane",
@@ -640,7 +640,7 @@
         far_grad = lax.ppermute(odd_send, SPACE, far)
         core_grad = lax.ppermute(core_send, "core", swap)
         plane = call_plane(got, ens).reshape(2 * ens, per, got.shape[2])
-        got = lax.all_to_all(plane, ("zhi", "ens"), 0, 0, tiled=True)
+        got = lax.all_to_all(plane, ("ens", "zhi"), 0, 0, tiled=True)
         score = call_score(where, codes, truth)
         grad_latent = call_latent(cft, summed_grad, src_weight, core_grad, far_grad, near_grad)
         scaling = 1.0 / math.sqrt(members * points * count)

time: 95.5 us -> 93.7 us (0.981)
  waiting for transfers between devices: 25.3 us -> 23.2 us
    all_to_all x1, waiting for transfers between devices: 2.06 us -> 0.01 us  [body(): got = lax.all_to_all(plane, ('ens', 'zhi'), 0, 0, tiled=True)]
  transfers between devices with their start and end apart: 11 -> 11, of which waited for: 4 -> 3; matrix products, arithmetic and copies ran while one was open for 2% -> 2% of each run, Pallas kernels for 21% -> 21%
where the time goes in v7:
time: 93.7 us; the launch traced here: 92.9 us
  starting transfers between devices  35.1 us (37%)
  Pallas kernels  27.1 us (29%)
  waiting for transfers between devices  23.2 us (25%)
  local copies, waits for them, and re-layouts  6.5 us (7%)
    pallas_call x11, Pallas kernels, call(): pl.pallas_call(kernel, out_shape=out_shape, in_specs=in_specs, out_specs=...  27.1 us
    all_to_all x1, waiting for transfers between devices, body(): got = lax.all_to_all(part, ('x', 'y'), 0, 0, tiled=True)  18.4 us
    all_to_all x1, starting transfers between devices, body(): got = lax.all_to_all(part, ('x', 'y'), 0, 0, tiled=True)  15.1 us
    all_to_all x1, starting transfers between devices, body(): got = lax.all_to_all(plane, ('ens', 'zhi'), 0, 0, tiled=True)  7.69 us
    unnamed x38, local copies, waits for them, and re-layouts  4.89 us
    ppermute x3, starting transfers between devices, body(): lax.ppermute(coded, 'ens', [(e, e ^ k) for e in range(ens)])  4.45 us
    ppermute x3, waiting for transfers between devices, body(): lax.ppermute(coded, 'ens', [(e, e ^ k) for e in range(ens)])  4.23 us
    ppermute x1, starting transfers between devices, body(): lax.ppermute(latent, SPACE, odd_pairs).reshape(local * rows, depth)  2.28 us
  transfers between devices with their start and end apart: 11, of which 3 were waited for; matrix products, arithmetic and copies ran while one was open for 2% of the time, Pallas kernels for 21%

profile of v7, /device:TPU:8, one launch (start us, length us, event | category | flops | bytes accessed | tf_op | source)
XLA Modules:
  0.0 92.9 jit_solution(601643847926481005)
XLA Ops:
  0.6 0.1 collective-permute-start.1
  0.7 2.3 %collective-permute-start = (bf16[2,128,1024]{2,1,0:T(8,128)(2,1)}, bf16[2,128,1024]{2,1,0:T(8,128)(2,1)S(1)}, u32[]{:S(2)}, u32[]{:S(2)}) collective-permute-start(bf16[2,128,1024]{2,1,0:T(8,128)(2,1)} %lat_ref.1), channel_id=1, source_target_pairs={{0,63},{1,2},{2,1},{3,4},{4,3},{5,6},{6,5},{7,8},{8,7},{9,10},{10,... | collective-permute-start | bytes 1572872 | tf_op jit(solution)/shard_map/ppermute | solution.py:614
  3.0 1.0 %pad.8.dpt_ref = bf16[128,1024]{1,0:T(8,128)(2,1)S(1)} pad(bf16[100,1024]{1,0:T(8,128)(2,1)} %bitcast.12, bf16[]{:T(256)} %constant.13.clone.1), padding=0_28x0_0 | pad | bytes 466946 | tf_op jit(solution)/shard_map/jit(_pad)/pad | solution.py:616
  4.0 0.7 pad_bitcast_fusion.var_ref
  4.6 0.1 pad_add_fusion.where_ref
  4.7 0.0 collective-permute-done.1.clat_hbm.clat_ref
  4.7 1.2 %copy-done.9 = bf16[2,128,1024]{2,1,0:T(8,128)(2,1)S(1)} copy-done((bf16[2,128,1024]{2,1,0:T(8,128)(2,1)S(1)}, bf16[2,128,1024]{2,1,0:T(8,128)(2,1)}, u32[]{:S(2)}) %copy-start.9) | copy-done | bytes 524312
  5.9 0.7 copy-done.12
  6.6 0.7 copy-done.13
  7.3 0.7 copy-done.14
  8.0 0.7 copy-done.16
  8.6 5.9 %prepare.1 = (bf16[256,768]{1,0:T(8,128)(2,1)S(1)}, bf16[384,512]{1,0:T(8,128)(2,1)S(1)}, bf16[256,256]{1,0:T(8,128)(2,1)S(1)}, f32[2,256,1024]{2,1,0:T(8,128)S(1)}) custom-call(s32[2]{0:T(128)S(1)} %pad_add_fusion.where_ref, s32[2]{0:T(128)S(1)} %copy-done.16, s32[2,512]{1,0:T(2,128)S(1)} %copy-done.12, s32[2,512]{1,0:T(2,128)S(1)} %copy-done.13, ...), custom_call_target="tpu_custom_call" | custom-call | flops 3000000000 | bytes 6000000 | tf_op jit(solution)/shard_map/prepare/pallas_call | solution.py:406
  14.5 0.0 copy-start.2
  14.5 0.0 collective-permute-done
  14.6 0.0 copy-done.1
  14.6 2.8 %forward.1 = (f32[2,256,1024]{2,1,0:T(8,128)S(1)}, bf16[2,256,1024]{2,1,0:T(8,128)(2,1)S(1)}, s16[2,112,256]{2,1,0:T(8,128)(2,1)S(1)}) custom-call(bf16[256,1024]{1,0:T(8,128)(2,1)S(1)} %bitcast.9, bf16[1024,1024]{1,0:T(8,128)(2,1)S(1)} %copy-done.1, bf16[256,256]{1,0:T(8,128)(2,1)S(1)} %get-tuple-element.24.cfo_ref, ...), custom_call_target="tpu_custom_call" | custom-call | flops 2000000000 | bytes 8000000 | tf_op jit(solution)/shard_map/forward/pallas_call | solution.py:406
  17.4 0.2 collective-permute-start.2
  17.6 3.3 %collective-permute-start.3 = (s16[2,112,256]{2,1,0:T(8,128)(2,1)S(1)}, s16[2,112,256]{2,1,0:T(8,128)(2,1)S(1)}, u32[]{:S(2)}, u32[]{:S(2)}) collective-permute-start(s16[2,112,256]{2,1,0:T(8,128)(2,1)S(1)} %get-tuple-element.26.c0_any.c0_ref), channel_id=1, source_target_pairs={{0,128},{64,192},{128,0},{192,64},{1,129},{65,193},{129,1},{193,65... | collective-permute-start | bytes 344072 | tf_op jit(solution)/shard_map/ppermute | solution.py:624
  20.9 0.9 %collective-permute-start.4 = (s16[2,112,256]{2,1,0:T(8,128)(2,1)S(1)}, s16[2,112,256]{2,1,0:T(8,128)(2,1)S(1)}, u32[]{:S(2)}, u32[]{:S(2)}) collective-permute-start(s16[2,112,256]{2,1,0:T(8,128)(2,1)S(1)} %get-tuple-element.26.c0_any.c0_ref), channel_id=1, source_target_pairs={{0,192},{64,128},{128,64},{192,0},{1,193},{65,129},{129,65},{193,1... | collective-permute-start | bytes 344072 | tf_op jit(solution)/shard_map/ppermute | solution.py:624
  21.8 3.5 %factors.1 = (bf16[1024,512]{1,0:T(8,128)(2,1)S(1)}, bf16[1024,512]{1,0:T(8,128)(2,1)S(1)}, f32[2,256,1024]{2,1,0:T(8,128)S(1)}) custom-call(s32[2]{0:T(128)S(1)} %pad_add_fusion.where_ref, bf16[2,128,1024]{2,1,0:T(8,128)(2,1)S(1)} %copy-done.9, bf16[2,128,1024]{2,1,0:T(8,128)(2,1)S(1)} %collective-permute-done.1.clat_hbm.clat_ref, ...), custom_call_target="tpu_custom_call" | custom-call | flops 3000000000 | bytes 10000000 | tf_op jit(solution)/shard_map/factors/pallas_call | solution.py:406
  25.3 0.0 collective-permute-done.2.c1_any.c1_ref
  25.3 4.2 %collective-permute-done.3.c2_any.c2_ref = s16[2,112,256]{2,1,0:T(8,128)(2,1)S(1)} collective-permute-done((s16[2,112,256]{2,1,0:T(8,128)(2,1)S(1)}, s16[2,112,256]{2,1,0:T(8,128)(2,1)S(1)}, u32[]{:S(2)}, u32[]{:S(2)}) %collective-permute-start.3) | collective-permute-done | bytes 114720 | tf_op jit(solution)/shard_map/ppermute | solution.py:624
  29.5 0.0 collective-permute-done.4.c3_any.c3_ref
  29.6 2.6 %backward.1 = (bf16[512,1152]{1,0:T(8,128)(2,1)S(1)}, bf16[512,1024]{1,0:T(8,128)(2,1)S(1)}, bf16[512,128]{1,0:T(8,128)(2,1)S(1)}) custom-call(s32[2]{0:T(128)S(1)} %pad_add_fusion.where_ref, s16[2,112,256]{2,1,0:T(8,128)(2,1)S(1)} %get-tuple-element.26.c0_any.c0_ref, s16[2,112,256]{2,1,0:T(8,128)(2,1)S(1)} %collective-permute-done.2.c1_any.c1_ref, ...), custom_call_target="tpu_custom_call" | custom-call | flops 2000000000 | bytes 5000000 | tf_op jit(solution)/shard_map/backward/pallas_call | solution.py:406
  32.2 0.4 collective-permute-start.5
  32.6 0.0 copy-done.2
  32.6 1.0 %rows.1 = (bf16[2,128,1024]{2,1,0:T(8,128)(2,1)S(1)}, bf16[2,128,1024]{2,1,0:T(8,128)(2,1)S(1)}) custom-call(bf16[384,512]{1,0:T(8,128)(2,1)S(1)} %get-tuple-element.27.cft_ref.cft_hbm, bf16[512,1024]{1,0:T(8,128)(2,1)S(1)} %get-tuple-element.34.sg_ref.sg_hbm), custom_call_target="tpu_custom_call" | custom-call | flops 1000000000 | bytes 3000000 | tf_op jit(solution)/shard_map/rows/pallas_call | solution.py:406
  33.7 0.0 copy-start.10
  33.7 0.9 mine.1.mine_ref
  34.6 0.6 collective-permute-done.5.theirs_ref
  35.2 1.1 %merge.1 = bf16[512,1152]{1,0:T(8,128)(2,1)} custom-call(bf16[512,1152]{1,0:T(8,128)(2,1)S(1)} %mine.1.mine_ref, bf16[512,1152]{1,0:T(8,128)(2,1)S(1)} %collective-permute-done.5.theirs_ref, bf16[2,128,1024]{2,1,0:T(8,128)(2,1)S(1)} %get-tuple-element.40.after_any), custom_call_target="tpu_custom_call" | custom-call | flops 1000000 | bytes 4000000 | tf_op jit(solution)/shard_map/merge/pallas_call | solution.py:406
  36.3 0.0 copy-start.11
  36.3 15.1 %all-to-all-start = ((bf16[16,32,1152]{2,1,0:T(8,128)(2,1)}), bf16[16,32,1152]{2,1,0:T(8,128)(2,1)S(1)}, u32[]{:S(2)}, u32[]{:S(2)}) async-start(bf16[16,32,1152]{2,1,0:T(8,128)(2,1)} %bitcast.6), calls=%async_computation | async-start | bytes 2359296 | tf_op jit(solution)/shard_map/all_to_all | solution.py:639
  51.4 1.9 %collective-permute-start.8 = (bf16[2,128,1024]{2,1,0:T(8,128)(2,1)S(1)}, bf16[2,128,1024]{2,1,0:T(8,128)(2,1)S(1)}, u32[]{:S(2)}, u32[]{:S(2)}) collective-permute-start(bf16[2,128,1024]{2,1,0:T(8,128)(2,1)S(1)} %get-tuple-element.40.after_any), channel_id=1, source_target_pairs={{1,2},{2,1},{3,4},{4,3},{5,6},{6,5},{7,8},{8,7},{9,10},{10,9},{11,... | collective-permute-start | bytes 1572872 | tf_op jit(solution)/shard_map/ppermute | solution.py:635
  53.3 1.7 %collective-permute-start.6 = (bf16[2,128,1024]{2,1,0:T(8,128)(2,1)S(1)}, bf16[2,128,1024]{2,1,0:T(8,128)(2,1)S(1)}, u32[]{:S(2)}, u32[]{:S(2)}) collective-permute-start(bf16[2,128,1024]{2,1,0:T(8,128)(2,1)S(1)} %copy-done.11), channel_id=1, source_target_pairs={{0,1},{1,0},{2,3},{3,2},{4,5},{5,4},{6,7},{7,6},{8,9},{9,8},{10,11... | collective-permute-start | bytes 1572872 | tf_op jit(solution)/shard_map/ppermute | solution.py:641
  55.0 1.5 %collective-permute-start.7 = (bf16[2,128,1024]{2,1,0:T(8,128)(2,1)S(1)}, bf16[2,128,1024]{2,1,0:T(8,128)(2,1)}, u32[]{:S(2)}, u32[]{:S(2)}) collective-permute-start(bf16[2,128,1024]{2,1,0:T(8,128)(2,1)S(1)} %get-tuple-element.40.after_any), channel_id=1, source_target_pairs={{0,63},{31,32},{32,31},{63,0},{64,127},{95,96},{96,95},{127,64},{1... | collective-permute-start | bytes 1572872 | tf_op jit(solution)/shard_map/ppermute | solution.py:640
  56.5 18.4 %all-to-all-done.got_ref = bf16[16,32,1152]{2,1,0:T(8,128)(2,1)S(1)} async-done(((bf16[16,32,1152]{2,1,0:T(8,128)(2,1)}), bf16[16,32,1152]{2,1,0:T(8,128)(2,1)S(1)}, u32[]{:S(2)}, u32[]{:S(2)}) %all-to-all-start) | async-done | bytes 1179680 | tf_op jit(solution)/shard_map/all_to_all | solution.py:639
  74.8 0.9 plane.1
  75.8 7.7 %all-to-all-start.1 = ((bf16[8,16,1152]{2,1,0:T(8,128)(2,1)}), bf16[8,16,1152]{2,1,0:T(8,128)(2,1)S(1)}, u32[]{:S(2)}, u32[]{:S(2)}) async-start(bf16[8,16,1152]{2,1,0:T(8,128)(2,1)} %bitcast.7), calls=%async_computation.1 | async-start | bytes 589824 | tf_op jit(solution)/shard_map/all_to_all | solution.py:643
  83.5 3.8 %score.1 = f32[100,256]{1,0:T(8,128)} custom-call(s32[2]{0:T(128)} %copy-done.8, s16[2,112,256]{2,1,0:T(8,128)(2,1)} %copy-done.3, s16[2,112,256]{2,1,0:T(8,128)(2,1)} %copy-done.4, s16[2,112,256]{2,1,0:T(8,128)(2,1)} %copy-done.5, s16[2,112,256]{2,1,0:T(8,128)(2,1)} %copy-done.6, f32[100,256]{1,0:T(8,128)} %truth_ref.1), custom_call_target="tpu_custom_call" | custom-call | flops 10000000 | bytes 1000000 | tf_op jit(solution)/shard_map/score/pallas_call | solution.py:406
  87.2 0.0 collective-permute-done.8.near_any
  87.3 0.0 collective-permute-done.6.core_any
  87.3 0.0 collective-permute-done.7.far_any
  87.3 0.8 copy-done.17
  88.1 0.2 copy-done.18
  88.2 4.0 %latent.1 = bf16[2,128,1024]{2,1,0:T(8,128)(2,1)} custom-call(bf16[384,512]{1,0:T(8,128)(2,1)} %copy-done.2, bf16[512,1024]{1,0:T(8,128)(2,1)} %copy-done, bf16[1024,1024]{1,0:T(8,128)(2,1)} %w_hbm.3, bf16[2,128,1024]{2,1,0:T(8,128)(2,1)} %copy-done.18, bf16[2,128,1024]{2,1,0:T(8,128)(2,1)} %collective-permute-done.7.far_any, bf16[2,128,1024]{2,1,0:T(8,128)(2,1)} %copy-done.17), custom_call_target="tpu_custom_call" | custom-call | flops 1000000000 | bytes 5000000 | tf_op jit(solution)/shard_map/latent/pallas_call | solution.py:406
  92.2 0.0 all-to-all-done.1.got_ref
  92.2 0.7 final.1
  (26 shorter events, 0.0 us)
Async XLA Ops:
  0.6 4.1 %collective-permute-start.1 = (bf16[2,128,1024]{2,1,0:T(8,128)(2,1)}, bf16[2,128,1024]{2,1,0:T(8,128)(2,1)S(1)}, u32[]{:S(2)}, u32[]{:S(2)}) collective-permute-start(bf16[2,128,1024]{2,1,0:T(8,128)(2,1)} %lat_ref.1), channel_id=1, source_target_pairs={{0,1},{1,0},{2,3},{3,2},{4,5},{5,4},{6,7},{7,6},{8,9},{9,8},{10,11... | collective-permute-start | bytes 1572872 | tf_op jit(solution)/shard_map/ppermute | solution.py:615
  0.7 13.8 %collective-permute-start = (bf16[2,128,1024]{2,1,0:T(8,128)(2,1)}, bf16[2,128,1024]{2,1,0:T(8,128)(2,1)S(1)}, u32[]{:S(2)}, u32[]{:S(2)}) collective-permute-start(bf16[2,128,1024]{2,1,0:T(8,128)(2,1)} %lat_ref.1), channel_id=1, source_target_pairs={{0,63},{1,2},{2,1},{3,4},{4,3},{5,6},{6,5},{7,8},{8,7},{9,10},{10,... | collective-permute-start | bytes 1572872 | tf_op jit(solution)/shard_map/ppermute | solution.py:614
  4.7 24.8 %copy-start.8 = (s32[2]{0:T(128)}, s32[2]{0:T(128)S(1)}, u32[]{:S(2)}) copy-start(s32[2]{0:T(128)S(1)} %pad_add_fusion.where_ref) | copy-start | bytes 28
  4.7 9.8 %copy-start.1 = (bf16[1024,1024]{1,0:T(8,128)(2,1)S(1)}, bf16[1024,1024]{1,0:T(8,128)(2,1)}, u32[]{:S(2)}) copy-start(bf16[1024,1024]{1,0:T(8,128)(2,1)} %w_hbm.3) | copy-start | bytes 6291460
  4.7 1.2 %copy-start.9 = (bf16[2,128,1024]{2,1,0:T(8,128)(2,1)S(1)}, bf16[2,128,1024]{2,1,0:T(8,128)(2,1)}, u32[]{:S(2)}) copy-start(bf16[2,128,1024]{2,1,0:T(8,128)(2,1)} %lat_ref.1) | copy-start | bytes 1572868
  5.9 0.7 copy-start.12
  6.6 0.7 copy-start.13
  7.3 0.7 copy-start.14
  8.0 0.7 copy-start.16
  14.5 18.1 %copy-start.2 = (bf16[384,512]{1,0:T(8,128)(2,1)}, bf16[384,512]{1,0:T(8,128)(2,1)S(1)}, u32[]{:S(2)}) copy-start(bf16[384,512]{1,0:T(8,128)(2,1)S(1)} %get-tuple-element.27.cft_ref.cft_hbm) | copy-start | bytes 1179652
  17.3 12.2 %copy-start.3 = (s16[2,112,256]{2,1,0:T(8,128)(2,1)}, s16[2,112,256]{2,1,0:T(8,128)(2,1)S(1)}, u32[]{:S(2)}) copy-start(s16[2,112,256]{2,1,0:T(8,128)(2,1)S(1)} %get-tuple-element.26.c0_any.c0_ref) | copy-start | bytes 344068
  17.4 7.9 %collective-permute-start.2 = (s16[2,112,256]{2,1,0:T(8,128)(2,1)S(1)}, s16[2,112,256]{2,1,0:T(8,128)(2,1)S(1)}, u32[]{:S(2)}, u32[]{:S(2)}) collective-permute-start(s16[2,112,256]{2,1,0:T(8,128)(2,1)S(1)} %get-tuple-element.26.c0_any.c0_ref), channel_id=1, source_target_pairs={{0,64},{64,0},{128,192},{192,128},{1,65},{65,1},{129,193},{193,129... | collective-permute-start | bytes 344072 | tf_op jit(solution)/shard_map/ppermute | solution.py:624
  17.6 11.9 %collective-permute-start.3 = (s16[2,112,256]{2,1,0:T(8,128)(2,1)S(1)}, s16[2,112,256]{2,1,0:T(8,128)(2,1)S(1)}, u32[]{:S(2)}, u32[]{:S(2)}) collective-permute-start(s16[2,112,256]{2,1,0:T(8,128)(2,1)S(1)} %get-tuple-element.26.c0_any.c0_ref), channel_id=1, source_target_pairs={{0,128},{64,192},{128,0},{192,64},{1,129},{65,193},{129,1},{193,65... | collective-permute-start | bytes 344072 | tf_op jit(solution)/shard_map/ppermute | solution.py:624
  20.9 8.7 %collective-permute-start.4 = (s16[2,112,256]{2,1,0:T(8,128)(2,1)S(1)}, s16[2,112,256]{2,1,0:T(8,128)(2,1)S(1)}, u32[]{:S(2)}, u32[]{:S(2)}) collective-permute-start(s16[2,112,256]{2,1,0:T(8,128)(2,1)S(1)} %get-tuple-element.26.c0_any.c0_ref), channel_id=1, source_target_pairs={{0,192},{64,128},{128,64},{192,0},{1,193},{65,129},{129,65},{193,1... | collective-permute-start | bytes 344072 | tf_op jit(solution)/shard_map/ppermute | solution.py:624
  21.8 7.7 %copy-start.7 = (f32[100,256]{1,0:T(8,128)S(1)}, f32[100,256]{1,0:T(8,128)}, u32[]{:S(2)}) copy-start(f32[100,256]{1,0:T(8,128)} %truth_ref.1) | copy-start | bytes 307204
  21.8 7.8 %copy-start.15 = (f32[256]{0:T(256)S(1)}, f32[256]{0:T(256)}, u32[]{:S(2)}) copy-start(f32[256]{0:T(256)} %param.14) | copy-start | bytes 3076
  25.3 6.9 %copy-start.4 = (s16[2,112,256]{2,1,0:T(8,128)(2,1)}, s16[2,112,256]{2,1,0:T(8,128)(2,1)S(1)}, u32[]{:S(2)}) copy-start(s16[2,112,256]{2,1,0:T(8,128)(2,1)S(1)} %collective-permute-done.2.c1_any.c1_ref) | copy-start | bytes 344068
  29.5 2.7 %copy-start.5 = (s16[2,112,256]{2,1,0:T(8,128)(2,1)}, s16[2,112,256]{2,1,0:T(8,128)(2,1)S(1)}, u32[]{:S(2)}) copy-start(s16[2,112,256]{2,1,0:T(8,128)(2,1)S(1)} %collective-permute-done.3.c2_any.c2_ref) | copy-start | bytes 344068
  29.5 2.7 %copy-start.6 = (s16[2,112,256]{2,1,0:T(8,128)(2,1)}, s16[2,112,256]{2,1,0:T(8,128)(2,1)S(1)}, u32[]{:S(2)}) copy-start(s16[2,112,256]{2,1,0:T(8,128)(2,1)S(1)} %collective-permute-done.4.c3_any.c3_ref) | copy-start | bytes 344068
  32.2 1.4 %copy-start = (bf16[512,1024]{1,0:T(8,128)(2,1)}, bf16[512,1024]{1,0:T(8,128)(2,1)S(1)}, u32[]{:S(2)}) copy-start(bf16[512,1024]{1,0:T(8,128)(2,1)S(1)} %get-tuple-element.34.sg_ref.sg_hbm) | copy-start | bytes 3145732
  32.2 2.9 %collective-permute-start.5 = (bf16[512,1152]{1,0:T(8,128)(2,1)S(1)}, bf16[512,1152]{1,0:T(8,128)(2,1)S(1)}, u32[]{:S(2)}, u32[]{:S(2)}) collective-permute-start(bf16[512,1152]{1,0:T(8,128)(2,1)S(1)} %get-tuple-element.36), channel_id=1, source_target_pairs={{0,1},{1,0},{2,3},{3,2},{4,5},{5,4},{6,7},{7,6},{8,9},{9,8},{10,11... | collective-permute-start | bytes 3538952 | tf_op jit(solution)/shard_map/ppermute | solution.py:632
  33.7 0.9 copy-start.10
  36.3 17.0 %copy-start.11 = (bf16[2,128,1024]{2,1,0:T(8,128)(2,1)S(1)}, bf16[2,128,1024]{2,1,0:T(8,128)(2,1)}, u32[]{:S(2)}) copy-start(bf16[2,128,1024]{2,1,0:T(8,128)(2,1)} %copy-done.10) | copy-start | bytes 1572868
  36.3 38.5 %all-to-all-start = ((bf16[16,32,1152]{2,1,0:T(8,128)(2,1)}), bf16[16,32,1152]{2,1,0:T(8,128)(2,1)S(1)}, u32[]{:S(2)}, u32[]{:S(2)}) async-start(bf16[16,32,1152]{2,1,0:T(8,128)(2,1)} %bitcast.6), calls=%async_computation | async-start | bytes 2359296 | tf_op jit(solution)/shard_map/all_to_all | solution.py:639
  51.4 35.8 %collective-permute-start.8 = (bf16[2,128,1024]{2,1,0:T(8,128)(2,1)S(1)}, bf16[2,128,1024]{2,1,0:T(8,128)(2,1)S(1)}, u32[]{:S(2)}, u32[]{:S(2)}) collective-permute-start(bf16[2,128,1024]{2,1,0:T(8,128)(2,1)S(1)} %get-tuple-element.40.after_any), channel_id=1, source_target_pairs={{1,2},{2,1},{3,4},{4,3},{5,6},{6,5},{7,8},{8,7},{9,10},{10,9},{11,... | collective-permute-start | bytes 1572872 | tf_op jit(solution)/shard_map/ppermute | solution.py:635
  53.3 33.9 %collective-permute-start.6 = (bf16[2,128,1024]{2,1,0:T(8,128)(2,1)S(1)}, bf16[2,128,1024]{2,1,0:T(8,128)(2,1)S(1)}, u32[]{:S(2)}, u32[]{:S(2)}) collective-permute-start(bf16[2,128,1024]{2,1,0:T(8,128)(2,1)S(1)} %copy-done.11), channel_id=1, source_target_pairs={{0,1},{1,0},{2,3},{3,2},{4,5},{5,4},{6,7},{7,6},{8,9},{9,8},{10,11... | collective-permute-start | bytes 1572872 | tf_op jit(solution)/shard_map/ppermute | solution.py:641
  55.0 32.3 %collective-permute-start.7 = (bf16[2,128,1024]{2,1,0:T(8,128)(2,1)S(1)}, bf16[2,128,1024]{2,1,0:T(8,128)(2,1)}, u32[]{:S(2)}, u32[]{:S(2)}) collective-permute-start(bf16[2,128,1024]{2,1,0:T(8,128)(2,1)S(1)} %get-tuple-element.40.after_any), channel_id=1, source_target_pairs={{0,63},{31,32},{32,31},{63,0},{64,127},{95,96},{96,95},{127,64},{1... | collective-permute-start | bytes 1572872 | tf_op jit(solution)/shard_map/ppermute | solution.py:640
  75.8 16.5 %all-to-all-start.1 = ((bf16[8,16,1152]{2,1,0:T(8,128)(2,1)}), bf16[8,16,1152]{2,1,0:T(8,128)(2,1)S(1)}, u32[]{:S(2)}, u32[]{:S(2)}) async-start(bf16[8,16,1152]{2,1,0:T(8,128)(2,1)} %bitcast.7), calls=%async_computation.1 | async-start | bytes 589824 | tf_op jit(solution)/shard_map/all_to_all | solution.py:643
  87.2 0.8 copy-start.17
  87.3 1.0 %copy-start.18 = (bf16[2,128,1024]{2,1,0:T(8,128)(2,1)}, bf16[2,128,1024]{2,1,0:T(8,128)(2,1)S(1)}, u32[]{:S(2)}) copy-start(bf16[2,128,1024]{2,1,0:T(8,128)(2,1)S(1)} %collective-permute-done.6.core_any) | copy-start | bytes 1572868

commit v8 on v7

--- a/solution.py
+++ b/solution.py
@@ -218,7 +218,7 @@
 def decode(where_ref, code_refs, f_ref):
     local = code_refs[0].shape[0]
     rows = [
-        ref[m, VROWS - 8 :, :].astype(jnp.int32).astype(F32)[:1, :VPAD]
+        ref[m, VROWS - 16 :, :].astype(jnp.int32).astype(F32)[8:9, :VPAD]
         for ref in code_refs
         for m in range(local)
     ]

time: 93.7 us -> 93.7 us (level)
  no operation moved by 1% of the time
where the time goes in v8:
time: 93.7 us; the launch traced here: 92.9 us
  starting transfers between devices  35.1 us (37%)
  Pallas kernels  27.1 us (29%)
  waiting for transfers between devices  23.2 us (25%)
  local copies, waits for them, and re-layouts  6.5 us (7%)
    pallas_call x11, Pallas kernels, call(): pl.pallas_call(kernel, out_shape=out_shape, in_specs=in_specs, out_specs=...  27.1 us
    all_to_all x1, waiting for transfers between devices, body(): got = lax.all_to_all(part, ('x', 'y'), 0, 0, tiled=True)  18.4 us
    all_to_all x1, starting transfers between devices, body(): got = lax.all_to_all(part, ('x', 'y'), 0, 0, tiled=True)  15.1 us
    all_to_all x1, starting transfers between devices, body(): got = lax.all_to_all(plane, ('ens', 'zhi'), 0, 0, tiled=True)  7.69 us
    unnamed x38, local copies, waits for them, and re-layouts  4.89 us
    ppermute x3, starting transfers between devices, body(): lax.ppermute(coded, 'ens', [(e, e ^ k) for e in range(ens)])  4.45 us
    ppermute x3, waiting for transfers between devices, body(): lax.ppermute(coded, 'ens', [(e, e ^ k) for e in range(ens)])  4.23 us
    ppermute x1, starting transfers between devices, body(): lax.ppermute(latent, SPACE, odd_pairs).reshape(local * rows, depth)  2.28 us
  transfers between devices with their start and end apart: 11, of which 3 were waited for; matrix products, arithmetic and copies ran while one was open for 2% of the time, Pallas kernels for 21%

profile of v8, /device:TPU:8, one launch (start us, length us, event | category | flops | bytes accessed | tf_op | source)
XLA Modules:
  0.0 92.9 jit_solution(601643847926481005)
XLA Ops:
  0.6 0.1 collective-permute-start.1
  0.7 2.3 %collective-permute-start = (bf16[2,128,1024]{2,1,0:T(8,128)(2,1)}, bf16[2,128,1024]{2,1,0:T(8,128)(2,1)S(1)}, u32[]{:S(2)}, u32[]{:S(2)}) collective-permute-start(bf16[2,128,1024]{2,1,0:T(8,128)(2,1)} %lat_ref.1), channel_id=1, source_target_pairs={{0,63},{1,2},{2,1},{3,4},{4,3},{5,6},{6,5},{7,8},{8,7},{9,10},{10,... | collective-permute-start | bytes 1572872 | tf_op jit(solution)/shard_map/ppermute | solution.py:614
  3.0 1.0 %pad.8.dpt_ref = bf16[128,1024]{1,0:T(8,128)(2,1)S(1)} pad(bf16[100,1024]{1,0:T(8,128)(2,1)} %bitcast.12, bf16[]{:T(256)} %constant.13.clone.1), padding=0_28x0_0 | pad | bytes 466946 | tf_op jit(solution)/shard_map/jit(_pad)/pad | solution.py:616
  4.0 0.7 pad_bitcast_fusion.var_ref
  4.6 0.1 pad_add_fusion.where_ref
  4.7 0.0 collective-permute-done.1.clat_hbm.clat_ref
  4.7 1.2 %copy-done.9 = bf16[2,128,1024]{2,1,0:T(8,128)(2,1)S(1)} copy-done((bf16[2,128,1024]{2,1,0:T(8,128)(2,1)S(1)}, bf16[2,128,1024]{2,1,0:T(8,128)(2,1)}, u32[]{:S(2)}) %copy-start.9) | copy-done | bytes 524312
  5.9 0.7 copy-done.12
  6.6 0.7 copy-done.13
  7.3 0.7 copy-done.14
  8.0 0.7 copy-done.16
  8.6 5.9 %prepare.1 = (bf16[256,768]{1,0:T(8,128)(2,1)S(1)}, bf16[384,512]{1,0:T(8,128)(2,1)S(1)}, bf16[256,256]{1,0:T(8,128)(2,1)S(1)}, f32[2,256,1024]{2,1,0:T(8,128)S(1)}) custom-call(s32[2]{0:T(128)S(1)} %pad_add_fusion.where_ref, s32[2]{0:T(128)S(1)} %copy-done.16, s32[2,512]{1,0:T(2,128)S(1)} %copy-done.12, s32[2,512]{1,0:T(2,128)S(1)} %copy-done.13, ...), custom_call_target="tpu_custom_call" | custom-call | flops 3000000000 | bytes 6000000 | tf_op jit(solution)/shard_map/prepare/pallas_call | solution.py:406
  14.5 0.0 copy-start.2
  14.5 0.0 collective-permute-done
  14.6 0.0 copy-done.1
  14.6 2.8 %forward.1 = (f32[2,256,1024]{2,1,0:T(8,128)S(1)}, bf16[2,256,1024]{2,1,0:T(8,128)(2,1)S(1)}, s16[2,112,256]{2,1,0:T(8,128)(2,1)S(1)}) custom-call(bf16[256,1024]{1,0:T(8,128)(2,1)S(1)} %bitcast.9, bf16[1024,1024]{1,0:T(8,128)(2,1)S(1)} %copy-done.1, bf16[256,256]{1,0:T(8,128)(2,1)S(1)} %get-tuple-element.24.cfo_ref, ...), custom_call_target="tpu_custom_call" | custom-call | flops 2000000000 | bytes 8000000 | tf_op jit(solution)/shard_map/forward/pallas_call | solution.py:406
  17.4 0.2 collective-permute-start.2
  17.6 3.3 %collective-permute-start.3 = (s16[2,112,256]{2,1,0:T(8,128)(2,1)S(1)}, s16[2,112,256]{2,1,0:T(8,128)(2,1)S(1)}, u32[]{:S(2)}, u32[]{:S(2)}) collective-permute-start(s16[2,112,256]{2,1,0:T(8,128)(2,1)S(1)} %get-tuple-element.26.c0_any.c0_ref), channel_id=1, source_target_pairs={{0,128},{64,192},{128,0},{192,64},{1,129},{65,193},{129,1},{193,65... | collective-permute-start | bytes 344072 | tf_op jit(solution)/shard_map/ppermute | solution.py:624
  20.9 0.9 %collective-permute-start.4 = (s16[2,112,256]{2,1,0:T(8,128)(2,1)S(1)}, s16[2,112,256]{2,1,0:T(8,128)(2,1)S(1)}, u32[]{:S(2)}, u32[]{:S(2)}) collective-permute-start(s16[2,112,256]{2,1,0:T(8,128)(2,1)S(1)} %get-tuple-element.26.c0_any.c0_ref), channel_id=1, source_target_pairs={{0,192},{64,128},{128,64},{192,0},{1,193},{65,129},{129,65},{193,1... | collective-permute-start | bytes 344072 | tf_op jit(solution)/shard_map/ppermute | solution.py:624
  21.8 3.5 %factors.1 = (bf16[1024,512]{1,0:T(8,128)(2,1)S(1)}, bf16[1024,512]{1,0:T(8,128)(2,1)S(1)}, f32[2,256,1024]{2,1,0:T(8,128)S(1)}) custom-call(s32[2]{0:T(128)S(1)} %pad_add_fusion.where_ref, bf16[2,128,1024]{2,1,0:T(8,128)(2,1)S(1)} %copy-done.9, bf16[2,128,1024]{2,1,0:T(8,128)(2,1)S(1)} %collective-permute-done.1.clat_hbm.clat_ref, ...), custom_call_target="tpu_custom_call" | custom-call | flops 3000000000 | bytes 10000000 | tf_op jit(solution)/shard_map/factors/pallas_call | solution.py:406
  25.3 0.0 collective-permute-done.2.c1_any.c1_ref
  25.3 4.2 %collective-permute-done.3.c2_any.c2_ref = s16[2,112,256]{2,1,0:T(8,128)(2,1)S(1)} collective-permute-done((s16[2,112,256]{2,1,0:T(8,128)(2,1)S(1)}, s16[2,112,256]{2,1,0:T(8,128)(2,1)S(1)}, u32[]{:S(2)}, u32[]{:S(2)}) %collective-permute-start.3) | collective-permute-done | bytes 114720 | tf_op jit(solution)/shard_map/ppermute | solution.py:624
  29.5 0.0 collective-permute-done.4.c3_any.c3_ref
  29.6 2.6 %backward.1 = (bf16[512,1152]{1,0:T(8,128)(2,1)S(1)}, bf16[512,1024]{1,0:T(8,128)(2,1)S(1)}, bf16[512,128]{1,0:T(8,128)(2,1)S(1)}) custom-call(s32[2]{0:T(128)S(1)} %pad_add_fusion.where_ref, s16[2,112,256]{2,1,0:T(8,128)(2,1)S(1)} %get-tuple-element.26.c0_any.c0_ref, s16[2,112,256]{2,1,0:T(8,128)(2,1)S(1)} %collective-permute-done.2.c1_any.c1_ref, ...), custom_call_target="tpu_custom_call" | custom-call | flops 2000000000 | bytes 5000000 | tf_op jit(solution)/shard_map/backward/pallas_call | solution.py:406
  32.2 0.4 collective-permute-start.5
  32.6 0.0 copy-done.2
  32.6 1.0 %rows.1 = (bf16[2,128,1024]{2,1,0:T(8,128)(2,1)S(1)}, bf16[2,128,1024]{2,1,0:T(8,128)(2,1)S(1)}) custom-call(bf16[384,512]{1,0:T(8,128)(2,1)S(1)} %get-tuple-element.27.cft_ref.cft_hbm, bf16[512,1024]{1,0:T(8,128)(2,1)S(1)} %get-tuple-element.34.sg_ref.sg_hbm), custom_call_target="tpu_custom_call" | custom-call | flops 1000000000 | bytes 3000000 | tf_op jit(solution)/shard_map/rows/pallas_call | solution.py:406
  33.7 0.0 copy-start.10
  33.7 0.9 mine.1.mine_ref
  34.6 0.6 collective-permute-done.5.theirs_ref
  35.2 1.1 %merge.1 = bf16[512,1152]{1,0:T(8,128)(2,1)} custom-call(bf16[512,1152]{1,0:T(8,128)(2,1)S(1)} %mine.1.mine_ref, bf16[512,1152]{1,0:T(8,128)(2,1)S(1)} %collective-permute-done.5.theirs_ref, bf16[2,128,1024]{2,1,0:T(8,128)(2,1)S(1)} %get-tuple-element.40.after_any), custom_call_target="tpu_custom_call" | custom-call | flops 1000000 | bytes 4000000 | tf_op jit(solution)/shard_map/merge/pallas_call | solution.py:406
  36.3 0.0 copy-start.11
  36.3 15.1 %all-to-all-start = ((bf16[16,32,1152]{2,1,0:T(8,128)(2,1)}), bf16[16,32,1152]{2,1,0:T(8,128)(2,1)S(1)}, u32[]{:S(2)}, u32[]{:S(2)}) async-start(bf16[16,32,1152]{2,1,0:T(8,128)(2,1)} %bitcast.6), calls=%async_computation | async-start | bytes 2359296 | tf_op jit(solution)/shard_map/all_to_all | solution.py:639
  51.4 1.9 %collective-permute-start.8 = (bf16[2,128,1024]{2,1,0:T(8,128)(2,1)S(1)}, bf16[2,128,1024]{2,1,0:T(8,128)(2,1)S(1)}, u32[]{:S(2)}, u32[]{:S(2)}) collective-permute-start(bf16[2,128,1024]{2,1,0:T(8,128)(2,1)S(1)} %get-tuple-element.40.after_any), channel_id=1, source_target_pairs={{1,2},{2,1},{3,4},{4,3},{5,6},{6,5},{7,8},{8,7},{9,10},{10,9},{11,... | collective-permute-start | bytes 1572872 | tf_op jit(solution)/shard_map/ppermute | solution.py:635
  53.3 1.7 %collective-permute-start.6 = (bf16[2,128,1024]{2,1,0:T(8,128)(2,1)S(1)}, bf16[2,128,1024]{2,1,0:T(8,128)(2,1)S(1)}, u32[]{:S(2)}, u32[]{:S(2)}) collective-permute-start(bf16[2,128,1024]{2,1,0:T(8,128)(2,1)S(1)} %copy-done.11), channel_id=1, source_target_pairs={{0,1},{1,0},{2,3},{3,2},{4,5},{5,4},{6,7},{7,6},{8,9},{9,8},{10,11... | collective-permute-start | bytes 1572872 | tf_op jit(solution)/shard_map/ppermute | solution.py:641
  55.0 1.5 %collective-permute-start.7 = (bf16[2,128,1024]{2,1,0:T(8,128)(2,1)S(1)}, bf16[2,128,1024]{2,1,0:T(8,128)(2,1)}, u32[]{:S(2)}, u32[]{:S(2)}) collective-permute-start(bf16[2,128,1024]{2,1,0:T(8,128)(2,1)S(1)} %get-tuple-element.40.after_any), channel_id=1, source_target_pairs={{0,63},{31,32},{32,31},{63,0},{64,127},{95,96},{96,95},{127,64},{1... | collective-permute-start | bytes 1572872 | tf_op jit(solution)/shard_map/ppermute | solution.py:640
  56.5 18.4 %all-to-all-done.got_ref = bf16[16,32,1152]{2,1,0:T(8,128)(2,1)S(1)} async-done(((bf16[16,32,1152]{2,1,0:T(8,128)(2,1)}), bf16[16,32,1152]{2,1,0:T(8,128)(2,1)S(1)}, u32[]{:S(2)}, u32[]{:S(2)}) %all-to-all-start) | async-done | bytes 1179680 | tf_op jit(solution)/shard_map/all_to_all | solution.py:639
  74.8 0.9 plane.1
  75.8 7.7 %all-to-all-start.1 = ((bf16[8,16,1152]{2,1,0:T(8,128)(2,1)}), bf16[8,16,1152]{2,1,0:T(8,128)(2,1)S(1)}, u32[]{:S(2)}, u32[]{:S(2)}) async-start(bf16[8,16,1152]{2,1,0:T(8,128)(2,1)} %bitcast.7), calls=%async_computation.1 | async-start | bytes 589824 | tf_op jit(solution)/shard_map/all_to_all | solution.py:643
  83.5 3.8 %score.1 = f32[100,256]{1,0:T(8,128)} custom-call(s32[2]{0:T(128)} %copy-done.8, s16[2,112,256]{2,1,0:T(8,128)(2,1)} %copy-done.3, s16[2,112,256]{2,1,0:T(8,128)(2,1)} %copy-done.4, s16[2,112,256]{2,1,0:T(8,128)(2,1)} %copy-done.5, s16[2,112,256]{2,1,0:T(8,128)(2,1)} %copy-done.6, f32[100,256]{1,0:T(8,128)} %truth_ref.1), custom_call_target="tpu_custom_call" | custom-call | flops 10000000 | bytes 1000000 | tf_op jit(solution)/shard_map/score/pallas_call | solution.py:406
  87.2 0.0 collective-permute-done.8.near_any
  87.3 0.0 collective-permute-done.6.core_any
  87.3 0.0 collective-permute-done.7.far_any
  87.3 0.8 copy-done.17
  88.1 0.2 copy-done.18
  88.2 4.0 %latent.1 = bf16[2,128,1024]{2,1,0:T(8,128)(2,1)} custom-call(bf16[384,512]{1,0:T(8,128)(2,1)} %copy-done.2, bf16[512,1024]{1,0:T(8,128)(2,1)} %copy-done, bf16[1024,1024]{1,0:T(8,128)(2,1)} %w_hbm.3, bf16[2,128,1024]{2,1,0:T(8,128)(2,1)} %copy-done.18, bf16[2,128,1024]{2,1,0:T(8,128)(2,1)} %collective-permute-done.7.far_any, bf16[2,128,1024]{2,1,0:T(8,128)(2,1)} %copy-done.17), custom_call_target="tpu_custom_call" | custom-call | flops 1000000000 | bytes 5000000 | tf_op jit(solution)/shard_map/latent/pallas_call | solution.py:406
  92.2 0.0 all-to-all-done.1.got_ref
  92.2 0.7 final.1
  (26 shorter events, 0.0 us)
Async XLA Ops:
  0.6 4.1 %collective-permute-start.1 = (bf16[2,128,1024]{2,1,0:T(8,128)(2,1)}, bf16[2,128,1024]{2,1,0:T(8,128)(2,1)S(1)}, u32[]{:S(2)}, u32[]{:S(2)}) collective-permute-start(bf16[2,128,1024]{2,1,0:T(8,128)(2,1)} %lat_ref.1), channel_id=1, source_target_pairs={{0,1},{1,0},{2,3},{3,2},{4,5},{5,4},{6,7},{7,6},{8,9},{9,8},{10,11... | collective-permute-start | bytes 1572872 | tf_op jit(solution)/shard_map/ppermute | solution.py:615
  0.7 13.8 %collective-permute-start = (bf16[2,128,1024]{2,1,0:T(8,128)(2,1)}, bf16[2,128,1024]{2,1,0:T(8,128)(2,1)S(1)}, u32[]{:S(2)}, u32[]{:S(2)}) collective-permute-start(bf16[2,128,1024]{2,1,0:T(8,128)(2,1)} %lat_ref.1), channel_id=1, source_target_pairs={{0,63},{1,2},{2,1},{3,4},{4,3},{5,6},{6,5},{7,8},{8,7},{9,10},{10,... | collective-permute-start | bytes 1572872 | tf_op jit(solution)/shard_map/ppermute | solution.py:614
  4.7 24.8 %copy-start.8 = (s32[2]{0:T(128)}, s32[2]{0:T(128)S(1)}, u32[]{:S(2)}) copy-start(s32[2]{0:T(128)S(1)} %pad_add_fusion.where_ref) | copy-start | bytes 28
  4.7 9.8 %copy-start.1 = (bf16[1024,1024]{1,0:T(8,128)(2,1)S(1)}, bf16[1024,1024]{1,0:T(8,128)(2,1)}, u32[]{:S(2)}) copy-start(bf16[1024,1024]{1,0:T(8,128)(2,1)} %w_hbm.3) | copy-start | bytes 6291460
  4.7 1.2 %copy-start.9 = (bf16[2,128,1024]{2,1,0:T(8,128)(2,1)S(1)}, bf16[2,128,1024]{2,1,0:T(8,128)(2,1)}, u32[]{:S(2)}) copy-start(bf16[2,128,1024]{2,1,0:T(8,128)(2,1)} %lat_ref.1) | copy-start | bytes 1572868
  5.9 0.7 copy-start.12
  6.6 0.7 copy-start.13
  7.3 0.7 copy-start.14
  8.0 0.7 copy-start.16
  14.5 18.1 %copy-start.2 = (bf16[384,512]{1,0:T(8,128)(2,1)}, bf16[384,512]{1,0:T(8,128)(2,1)S(1)}, u32[]{:S(2)}) copy-start(bf16[384,512]{1,0:T(8,128)(2,1)S(1)} %get-tuple-element.27.cft_ref.cft_hbm) | copy-start | bytes 1179652
  17.3 12.2 %copy-start.3 = (s16[2,112,256]{2,1,0:T(8,128)(2,1)}, s16[2,112,256]{2,1,0:T(8,128)(2,1)S(1)}, u32[]{:S(2)}) copy-start(s16[2,112,256]{2,1,0:T(8,128)(2,1)S(1)} %get-tuple-element.26.c0_any.c0_ref) | copy-start | bytes 344068
  17.4 7.9 %collective-permute-start.2 = (s16[2,112,256]{2,1,0:T(8,128)(2,1)S(1)}, s16[2,112,256]{2,1,0:T(8,128)(2,1)S(1)}, u32[]{:S(2)}, u32[]{:S(2)}) collective-permute-start(s16[2,112,256]{2,1,0:T(8,128)(2,1)S(1)} %get-tuple-element.26.c0_any.c0_ref), channel_id=1, source_target_pairs={{0,64},{64,0},{128,192},{192,128},{1,65},{65,1},{129,193},{193,129... | collective-permute-start | bytes 344072 | tf_op jit(solution)/shard_map/ppermute | solution.py:624
  17.6 11.9 %collective-permute-start.3 = (s16[2,112,256]{2,1,0:T(8,128)(2,1)S(1)}, s16[2,112,256]{2,1,0:T(8,128)(2,1)S(1)}, u32[]{:S(2)}, u32[]{:S(2)}) collective-permute-start(s16[2,112,256]{2,1,0:T(8,128)(2,1)S(1)} %get-tuple-element.26.c0_any.c0_ref), channel_id=1, source_target_pairs={{0,128},{64,192},{128,0},{192,64},{1,129},{65,193},{129,1},{193,65... | collective-permute-start | bytes 344072 | tf_op jit(solution)/shard_map/ppermute | solution.py:624
  20.9 8.7 %collective-permute-start.4 = (s16[2,112,256]{2,1,0:T(8,128)(2,1)S(1)}, s16[2,112,256]{2,1,0:T(8,128)(2,1)S(1)}, u32[]{:S(2)}, u32[]{:S(2)}) collective-permute-start(s16[2,112,256]{2,1,0:T(8,128)(2,1)S(1)} %get-tuple-element.26.c0_any.c0_ref), channel_id=1, source_target_pairs={{0,192},{64,128},{128,64},{192,0},{1,193},{65,129},{129,65},{193,1... | collective-permute-start | bytes 344072 | tf_op jit(solution)/shard_map/ppermute | solution.py:624
  21.8 7.7 %copy-start.7 = (f32[100,256]{1,0:T(8,128)S(1)}, f32[100,256]{1,0:T(8,128)}, u32[]{:S(2)}) copy-start(f32[100,256]{1,0:T(8,128)} %truth_ref.1) | copy-start | bytes 307204
  21.8 7.8 %copy-start.15 = (f32[256]{0:T(256)S(1)}, f32[256]{0:T(256)}, u32[]{:S(2)}) copy-start(f32[256]{0:T(256)} %param.14) | copy-start | bytes 3076
  25.3 6.9 %copy-start.4 = (s16[2,112,256]{2,1,0:T(8,128)(2,1)}, s16[2,112,256]{2,1,0:T(8,128)(2,1)S(1)}, u32[]{:S(2)}) copy-start(s16[2,112,256]{2,1,0:T(8,128)(2,1)S(1)} %collective-permute-done.2.c1_any.c1_ref) | copy-start | bytes 344068
  29.5 2.7 %copy-start.5 = (s16[2,112,256]{2,1,0:T(8,128)(2,1)}, s16[2,112,256]{2,1,0:T(8,128)(2,1)S(1)}, u32[]{:S(2)}) copy-start(s16[2,112,256]{2,1,0:T(8,128)(2,1)S(1)} %collective-permute-done.3.c2_any.c2_ref) | copy-start | bytes 344068
  29.5 2.7 %copy-start.6 = (s16[2,112,256]{2,1,0:T(8,128)(2,1)}, s16[2,112,256]{2,1,0:T(8,128)(2,1)S(1)}, u32[]{:S(2)}) copy-start(s16[2,112,256]{2,1,0:T(8,128)(2,1)S(1)} %collective-permute-done.4.c3_any.c3_ref) | copy-start | bytes 344068
  32.2 1.4 %copy-start = (bf16[512,1024]{1,0:T(8,128)(2,1)}, bf16[512,1024]{1,0:T(8,128)(2,1)S(1)}, u32[]{:S(2)}) copy-start(bf16[512,1024]{1,0:T(8,128)(2,1)S(1)} %get-tuple-element.34.sg_ref.sg_hbm) | copy-start | bytes 3145732
  32.2 2.9 %collective-permute-start.5 = (bf16[512,1152]{1,0:T(8,128)(2,1)S(1)}, bf16[512,1152]{1,0:T(8,128)(2,1)S(1)}, u32[]{:S(2)}, u32[]{:S(2)}) collective-permute-start(bf16[512,1152]{1,0:T(8,128)(2,1)S(1)} %get-tuple-element.36), channel_id=1, source_target_pairs={{0,1},{1,0},{2,3},{3,2},{4,5},{5,4},{6,7},{7,6},{8,9},{9,8},{10,11... | collective-permute-start | bytes 3538952 | tf_op jit(solution)/shard_map/ppermute | solution.py:632
  33.7 0.9 copy-start.10
  36.3 17.0 %copy-start.11 = (bf16[2,128,1024]{2,1,0:T(8,128)(2,1)S(1)}, bf16[2,128,1024]{2,1,0:T(8,128)(2,1)}, u32[]{:S(2)}) copy-start(bf16[2,128,1024]{2,1,0:T(8,128)(2,1)} %copy-done.10) | copy-start | bytes 1572868
  36.3 38.5 %all-to-all-start = ((bf16[16,32,1152]{2,1,0:T(8,128)(2,1)}), bf16[16,32,1152]{2,1,0:T(8,128)(2,1)S(1)}, u32[]{:S(2)}, u32[]{:S(2)}) async-start(bf16[16,32,1152]{2,1,0:T(8,128)(2,1)} %bitcast.6), calls=%async_computation | async-start | bytes 2359296 | tf_op jit(solution)/shard_map/all_to_all | solution.py:639
  51.4 35.8 %collective-permute-start.8 = (bf16[2,128,1024]{2,1,0:T(8,128)(2,1)S(1)}, bf16[2,128,1024]{2,1,0:T(8,128)(2,1)S(1)}, u32[]{:S(2)}, u32[]{:S(2)}) collective-permute-start(bf16[2,128,1024]{2,1,0:T(8,128)(2,1)S(1)} %get-tuple-element.40.after_any), channel_id=1, source_target_pairs={{1,2},{2,1},{3,4},{4,3},{5,6},{6,5},{7,8},{8,7},{9,10},{10,9},{11,... | collective-permute-start | bytes 1572872 | tf_op jit(solution)/shard_map/ppermute | solution.py:635
  53.3 33.9 %collective-permute-start.6 = (bf16[2,128,1024]{2,1,0:T(8,128)(2,1)S(1)}, bf16[2,128,1024]{2,1,0:T(8,128)(2,1)S(1)}, u32[]{:S(2)}, u32[]{:S(2)}) collective-permute-start(bf16[2,128,1024]{2,1,0:T(8,128)(2,1)S(1)} %copy-done.11), channel_id=1, source_target_pairs={{0,1},{1,0},{2,3},{3,2},{4,5},{5,4},{6,7},{7,6},{8,9},{9,8},{10,11... | collective-permute-start | bytes 1572872 | tf_op jit(solution)/shard_map/ppermute | solution.py:641
  55.0 32.3 %collective-permute-start.7 = (bf16[2,128,1024]{2,1,0:T(8,128)(2,1)S(1)}, bf16[2,128,1024]{2,1,0:T(8,128)(2,1)}, u32[]{:S(2)}, u32[]{:S(2)}) collective-permute-start(bf16[2,128,1024]{2,1,0:T(8,128)(2,1)S(1)} %get-tuple-element.40.after_any), channel_id=1, source_target_pairs={{0,63},{31,32},{32,31},{63,0},{64,127},{95,96},{96,95},{127,64},{1... | collective-permute-start | bytes 1572872 | tf_op jit(solution)/shard_map/ppermute | solution.py:640
  75.8 16.5 %all-to-all-start.1 = ((bf16[8,16,1152]{2,1,0:T(8,128)(2,1)}), bf16[8,16,1152]{2,1,0:T(8,128)(2,1)S(1)}, u32[]{:S(2)}, u32[]{:S(2)}) async-start(bf16[8,16,1152]{2,1,0:T(8,128)(2,1)} %bitcast.7), calls=%async_computation.1 | async-start | bytes 589824 | tf_op jit(solution)/shard_map/all_to_all | solution.py:643
  87.2 0.8 copy-start.17
  87.3 1.0 %copy-start.18 = (bf16[2,128,1024]{2,1,0:T(8,128)(2,1)}, bf16[2,128,1024]{2,1,0:T(8,128)(2,1)S(1)}, u32[]{:S(2)}) copy-start(bf16[2,128,1024]{2,1,0:T(8,128)(2,1)S(1)} %collective-permute-done.6.core_any) | copy-start | bytes 1572868

commit v9 on v8

--- a/solution.py
+++ b/solution.py
@@ -225,7 +225,7 @@
     rows.append(jnp.zeros((VPAD - len(rows), VPAD), F32))
     power = (jnp.exp2(jnp.concatenate(rows, axis=0)) * (1.0 / QMAX)).T
     for k, ref in enumerate(code_refs):
-        first = lax.bitwise_xor(where_ref[1], k) * local
+        first = lax.rem(where_ref[1] + k, len(code_refs)) * local
         for m in range(local):
             code = ref[m].astype(jnp.int32).astype(F32)[:VUSE]
             at = k * local + m
@@ -621,7 +621,8 @@
         area_row = area_weight.reshape(1, points)
         summed, hidden, coded = call_forward(odd_lat, src_weight, cfo, part, dpt)
         codes = [coded] + [
-            lax.ppermute(coded, "ens", [(e, e ^ k) for e in range(ens)]) for k in range(1, ens)
+            lax.ppermute(coded, "ens", [((e + k) % ens, e) for e in range(ens)])
+            for k in range(1, ens)
         ]
         aggt, hidt, slope = call_factors(
             where, latent, core_lat, odd_lat, cf, summed, hidden

time: 93.7 us -> 91.4 us (0.975)
  starting transfers between devices: 35.1 us -> 29.4 us
  waiting for transfers between devices: 23.2 us -> 26.8 us
    all_to_all x1, starting transfers between devices: 15.1 us -> 11 us  [body(): got = lax.all_to_all(part, ('x', 'y'), 0, 0, tiled=True)]
    ppermute x3, waiting for transfers between devices: 4.23 us -> 7.3 us  [body(): lax.ppermute(coded, 'ens', [((e + k) % ens, e) for e in range(ens)])]
  transfers between devices with their start and end apart: 11 -> 11, of which waited for: 3 -> 4; matrix products, arithmetic and copies ran while one was open for 2% -> 2% of each run, Pallas kernels for 21% -> 22%
where the time goes in v9:
time: 91.4 us; the launch traced here: 90.6 us
  starting transfers between devices  29.4 us (32%)
  Pallas kernels  26.9 us (29%)
  waiting for transfers between devices  26.8 us (29%)
  local copies, waits for them, and re-layouts  6.5 us (7%)
  between operations  0.92 us (1%)
    pallas_call x11, Pallas kernels, call(): pl.pallas_call(kernel, out_shape=out_shape, in_specs=in_specs, out_specs=...  26.9 us
    all_to_all x1, waiting for transfers between devices, body(): got = lax.all_to_all(part, ('x', 'y'), 0, 0, tiled=True)  18.4 us
    all_to_all x1, starting transfers between devices, body(): got = lax.all_to_all(part, ('x', 'y'), 0, 0, tiled=True)  11 us
    ppermute x3, waiting for transfers between devices, body(): lax.ppermute(coded, 'ens', [((e + k) % ens, e) for e in range(ens)])  7.3 us
    all_to_all x1, starting transfers between devices, body(): got = lax.all_to_all(plane, ('ens', 'zhi'), 0, 0, tiled=True)  7.18 us
    unnamed x38, local copies, waits for them, and re-layouts  4.89 us
    ppermute x3, starting transfers between devices, body(): lax.ppermute(coded, 'ens', [((e + k) % ens, e) for e in range(ens)])  3.62 us
    ppermute x1, starting transfers between devices, body(): lax.ppermute(latent, SPACE, odd_pairs).reshape(local * rows, depth)  2.28 us
  transfers between devices with their start and end apart: 11, of which 4 were waited for; matrix products, arithmetic and copies ran while one was open for 2% of the time, Pallas kernels for 22%

profile of v9, /device:TPU:8, one launch (start us, length us, event | category | flops | bytes accessed | tf_op | source)
XLA Modules:
  0.0 90.6 jit_solution(11520841362096194718)
XLA Ops:
  0.6 0.1 collective-permute-start.1
  0.7 2.3 %collective-permute-start = (bf16[2,128,1024]{2,1,0:T(8,128)(2,1)}, bf16[2,128,1024]{2,1,0:T(8,128)(2,1)S(1)}, u32[]{:S(2)}, u32[]{:S(2)}) collective-permute-start(bf16[2,128,1024]{2,1,0:T(8,128)(2,1)} %lat_ref.1), channel_id=1, source_target_pairs={{0,63},{1,2},{2,1},{3,4},{4,3},{5,6},{6,5},{7,8},{8,7},{9,10},{10,... | collective-permute-start | bytes 1572872 | tf_op jit(solution)/shard_map/ppermute | solution.py:614
  3.0 1.0 %pad.8.dpt_ref = bf16[128,1024]{1,0:T(8,128)(2,1)S(1)} pad(bf16[100,1024]{1,0:T(8,128)(2,1)} %bitcast.12, bf16[]{:T(256)} %constant.13.clone.1), padding=0_28x0_0 | pad | bytes 466946 | tf_op jit(solution)/shard_map/jit(_pad)/pad | solution.py:616
  4.0 0.7 pad_bitcast_fusion.var_ref
  4.6 0.1 pad_add_fusion.where_ref
  4.7 0.0 collective-permute-done.1.clat_hbm.clat_ref
  4.7 1.2 %copy-done.9 = bf16[2,128,1024]{2,1,0:T(8,128)(2,1)S(1)} copy-done((bf16[2,128,1024]{2,1,0:T(8,128)(2,1)S(1)}, bf16[2,128,1024]{2,1,0:T(8,128)(2,1)}, u32[]{:S(2)}) %copy-start.9) | copy-done | bytes 524312
  5.9 0.7 copy-done.12
  6.6 0.7 copy-done.13
  7.3 0.7 copy-done.14
  8.0 0.7 copy-done.16
  8.6 5.9 %prepare.1 = (bf16[256,768]{1,0:T(8,128)(2,1)S(1)}, bf16[384,512]{1,0:T(8,128)(2,1)S(1)}, bf16[256,256]{1,0:T(8,128)(2,1)S(1)}, f32[2,256,1024]{2,1,0:T(8,128)S(1)}) custom-call(s32[2]{0:T(128)S(1)} %pad_add_fusion.where_ref, s32[2]{0:T(128)S(1)} %copy-done.16, s32[2,512]{1,0:T(2,128)S(1)} %copy-done.12, s32[2,512]{1,0:T(2,128)S(1)} %copy-done.13, ...), custom_call_target="tpu_custom_call" | custom-call | flops 3000000000 | bytes 6000000 | tf_op jit(solution)/shard_map/prepare/pallas_call | solution.py:406
  14.5 0.0 collective-permute-done
  14.6 2.8 %forward.1 = (f32[2,256,1024]{2,1,0:T(8,128)S(1)}, bf16[2,256,1024]{2,1,0:T(8,128)(2,1)S(1)}, s16[2,112,256]{2,1,0:T(8,128)(2,1)S(1)}) custom-call(bf16[256,1024]{1,0:T(8,128)(2,1)S(1)} %bitcast.9, bf16[1024,1024]{1,0:T(8,128)(2,1)S(1)} %copy-done.1, bf16[256,256]{1,0:T(8,128)(2,1)S(1)} %get-tuple-element.24.cfo_ref, ...), custom_call_target="tpu_custom_call" | custom-call | flops 2000000000 | bytes 8000000 | tf_op jit(solution)/shard_map/forward/pallas_call | solution.py:406
  17.4 2.9 %collective-permute-start.2 = (s16[2,112,256]{2,1,0:T(8,128)(2,1)S(1)}, s16[2,112,256]{2,1,0:T(8,128)(2,1)S(1)}, u32[]{:S(2)}, u32[]{:S(2)}) collective-permute-start(s16[2,112,256]{2,1,0:T(8,128)(2,1)S(1)} %get-tuple-element.26.c0_any.c0_ref), channel_id=1, source_target_pairs={{64,0},{128,64},{192,128},{0,192},{65,1},{129,65},{193,129},{1,193... | collective-permute-start | bytes 344072 | tf_op jit(solution)/shard_map/ppermute | solution.py:624
  20.3 0.0 collective-permute-start.3
  20.3 0.7 collective-permute-start.4
  21.0 3.5 %factors.1 = (bf16[1024,512]{1,0:T(8,128)(2,1)S(1)}, bf16[1024,512]{1,0:T(8,128)(2,1)S(1)}, f32[2,256,1024]{2,1,0:T(8,128)S(1)}) custom-call(s32[2]{0:T(128)S(1)} %pad_add_fusion.where_ref, bf16[2,128,1024]{2,1,0:T(8,128)(2,1)S(1)} %copy-done.9, bf16[2,128,1024]{2,1,0:T(8,128)(2,1)S(1)} %collective-permute-done.1.clat_hbm.clat_ref, ...), custom_call_target="tpu_custom_call" | custom-call | flops 3000000000 | bytes 10000000 | tf_op jit(solution)/shard_map/factors/pallas_call | solution.py:406
  24.4 0.0 collective-permute-done.2.c1_any.c1_ref
  24.5 7.3 %collective-permute-done.3.c2_any.c2_ref = s16[2,112,256]{2,1,0:T(8,128)(2,1)S(1)} collective-permute-done((s16[2,112,256]{2,1,0:T(8,128)(2,1)S(1)}, s16[2,112,256]{2,1,0:T(8,128)(2,1)S(1)}, u32[]{:S(2)}, u32[]{:S(2)}) %collective-permute-start.3) | collective-permute-done | bytes 114720 | tf_op jit(solution)/shard_map/ppermute | solution.py:624
  31.8 0.0 collective-permute-done.4.c3_any.c3_ref
  31.8 0.0 copy-done.3
  31.8 0.0 copy-done.7
  31.8 0.0 copy-done.15
  31.8 2.6 %backward.1 = (bf16[512,1152]{1,0:T(8,128)(2,1)S(1)}, bf16[512,1024]{1,0:T(8,128)(2,1)S(1)}, bf16[512,128]{1,0:T(8,128)(2,1)S(1)}) custom-call(s32[2]{0:T(128)S(1)} %pad_add_fusion.where_ref, s16[2,112,256]{2,1,0:T(8,128)(2,1)S(1)} %get-tuple-element.26.c0_any.c0_ref, s16[2,112,256]{2,1,0:T(8,128)(2,1)S(1)} %collective-permute-done.2.c1_any.c1_ref, ...), custom_call_target="tpu_custom_call" | custom-call | flops 2000000000 | bytes 5000000 | tf_op jit(solution)/shard_map/backward/pallas_call | solution.py:406
  34.5 0.2 collective-permute-start.5
  34.6 1.0 %rows.1 = (bf16[2,128,1024]{2,1,0:T(8,128)(2,1)S(1)}, bf16[2,128,1024]{2,1,0:T(8,128)(2,1)S(1)}) custom-call(bf16[384,512]{1,0:T(8,128)(2,1)S(1)} %get-tuple-element.27.cft_ref.cft_hbm, bf16[512,1024]{1,0:T(8,128)(2,1)S(1)} %get-tuple-element.34.sg_ref.sg_hbm), custom_call_target="tpu_custom_call" | custom-call | flops 1000000000 | bytes 3000000 | tf_op jit(solution)/shard_map/rows/pallas_call | solution.py:406
  35.7 0.0 copy-start.10
  35.7 0.9 mine.1.mine_ref
  36.6 0.8 collective-permute-done.5.theirs_ref
  37.4 1.1 %merge.1 = bf16[512,1152]{1,0:T(8,128)(2,1)} custom-call(bf16[512,1152]{1,0:T(8,128)(2,1)S(1)} %mine.1.mine_ref, bf16[512,1152]{1,0:T(8,128)(2,1)S(1)} %collective-permute-done.5.theirs_ref, bf16[2,128,1024]{2,1,0:T(8,128)(2,1)S(1)} %get-tuple-element.40.after_any), custom_call_target="tpu_custom_call" | custom-call | flops 1000000 | bytes 4000000 | tf_op jit(solution)/shard_map/merge/pallas_call | solution.py:406
  38.5 0.0 copy-start.11
  38.6 11.0 %all-to-all-start = ((bf16[16,32,1152]{2,1,0:T(8,128)(2,1)}), bf16[16,32,1152]{2,1,0:T(8,128)(2,1)S(1)}, u32[]{:S(2)}, u32[]{:S(2)}) async-start(bf16[16,32,1152]{2,1,0:T(8,128)(2,1)} %bitcast.6), calls=%async_computation | async-start | bytes 2359296 | tf_op jit(solution)/shard_map/all_to_all | solution.py:640
  49.5 1.9 %collective-permute-start.8 = (bf16[2,128,1024]{2,1,0:T(8,128)(2,1)S(1)}, bf16[2,128,1024]{2,1,0:T(8,128)(2,1)S(1)}, u32[]{:S(2)}, u32[]{:S(2)}) collective-permute-start(bf16[2,128,1024]{2,1,0:T(8,128)(2,1)S(1)} %get-tuple-element.40.after_any), channel_id=1, source_target_pairs={{1,2},{2,1},{3,4},{4,3},{5,6},{6,5},{7,8},{8,7},{9,10},{10,9},{11,... | collective-permute-start | bytes 1572872 | tf_op jit(solution)/shard_map/ppermute | solution.py:636
  51.5 1.7 %collective-permute-start.6 = (bf16[2,128,1024]{2,1,0:T(8,128)(2,1)S(1)}, bf16[2,128,1024]{2,1,0:T(8,128)(2,1)S(1)}, u32[]{:S(2)}, u32[]{:S(2)}) collective-permute-start(bf16[2,128,1024]{2,1,0:T(8,128)(2,1)S(1)} %copy-done.11), channel_id=1, source_target_pairs={{0,1},{1,0},{2,3},{3,2},{4,5},{5,4},{6,7},{7,6},{8,9},{9,8},{10,11... | collective-permute-start | bytes 1572872 | tf_op jit(solution)/shard_map/ppermute | solution.py:642
  53.1 1.5 %collective-permute-start.7 = (bf16[2,128,1024]{2,1,0:T(8,128)(2,1)S(1)}, bf16[2,128,1024]{2,1,0:T(8,128)(2,1)}, u32[]{:S(2)}, u32[]{:S(2)}) collective-permute-start(bf16[2,128,1024]{2,1,0:T(8,128)(2,1)S(1)} %get-tuple-element.40.after_any), channel_id=1, source_target_pairs={{0,63},{31,32},{32,31},{63,0},{64,127},{95,96},{96,95},{127,64},{1... | collective-permute-start | bytes 1572872 | tf_op jit(solution)/shard_map/ppermute | solution.py:641
  54.6 18.4 %all-to-all-done.got_ref = bf16[16,32,1152]{2,1,0:T(8,128)(2,1)S(1)} async-done(((bf16[16,32,1152]{2,1,0:T(8,128)(2,1)}), bf16[16,32,1152]{2,1,0:T(8,128)(2,1)S(1)}, u32[]{:S(2)}, u32[]{:S(2)}) %all-to-all-start) | async-done | bytes 1179680 | tf_op jit(solution)/shard_map/all_to_all | solution.py:640
  73.0 0.9 %plane.1 = bf16[4,2,16,1152]{3,2,1,0:T(8,128)(2,1)} custom-call(bf16[16,32,1152]{2,1,0:T(8,128)(2,1)S(1)} %all-to-all-done.got_ref), custom_call_target="tpu_custom_call" | custom-call | flops 1000000 | bytes 1000000 | tf_op jit(solution)/shard_map/plane/pallas_call | solution.py:406
  73.9 7.2 %all-to-all-start.1 = ((bf16[8,16,1152]{2,1,0:T(8,128)(2,1)}), bf16[8,16,1152]{2,1,0:T(8,128)(2,1)S(1)}, u32[]{:S(2)}, u32[]{:S(2)}) async-start(bf16[8,16,1152]{2,1,0:T(8,128)(2,1)} %bitcast.7), calls=%async_computation.1 | async-start | bytes 589824 | tf_op jit(solution)/shard_map/all_to_all | solution.py:644
  81.1 3.6 %score.1 = f32[100,256]{1,0:T(8,128)} custom-call(s32[2]{0:T(128)} %copy-done.8, s16[2,112,256]{2,1,0:T(8,128)(2,1)} %copy-done.3, s16[2,112,256]{2,1,0:T(8,128)(2,1)} %copy-done.4, s16[2,112,256]{2,1,0:T(8,128)(2,1)} %copy-done.5, s16[2,112,256]{2,1,0:T(8,128)(2,1)} %copy-done.6, f32[100,256]{1,0:T(8,128)} %truth_ref.1), custom_call_target="tpu_custom_call" | custom-call | flops 10000000 | bytes 1000000 | tf_op jit(solution)/shard_map/score/pallas_call | solution.py:406
  84.7 0.0 collective-permute-done.8.near_any
  84.7 0.0 collective-permute-done.6.core_any
  84.7 0.0 collective-permute-done.7.far_any
  84.7 0.8 copy-done.17
  85.5 0.2 copy-done.18
  85.7 4.0 %latent.1 = bf16[2,128,1024]{2,1,0:T(8,128)(2,1)} custom-call(bf16[384,512]{1,0:T(8,128)(2,1)} %copy-done.2, bf16[512,1024]{1,0:T(8,128)(2,1)} %copy-done, bf16[1024,1024]{1,0:T(8,128)(2,1)} %w_hbm.3, bf16[2,128,1024]{2,1,0:T(8,128)(2,1)} %copy-done.18, bf16[2,128,1024]{2,1,0:T(8,128)(2,1)} %collective-permute-done.7.far_any, bf16[2,128,1024]{2,1,0:T(8,128)(2,1)} %copy-done.17), custom_call_target="tpu_custom_call" | custom-call | flops 1000000000 | bytes 5000000 | tf_op jit(solution)/shard_map/latent/pallas_call | solution.py:406
  89.7 0.2 all-to-all-done.1.got_ref
  89.9 0.7 final.1
  (26 shorter events, 0.0 us)
Async XLA Ops:
  0.6 4.1 %collective-permute-start.1 = (bf16[2,128,1024]{2,1,0:T(8,128)(2,1)}, bf16[2,128,1024]{2,1,0:T(8,128)(2,1)S(1)}, u32[]{:S(2)}, u32[]{:S(2)}) collective-permute-start(bf16[2,128,1024]{2,1,0:T(8,128)(2,1)} %lat_ref.1), channel_id=1, source_target_pairs={{0,1},{1,0},{2,3},{3,2},{4,5},{5,4},{6,7},{7,6},{8,9},{9,8},{10,11... | collective-permute-start | bytes 1572872 | tf_op jit(solution)/shard_map/ppermute | solution.py:615
  0.7 13.8 %collective-permute-start = (bf16[2,128,1024]{2,1,0:T(8,128)(2,1)}, bf16[2,128,1024]{2,1,0:T(8,128)(2,1)S(1)}, u32[]{:S(2)}, u32[]{:S(2)}) collective-permute-start(bf16[2,128,1024]{2,1,0:T(8,128)(2,1)} %lat_ref.1), channel_id=1, source_target_pairs={{0,63},{1,2},{2,1},{3,4},{4,3},{5,6},{6,5},{7,8},{8,7},{9,10},{10,... | collective-permute-start | bytes 1572872 | tf_op jit(solution)/shard_map/ppermute | solution.py:614
  4.7 27.1 %copy-start.8 = (s32[2]{0:T(128)}, s32[2]{0:T(128)S(1)}, u32[]{:S(2)}) copy-start(s32[2]{0:T(128)S(1)} %pad_add_fusion.where_ref) | copy-start | bytes 28
  4.7 9.8 %copy-start.1 = (bf16[1024,1024]{1,0:T(8,128)(2,1)S(1)}, bf16[1024,1024]{1,0:T(8,128)(2,1)}, u32[]{:S(2)}) copy-start(bf16[1024,1024]{1,0:T(8,128)(2,1)} %w_hbm.3) | copy-start | bytes 6291460
  4.7 1.2 %copy-start.9 = (bf16[2,128,1024]{2,1,0:T(8,128)(2,1)S(1)}, bf16[2,128,1024]{2,1,0:T(8,128)(2,1)}, u32[]{:S(2)}) copy-start(bf16[2,128,1024]{2,1,0:T(8,128)(2,1)} %lat_ref.1) | copy-start | bytes 1572868
  5.9 0.7 copy-start.12
  6.6 0.7 copy-start.13
  7.3 0.7 copy-start.14
  8.0 0.7 copy-start.16
  14.5 20.1 %copy-start.2 = (bf16[384,512]{1,0:T(8,128)(2,1)}, bf16[384,512]{1,0:T(8,128)(2,1)S(1)}, u32[]{:S(2)}) copy-start(bf16[384,512]{1,0:T(8,128)(2,1)S(1)} %get-tuple-element.27.cft_ref.cft_hbm) | copy-start | bytes 1179652
  17.3 14.4 %copy-start.3 = (s16[2,112,256]{2,1,0:T(8,128)(2,1)}, s16[2,112,256]{2,1,0:T(8,128)(2,1)S(1)}, u32[]{:S(2)}) copy-start(s16[2,112,256]{2,1,0:T(8,128)(2,1)S(1)} %get-tuple-element.26.c0_any.c0_ref) | copy-start | bytes 344068
  17.4 7.1 %collective-permute-start.2 = (s16[2,112,256]{2,1,0:T(8,128)(2,1)S(1)}, s16[2,112,256]{2,1,0:T(8,128)(2,1)S(1)}, u32[]{:S(2)}, u32[]{:S(2)}) collective-permute-start(s16[2,112,256]{2,1,0:T(8,128)(2,1)S(1)} %get-tuple-element.26.c0_any.c0_ref), channel_id=1, source_target_pairs={{64,0},{128,64},{192,128},{0,192},{65,1},{129,65},{193,129},{1,193... | collective-permute-start | bytes 344072 | tf_op jit(solution)/shard_map/ppermute | solution.py:624
  20.3 11.5 %collective-permute-start.3 = (s16[2,112,256]{2,1,0:T(8,128)(2,1)S(1)}, s16[2,112,256]{2,1,0:T(8,128)(2,1)S(1)}, u32[]{:S(2)}, u32[]{:S(2)}) collective-permute-start(s16[2,112,256]{2,1,0:T(8,128)(2,1)S(1)} %get-tuple-element.26.c0_any.c0_ref), channel_id=1, source_target_pairs={{128,0},{192,64},{0,128},{64,192},{129,1},{193,65},{1,129},{65,193... | collective-permute-start | bytes 344072 | tf_op jit(solution)/shard_map/ppermute | solution.py:624
  20.3 11.5 %collective-permute-start.4 = (s16[2,112,256]{2,1,0:T(8,128)(2,1)S(1)}, s16[2,112,256]{2,1,0:T(8,128)(2,1)S(1)}, u32[]{:S(2)}, u32[]{:S(2)}) collective-permute-start(s16[2,112,256]{2,1,0:T(8,128)(2,1)S(1)} %get-tuple-element.26.c0_any.c0_ref), channel_id=1, source_target_pairs={{192,0},{0,64},{64,128},{128,192},{193,1},{1,65},{65,129},{129,193... | collective-permute-start | bytes 344072 | tf_op jit(solution)/shard_map/ppermute | solution.py:624
  21.0 10.8 %copy-start.7 = (f32[100,256]{1,0:T(8,128)S(1)}, f32[100,256]{1,0:T(8,128)}, u32[]{:S(2)}) copy-start(f32[100,256]{1,0:T(8,128)} %truth_ref.1) | copy-start | bytes 307204
  21.0 10.8 %copy-start.15 = (f32[256]{0:T(256)S(1)}, f32[256]{0:T(256)}, u32[]{:S(2)}) copy-start(f32[256]{0:T(256)} %param.14) | copy-start | bytes 3076
  24.5 10.0 %copy-start.4 = (s16[2,112,256]{2,1,0:T(8,128)(2,1)}, s16[2,112,256]{2,1,0:T(8,128)(2,1)S(1)}, u32[]{:S(2)}) copy-start(s16[2,112,256]{2,1,0:T(8,128)(2,1)S(1)} %collective-permute-done.2.c1_any.c1_ref) | copy-start | bytes 344068
  31.8 2.7 %copy-start.5 = (s16[2,112,256]{2,1,0:T(8,128)(2,1)}, s16[2,112,256]{2,1,0:T(8,128)(2,1)S(1)}, u32[]{:S(2)}) copy-start(s16[2,112,256]{2,1,0:T(8,128)(2,1)S(1)} %collective-permute-done.3.c2_any.c2_ref) | copy-start | bytes 344068
  31.8 2.7 %copy-start.6 = (s16[2,112,256]{2,1,0:T(8,128)(2,1)}, s16[2,112,256]{2,1,0:T(8,128)(2,1)S(1)}, u32[]{:S(2)}) copy-start(s16[2,112,256]{2,1,0:T(8,128)(2,1)S(1)} %collective-permute-done.4.c3_any.c3_ref) | copy-start | bytes 344068
  34.4 1.2 %copy-start = (bf16[512,1024]{1,0:T(8,128)(2,1)}, bf16[512,1024]{1,0:T(8,128)(2,1)S(1)}, u32[]{:S(2)}) copy-start(bf16[512,1024]{1,0:T(8,128)(2,1)S(1)} %get-tuple-element.34.sg_ref.sg_hbm) | copy-start | bytes 3145732
  34.5 2.9 %collective-permute-start.5 = (bf16[512,1152]{1,0:T(8,128)(2,1)S(1)}, bf16[512,1152]{1,0:T(8,128)(2,1)S(1)}, u32[]{:S(2)}, u32[]{:S(2)}) collective-permute-start(bf16[512,1152]{1,0:T(8,128)(2,1)S(1)} %get-tuple-element.36), channel_id=1, source_target_pairs={{0,1},{1,0},{2,3},{3,2},{4,5},{5,4},{6,7},{7,6},{8,9},{9,8},{10,11... | collective-permute-start | bytes 3538952 | tf_op jit(solution)/shard_map/ppermute | solution.py:633
  35.7 0.9 copy-start.10
  38.5 12.9 %copy-start.11 = (bf16[2,128,1024]{2,1,0:T(8,128)(2,1)S(1)}, bf16[2,128,1024]{2,1,0:T(8,128)(2,1)}, u32[]{:S(2)}) copy-start(bf16[2,128,1024]{2,1,0:T(8,128)(2,1)} %copy-done.10) | copy-start | bytes 1572868
  38.6 34.4 %all-to-all-start = ((bf16[16,32,1152]{2,1,0:T(8,128)(2,1)}), bf16[16,32,1152]{2,1,0:T(8,128)(2,1)S(1)}, u32[]{:S(2)}, u32[]{:S(2)}) async-start(bf16[16,32,1152]{2,1,0:T(8,128)(2,1)} %bitcast.6), calls=%async_computation | async-start | bytes 2359296 | tf_op jit(solution)/shard_map/all_to_all | solution.py:640
  49.5 35.1 %collective-permute-start.8 = (bf16[2,128,1024]{2,1,0:T(8,128)(2,1)S(1)}, bf16[2,128,1024]{2,1,0:T(8,128)(2,1)S(1)}, u32[]{:S(2)}, u32[]{:S(2)}) collective-permute-start(bf16[2,128,1024]{2,1,0:T(8,128)(2,1)S(1)} %get-tuple-element.40.after_any), channel_id=1, source_target_pairs={{1,2},{2,1},{3,4},{4,3},{5,6},{6,5},{7,8},{8,7},{9,10},{10,9},{11,... | collective-permute-start | bytes 1572872 | tf_op jit(solution)/shard_map/ppermute | solution.py:636
  51.5 33.2 %collective-permute-start.6 = (bf16[2,128,1024]{2,1,0:T(8,128)(2,1)S(1)}, bf16[2,128,1024]{2,1,0:T(8,128)(2,1)S(1)}, u32[]{:S(2)}, u32[]{:S(2)}) collective-permute-start(bf16[2,128,1024]{2,1,0:T(8,128)(2,1)S(1)} %copy-done.11), channel_id=1, source_target_pairs={{0,1},{1,0},{2,3},{3,2},{4,5},{5,4},{6,7},{7,6},{8,9},{9,8},{10,11... | collective-permute-start | bytes 1572872 | tf_op jit(solution)/shard_map/ppermute | solution.py:642
  53.1 31.6 %collective-permute-start.7 = (bf16[2,128,1024]{2,1,0:T(8,128)(2,1)S(1)}, bf16[2,128,1024]{2,1,0:T(8,128)(2,1)}, u32[]{:S(2)}, u32[]{:S(2)}) collective-permute-start(bf16[2,128,1024]{2,1,0:T(8,128)(2,1)S(1)} %get-tuple-element.40.after_any), channel_id=1, source_target_pairs={{0,63},{31,32},{32,31},{63,0},{64,127},{95,96},{96,95},{127,64},{1... | collective-permute-start | bytes 1572872 | tf_op jit(solution)/shard_map/ppermute | solution.py:641
  73.9 16.0 %all-to-all-start.1 = ((bf16[8,16,1152]{2,1,0:T(8,128)(2,1)}), bf16[8,16,1152]{2,1,0:T(8,128)(2,1)S(1)}, u32[]{:S(2)}, u32[]{:S(2)}) async-start(bf16[8,16,1152]{2,1,0:T(8,128)(2,1)} %bitcast.7), calls=%async_computation.1 | async-start | bytes 589824 | tf_op jit(solution)/shard_map/all_to_all | solution.py:644
  84.7 0.8 copy-start.17
  84.7 1.0 %copy-start.18 = (bf16[2,128,1024]{2,1,0:T(8,128)(2,1)}, bf16[2,128,1024]{2,1,0:T(8,128)(2,1)S(1)}, u32[]{:S(2)}) copy-start(bf16[2,128,1024]{2,1,0:T(8,128)(2,1)S(1)} %collective-permute-done.6.core_any) | copy-start | bytes 1572868

commit v10 on v9

--- a/solution.py
+++ b/solution.py
@@ -620,10 +620,12 @@
         var_row = jnp.pad(var_weight, (0, VPAD - nvar)).reshape(1, VPAD)
         area_row = area_weight.reshape(1, points)
         summed, hidden, coded = call_forward(odd_lat, src_weight, cfo, part, dpt)
-        codes = [coded] + [
-            lax.ppermute(coded, "ens", [((e + k) % ens, e) for e in range(ens)])
-            for k in range(1, ens)
-        ]
+        order = sorted(range(1, ens), key=lambda k: -min(k, ens - k))
+        moved = {
+            k: lax.ppermute(coded, "ens", [((e + k) % ens, e) for e in range(ens)])
+            for k in order
+        }
+        codes = [coded] + [moved[k] for k in range(1, ens)]
         aggt, hidt, slope = call_factors(
             where, latent, core_lat, odd_lat, cf, summed, hidden
         )

time: 91.4 us -> 91.4 us (level)
  no operation moved by 1% of the time
where the time goes in v10:
time: 91.4 us; the launch traced here: 90.6 us
  starting transfers between devices  29.4 us (32%)
  Pallas kernels  26.9 us (29%)
  waiting for transfers between devices  26.8 us (29%)
  local copies, waits for them, and re-layouts  6.5 us (7%)
  between operations  0.92 us (1%)
    pallas_call x11, Pallas kernels, call(): pl.pallas_call(kernel, out_shape=out_shape, in_specs=in_specs, out_specs=...  26.9 us
    all_to_all x1, waiting for transfers between devices, body(): got = lax.all_to_all(part, ('x', 'y'), 0, 0, tiled=True)  18.4 us
    all_to_all x1, starting transfers between devices, body(): got = lax.all_to_all(part, ('x', 'y'), 0, 0, tiled=True)  11 us
    ppermute x3, waiting for transfers between devices, body(): lax.ppermute(coded, 'ens', [((e + k) % ens, e) for e in range(ens)])  7.3 us
    all_to_all x1, starting transfers between devices, body(): got = lax.all_to_all(plane, ('ens', 'zhi'), 0, 0, tiled=True)  7.18 us
    unnamed x38, local copies, waits for them, and re-layouts  4.89 us
    ppermute x3, starting transfers between devices, body(): lax.ppermute(coded, 'ens', [((e + k) % ens, e) for e in range(ens)])  3.62 us
    ppermute x1, starting transfers between devices, body(): lax.ppermute(latent, SPACE, odd_pairs).reshape(local * rows, depth)  2.28 us
  transfers between devices with their start and end apart: 11, of which 4 were waited for; matrix products, arithmetic and copies ran while one was open for 2% of the time, Pallas kernels for 22%

profile of v10, /device:TPU:8, one launch (start us, length us, event | category | flops | bytes accessed | tf_op | source)
XLA Modules:
  0.0 90.6 jit_solution(11520841362096194718)
XLA Ops:
  0.6 0.1 collective-permute-start.1
  0.7 2.3 %collective-permute-start = (bf16[2,128,1024]{2,1,0:T(8,128)(2,1)}, bf16[2,128,1024]{2,1,0:T(8,128)(2,1)S(1)}, u32[]{:S(2)}, u32[]{:S(2)}) collective-permute-start(bf16[2,128,1024]{2,1,0:T(8,128)(2,1)} %lat_ref.1), channel_id=1, source_target_pairs={{0,63},{1,2},{2,1},{3,4},{4,3},{5,6},{6,5},{7,8},{8,7},{9,10},{10,... | collective-permute-start | bytes 1572872 | tf_op jit(solution)/shard_map/ppermute | solution.py:614
  3.0 1.0 %pad.8.dpt_ref = bf16[128,1024]{1,0:T(8,128)(2,1)S(1)} pad(bf16[100,1024]{1,0:T(8,128)(2,1)} %bitcast.12, bf16[]{:T(256)} %constant.13.clone.1), padding=0_28x0_0 | pad | bytes 466946 | tf_op jit(solution)/shard_map/jit(_pad)/pad | solution.py:616
  4.0 0.7 pad_bitcast_fusion.var_ref
  4.6 0.1 pad_add_fusion.where_ref
  4.7 0.0 collective-permute-done.1.clat_hbm.clat_ref
  4.7 1.2 %copy-done.9 = bf16[2,128,1024]{2,1,0:T(8,128)(2,1)S(1)} copy-done((bf16[2,128,1024]{2,1,0:T(8,128)(2,1)S(1)}, bf16[2,128,1024]{2,1,0:T(8,128)(2,1)}, u32[]{:S(2)}) %copy-start.9) | copy-done | bytes 524312
  5.9 0.7 copy-done.12
  6.6 0.7 copy-done.13
  7.3 0.7 copy-done.14
  8.0 0.7 copy-done.16
  8.6 5.9 %prepare.1 = (bf16[256,768]{1,0:T(8,128)(2,1)S(1)}, bf16[384,512]{1,0:T(8,128)(2,1)S(1)}, bf16[256,256]{1,0:T(8,128)(2,1)S(1)}, f32[2,256,1024]{2,1,0:T(8,128)S(1)}) custom-call(s32[2]{0:T(128)S(1)} %pad_add_fusion.where_ref, s32[2]{0:T(128)S(1)} %copy-done.16, s32[2,512]{1,0:T(2,128)S(1)} %copy-done.12, s32[2,512]{1,0:T(2,128)S(1)} %copy-done.13, ...), custom_call_target="tpu_custom_call" | custom-call | flops 3000000000 | bytes 6000000 | tf_op jit(solution)/shard_map/prepare/pallas_call | solution.py:406
  14.5 0.0 collective-permute-done
  14.6 2.8 %forward.1 = (f32[2,256,1024]{2,1,0:T(8,128)S(1)}, bf16[2,256,1024]{2,1,0:T(8,128)(2,1)S(1)}, s16[2,112,256]{2,1,0:T(8,128)(2,1)S(1)}) custom-call(bf16[256,1024]{1,0:T(8,128)(2,1)S(1)} %bitcast.9, bf16[1024,1024]{1,0:T(8,128)(2,1)S(1)} %copy-done.1, bf16[256,256]{1,0:T(8,128)(2,1)S(1)} %get-tuple-element.24.cfo_ref, ...), custom_call_target="tpu_custom_call" | custom-call | flops 2000000000 | bytes 8000000 | tf_op jit(solution)/shard_map/forward/pallas_call | solution.py:406
  17.4 2.9 %collective-permute-start.2 = (s16[2,112,256]{2,1,0:T(8,128)(2,1)S(1)}, s16[2,112,256]{2,1,0:T(8,128)(2,1)S(1)}, u32[]{:S(2)}, u32[]{:S(2)}) collective-permute-start(s16[2,112,256]{2,1,0:T(8,128)(2,1)S(1)} %get-tuple-element.26.c0_any.c0_ref), channel_id=1, source_target_pairs={{64,0},{128,64},{192,128},{0,192},{65,1},{129,65},{193,129},{1,193... | collective-permute-start | bytes 344072 | tf_op jit(solution)/shard_map/ppermute | solution.py:625
  20.3 0.0 collective-permute-start.3
  20.3 0.7 collective-permute-start.4
  21.0 3.5 %factors.1 = (bf16[1024,512]{1,0:T(8,128)(2,1)S(1)}, bf16[1024,512]{1,0:T(8,128)(2,1)S(1)}, f32[2,256,1024]{2,1,0:T(8,128)S(1)}) custom-call(s32[2]{0:T(128)S(1)} %pad_add_fusion.where_ref, bf16[2,128,1024]{2,1,0:T(8,128)(2,1)S(1)} %copy-done.9, bf16[2,128,1024]{2,1,0:T(8,128)(2,1)S(1)} %collective-permute-done.1.clat_hbm.clat_ref, ...), custom_call_target="tpu_custom_call" | custom-call | flops 3000000000 | bytes 10000000 | tf_op jit(solution)/shard_map/factors/pallas_call | solution.py:406
  24.4 0.0 collective-permute-done.2.c1_any.c1_ref
  24.5 7.3 %collective-permute-done.3.c2_any.c2_ref = s16[2,112,256]{2,1,0:T(8,128)(2,1)S(1)} collective-permute-done((s16[2,112,256]{2,1,0:T(8,128)(2,1)S(1)}, s16[2,112,256]{2,1,0:T(8,128)(2,1)S(1)}, u32[]{:S(2)}, u32[]{:S(2)}) %collective-permute-start.3) | collective-permute-done | bytes 114720 | tf_op jit(solution)/shard_map/ppermute | solution.py:625
  31.8 0.0 collective-permute-done.4.c3_any.c3_ref
  31.8 0.0 copy-done.3
  31.8 0.0 copy-done.7
  31.8 0.0 copy-done.15
  31.8 2.6 %backward.1 = (bf16[512,1152]{1,0:T(8,128)(2,1)S(1)}, bf16[512,1024]{1,0:T(8,128)(2,1)S(1)}, bf16[512,128]{1,0:T(8,128)(2,1)S(1)}) custom-call(s32[2]{0:T(128)S(1)} %pad_add_fusion.where_ref, s16[2,112,256]{2,1,0:T(8,128)(2,1)S(1)} %get-tuple-element.26.c0_any.c0_ref, s16[2,112,256]{2,1,0:T(8,128)(2,1)S(1)} %collective-permute-done.2.c1_any.c1_ref, ...), custom_call_target="tpu_custom_call" | custom-call | flops 2000000000 | bytes 5000000 | tf_op jit(solution)/shard_map/backward/pallas_call | solution.py:406
  34.5 0.2 collective-permute-start.5
  34.6 1.0 %rows.1 = (bf16[2,128,1024]{2,1,0:T(8,128)(2,1)S(1)}, bf16[2,128,1024]{2,1,0:T(8,128)(2,1)S(1)}) custom-call(bf16[384,512]{1,0:T(8,128)(2,1)S(1)} %get-tuple-element.27.cft_ref.cft_hbm, bf16[512,1024]{1,0:T(8,128)(2,1)S(1)} %get-tuple-element.34.sg_ref.sg_hbm), custom_call_target="tpu_custom_call" | custom-call | flops 1000000000 | bytes 3000000 | tf_op jit(solution)/shard_map/rows/pallas_call | solution.py:406
  35.7 0.0 copy-start.10
  35.7 0.9 mine.1.mine_ref
  36.6 0.8 collective-permute-done.5.theirs_ref
  37.4 1.1 %merge.1 = bf16[512,1152]{1,0:T(8,128)(2,1)} custom-call(bf16[512,1152]{1,0:T(8,128)(2,1)S(1)} %mine.1.mine_ref, bf16[512,1152]{1,0:T(8,128)(2,1)S(1)} %collective-permute-done.5.theirs_ref, bf16[2,128,1024]{2,1,0:T(8,128)(2,1)S(1)} %get-tuple-element.40.after_any), custom_call_target="tpu_custom_call" | custom-call | flops 1000000 | bytes 4000000 | tf_op jit(solution)/shard_map/merge/pallas_call | solution.py:406
  38.5 0.0 copy-start.11
  38.6 11.0 %all-to-all-start = ((bf16[16,32,1152]{2,1,0:T(8,128)(2,1)}), bf16[16,32,1152]{2,1,0:T(8,128)(2,1)S(1)}, u32[]{:S(2)}, u32[]{:S(2)}) async-start(bf16[16,32,1152]{2,1,0:T(8,128)(2,1)} %bitcast.6), calls=%async_computation | async-start | bytes 2359296 | tf_op jit(solution)/shard_map/all_to_all | solution.py:642
  49.5 1.9 %collective-permute-start.8 = (bf16[2,128,1024]{2,1,0:T(8,128)(2,1)S(1)}, bf16[2,128,1024]{2,1,0:T(8,128)(2,1)S(1)}, u32[]{:S(2)}, u32[]{:S(2)}) collective-permute-start(bf16[2,128,1024]{2,1,0:T(8,128)(2,1)S(1)} %get-tuple-element.40.after_any), channel_id=1, source_target_pairs={{1,2},{2,1},{3,4},{4,3},{5,6},{6,5},{7,8},{8,7},{9,10},{10,9},{11,... | collective-permute-start | bytes 1572872 | tf_op jit(solution)/shard_map/ppermute | solution.py:638
  51.5 1.7 %collective-permute-start.6 = (bf16[2,128,1024]{2,1,0:T(8,128)(2,1)S(1)}, bf16[2,128,1024]{2,1,0:T(8,128)(2,1)S(1)}, u32[]{:S(2)}, u32[]{:S(2)}) collective-permute-start(bf16[2,128,1024]{2,1,0:T(8,128)(2,1)S(1)} %copy-done.11), channel_id=1, source_target_pairs={{0,1},{1,0},{2,3},{3,2},{4,5},{5,4},{6,7},{7,6},{8,9},{9,8},{10,11... | collective-permute-start | bytes 1572872 | tf_op jit(solution)/shard_map/ppermute | solution.py:644
  53.1 1.5 %collective-permute-start.7 = (bf16[2,128,1024]{2,1,0:T(8,128)(2,1)S(1)}, bf16[2,128,1024]{2,1,0:T(8,128)(2,1)}, u32[]{:S(2)}, u32[]{:S(2)}) collective-permute-start(bf16[2,128,1024]{2,1,0:T(8,128)(2,1)S(1)} %get-tuple-element.40.after_any), channel_id=1, source_target_pairs={{0,63},{31,32},{32,31},{63,0},{64,127},{95,96},{96,95},{127,64},{1... | collective-permute-start | bytes 1572872 | tf_op jit(solution)/shard_map/ppermute | solution.py:643
  54.6 18.4 %all-to-all-done.got_ref = bf16[16,32,1152]{2,1,0:T(8,128)(2,1)S(1)} async-done(((bf16[16,32,1152]{2,1,0:T(8,128)(2,1)}), bf16[16,32,1152]{2,1,0:T(8,128)(2,1)S(1)}, u32[]{:S(2)}, u32[]{:S(2)}) %all-to-all-start) | async-done | bytes 1179680 | tf_op jit(solution)/shard_map/all_to_all | solution.py:642
  73.0 0.9 %plane.1 = bf16[4,2,16,1152]{3,2,1,0:T(8,128)(2,1)} custom-call(bf16[16,32,1152]{2,1,0:T(8,128)(2,1)S(1)} %all-to-all-done.got_ref), custom_call_target="tpu_custom_call" | custom-call | flops 1000000 | bytes 1000000 | tf_op jit(solution)/shard_map/plane/pallas_call | solution.py:406
  73.9 7.2 %all-to-all-start.1 = ((bf16[8,16,1152]{2,1,0:T(8,128)(2,1)}), bf16[8,16,1152]{2,1,0:T(8,128)(2,1)S(1)}, u32[]{:S(2)}, u32[]{:S(2)}) async-start(bf16[8,16,1152]{2,1,0:T(8,128)(2,1)} %bitcast.7), calls=%async_computation.1 | async-start | bytes 589824 | tf_op jit(solution)/shard_map/all_to_all | solution.py:646
  81.1 3.6 %score.1 = f32[100,256]{1,0:T(8,128)} custom-call(s32[2]{0:T(128)} %copy-done.8, s16[2,112,256]{2,1,0:T(8,128)(2,1)} %copy-done.3, s16[2,112,256]{2,1,0:T(8,128)(2,1)} %copy-done.4, s16[2,112,256]{2,1,0:T(8,128)(2,1)} %copy-done.5, s16[2,112,256]{2,1,0:T(8,128)(2,1)} %copy-done.6, f32[100,256]{1,0:T(8,128)} %truth_ref.1), custom_call_target="tpu_custom_call" | custom-call | flops 10000000 | bytes 1000000 | tf_op jit(solution)/shard_map/score/pallas_call | solution.py:406
  84.7 0.0 collective-permute-done.8.near_any
  84.7 0.0 collective-permute-done.6.core_any
  84.7 0.0 collective-permute-done.7.far_any
  84.7 0.8 copy-done.17
  85.5 0.2 copy-done.18
  85.7 4.0 %latent.1 = bf16[2,128,1024]{2,1,0:T(8,128)(2,1)} custom-call(bf16[384,512]{1,0:T(8,128)(2,1)} %copy-done.2, bf16[512,1024]{1,0:T(8,128)(2,1)} %copy-done, bf16[1024,1024]{1,0:T(8,128)(2,1)} %w_hbm.3, bf16[2,128,1024]{2,1,0:T(8,128)(2,1)} %copy-done.18, bf16[2,128,1024]{2,1,0:T(8,128)(2,1)} %collective-permute-done.7.far_any, bf16[2,128,1024]{2,1,0:T(8,128)(2,1)} %copy-done.17), custom_call_target="tpu_custom_call" | custom-call | flops 1000000000 | bytes 5000000 | tf_op jit(solution)/shard_map/latent/pallas_call | solution.py:406
  89.7 0.2 all-to-all-done.1.got_ref
  89.9 0.7 final.1
  (26 shorter events, 0.0 us)
Async XLA Ops:
  0.6 4.1 %collective-permute-start.1 = (bf16[2,128,1024]{2,1,0:T(8,128)(2,1)}, bf16[2,128,1024]{2,1,0:T(8,128)(2,1)S(1)}, u32[]{:S(2)}, u32[]{:S(2)}) collective-permute-start(bf16[2,128,1024]{2,1,0:T(8,128)(2,1)} %lat_ref.1), channel_id=1, source_target_pairs={{0,1},{1,0},{2,3},{3,2},{4,5},{5,4},{6,7},{7,6},{8,9},{9,8},{10,11... | collective-permute-start | bytes 1572872 | tf_op jit(solution)/shard_map/ppermute | solution.py:615
  0.7 13.8 %collective-permute-start = (bf16[2,128,1024]{2,1,0:T(8,128)(2,1)}, bf16[2,128,1024]{2,1,0:T(8,128)(2,1)S(1)}, u32[]{:S(2)}, u32[]{:S(2)}) collective-permute-start(bf16[2,128,1024]{2,1,0:T(8,128)(2,1)} %lat_ref.1), channel_id=1, source_target_pairs={{0,63},{1,2},{2,1},{3,4},{4,3},{5,6},{6,5},{7,8},{8,7},{9,10},{10,... | collective-permute-start | bytes 1572872 | tf_op jit(solution)/shard_map/ppermute | solution.py:614
  4.7 27.1 %copy-start.8 = (s32[2]{0:T(128)}, s32[2]{0:T(128)S(1)}, u32[]{:S(2)}) copy-start(s32[2]{0:T(128)S(1)} %pad_add_fusion.where_ref) | copy-start | bytes 28
  4.7 9.8 %copy-start.1 = (bf16[1024,1024]{1,0:T(8,128)(2,1)S(1)}, bf16[1024,1024]{1,0:T(8,128)(2,1)}, u32[]{:S(2)}) copy-start(bf16[1024,1024]{1,0:T(8,128)(2,1)} %w_hbm.3) | copy-start | bytes 6291460
  4.7 1.2 %copy-start.9 = (bf16[2,128,1024]{2,1,0:T(8,128)(2,1)S(1)}, bf16[2,128,1024]{2,1,0:T(8,128)(2,1)}, u32[]{:S(2)}) copy-start(bf16[2,128,1024]{2,1,0:T(8,128)(2,1)} %lat_ref.1) | copy-start | bytes 1572868
  5.9 0.7 copy-start.12
  6.6 0.7 copy-start.13
  7.3 0.7 copy-start.14
  8.0 0.7 copy-start.16
  14.5 20.1 %copy-start.2 = (bf16[384,512]{1,0:T(8,128)(2,1)}, bf16[384,512]{1,0:T(8,128)(2,1)S(1)}, u32[]{:S(2)}) copy-start(bf16[384,512]{1,0:T(8,128)(2,1)S(1)} %get-tuple-element.27.cft_ref.cft_hbm) | copy-start | bytes 1179652
  17.3 14.4 %copy-start.3 = (s16[2,112,256]{2,1,0:T(8,128)(2,1)}, s16[2,112,256]{2,1,0:T(8,128)(2,1)S(1)}, u32[]{:S(2)}) copy-start(s16[2,112,256]{2,1,0:T(8,128)(2,1)S(1)} %get-tuple-element.26.c0_any.c0_ref) | copy-start | bytes 344068
  17.4 7.1 %collective-permute-start.2 = (s16[2,112,256]{2,1,0:T(8,128)(2,1)S(1)}, s16[2,112,256]{2,1,0:T(8,128)(2,1)S(1)}, u32[]{:S(2)}, u32[]{:S(2)}) collective-permute-start(s16[2,112,256]{2,1,0:T(8,128)(2,1)S(1)} %get-tuple-element.26.c0_any.c0_ref), channel_id=1, source_target_pairs={{64,0},{128,64},{192,128},{0,192},{65,1},{129,65},{193,129},{1,193... | collective-permute-start | bytes 344072 | tf_op jit(solution)/shard_map/ppermute | solution.py:625
  20.3 11.5 %collective-permute-start.3 = (s16[2,112,256]{2,1,0:T(8,128)(2,1)S(1)}, s16[2,112,256]{2,1,0:T(8,128)(2,1)S(1)}, u32[]{:S(2)}, u32[]{:S(2)}) collective-permute-start(s16[2,112,256]{2,1,0:T(8,128)(2,1)S(1)} %get-tuple-element.26.c0_any.c0_ref), channel_id=1, source_target_pairs={{128,0},{192,64},{0,128},{64,192},{129,1},{193,65},{1,129},{65,193... | collective-permute-start | bytes 344072 | tf_op jit(solution)/shard_map/ppermute | solution.py:625
  20.3 11.5 %collective-permute-start.4 = (s16[2,112,256]{2,1,0:T(8,128)(2,1)S(1)}, s16[2,112,256]{2,1,0:T(8,128)(2,1)S(1)}, u32[]{:S(2)}, u32[]{:S(2)}) collective-permute-start(s16[2,112,256]{2,1,0:T(8,128)(2,1)S(1)} %get-tuple-element.26.c0_any.c0_ref), channel_id=1, source_target_pairs={{192,0},{0,64},{64,128},{128,192},{193,1},{1,65},{65,129},{129,193... | collective-permute-start | bytes 344072 | tf_op jit(solution)/shard_map/ppermute | solution.py:625
  21.0 10.8 %copy-start.7 = (f32[100,256]{1,0:T(8,128)S(1)}, f32[100,256]{1,0:T(8,128)}, u32[]{:S(2)}) copy-start(f32[100,256]{1,0:T(8,128)} %truth_ref.1) | copy-start | bytes 307204
  21.0 10.8 %copy-start.15 = (f32[256]{0:T(256)S(1)}, f32[256]{0:T(256)}, u32[]{:S(2)}) copy-start(f32[256]{0:T(256)} %param.14) | copy-start | bytes 3076
  24.5 10.0 %copy-start.4 = (s16[2,112,256]{2,1,0:T(8,128)(2,1)}, s16[2,112,256]{2,1,0:T(8,128)(2,1)S(1)}, u32[]{:S(2)}) copy-start(s16[2,112,256]{2,1,0:T(8,128)(2,1)S(1)} %collective-permute-done.2.c1_any.c1_ref) | copy-start | bytes 344068
  31.8 2.7 %copy-start.5 = (s16[2,112,256]{2,1,0:T(8,128)(2,1)}, s16[2,112,256]{2,1,0:T(8,128)(2,1)S(1)}, u32[]{:S(2)}) copy-start(s16[2,112,256]{2,1,0:T(8,128)(2,1)S(1)} %collective-permute-done.3.c2_any.c2_ref) | copy-start | bytes 344068
  31.8 2.7 %copy-start.6 = (s16[2,112,256]{2,1,0:T(8,128)(2,1)}, s16[2,112,256]{2,1,0:T(8,128)(2,1)S(1)}, u32[]{:S(2)}) copy-start(s16[2,112,256]{2,1,0:T(8,128)(2,1)S(1)} %collective-permute-done.4.c3_any.c3_ref) | copy-start | bytes 344068
  34.4 1.2 %copy-start = (bf16[512,1024]{1,0:T(8,128)(2,1)}, bf16[512,1024]{1,0:T(8,128)(2,1)S(1)}, u32[]{:S(2)}) copy-start(bf16[512,1024]{1,0:T(8,128)(2,1)S(1)} %get-tuple-element.34.sg_ref.sg_hbm) | copy-start | bytes 3145732
  34.5 2.9 %collective-permute-start.5 = (bf16[512,1152]{1,0:T(8,128)(2,1)S(1)}, bf16[512,1152]{1,0:T(8,128)(2,1)S(1)}, u32[]{:S(2)}, u32[]{:S(2)}) collective-permute-start(bf16[512,1152]{1,0:T(8,128)(2,1)S(1)} %get-tuple-element.36), channel_id=1, source_target_pairs={{0,1},{1,0},{2,3},{3,2},{4,5},{5,4},{6,7},{7,6},{8,9},{9,8},{10,11... | collective-permute-start | bytes 3538952 | tf_op jit(solution)/shard_map/ppermute | solution.py:635
  35.7 0.9 copy-start.10
  38.5 12.9 %copy-start.11 = (bf16[2,128,1024]{2,1,0:T(8,128)(2,1)S(1)}, bf16[2,128,1024]{2,1,0:T(8,128)(2,1)}, u32[]{:S(2)}) copy-start(bf16[2,128,1024]{2,1,0:T(8,128)(2,1)} %copy-done.10) | copy-start | bytes 1572868
  38.6 34.4 %all-to-all-start = ((bf16[16,32,1152]{2,1,0:T(8,128)(2,1)}), bf16[16,32,1152]{2,1,0:T(8,128)(2,1)S(1)}, u32[]{:S(2)}, u32[]{:S(2)}) async-start(bf16[16,32,1152]{2,1,0:T(8,128)(2,1)} %bitcast.6), calls=%async_computation | async-start | bytes 2359296 | tf_op jit(solution)/shard_map/all_to_all | solution.py:642
  49.5 35.1 %collective-permute-start.8 = (bf16[2,128,1024]{2,1,0:T(8,128)(2,1)S(1)}, bf16[2,128,1024]{2,1,0:T(8,128)(2,1)S(1)}, u32[]{:S(2)}, u32[]{:S(2)}) collective-permute-start(bf16[2,128,1024]{2,1,0:T(8,128)(2,1)S(1)} %get-tuple-element.40.after_any), channel_id=1, source_target_pairs={{1,2},{2,1},{3,4},{4,3},{5,6},{6,5},{7,8},{8,7},{9,10},{10,9},{11,... | collective-permute-start | bytes 1572872 | tf_op jit(solution)/shard_map/ppermute | solution.py:638
  51.5 33.2 %collective-permute-start.6 = (bf16[2,128,1024]{2,1,0:T(8,128)(2,1)S(1)}, bf16[2,128,1024]{2,1,0:T(8,128)(2,1)S(1)}, u32[]{:S(2)}, u32[]{:S(2)}) collective-permute-start(bf16[2,128,1024]{2,1,0:T(8,128)(2,1)S(1)} %copy-done.11), channel_id=1, source_target_pairs={{0,1},{1,0},{2,3},{3,2},{4,5},{5,4},{6,7},{7,6},{8,9},{9,8},{10,11... | collective-permute-start | bytes 1572872 | tf_op jit(solution)/shard_map/ppermute | solution.py:644
  53.1 31.6 %collective-permute-start.7 = (bf16[2,128,1024]{2,1,0:T(8,128)(2,1)S(1)}, bf16[2,128,1024]{2,1,0:T(8,128)(2,1)}, u32[]{:S(2)}, u32[]{:S(2)}) collective-permute-start(bf16[2,128,1024]{2,1,0:T(8,128)(2,1)S(1)} %get-tuple-element.40.after_any), channel_id=1, source_target_pairs={{0,63},{31,32},{32,31},{63,0},{64,127},{95,96},{96,95},{127,64},{1... | collective-permute-start | bytes 1572872 | tf_op jit(solution)/shard_map/ppermute | solution.py:643
  73.9 16.0 %all-to-all-start.1 = ((bf16[8,16,1152]{2,1,0:T(8,128)(2,1)}), bf16[8,16,1152]{2,1,0:T(8,128)(2,1)S(1)}, u32[]{:S(2)}, u32[]{:S(2)}) async-start(bf16[8,16,1152]{2,1,0:T(8,128)(2,1)} %bitcast.7), calls=%async_computation.1 | async-start | bytes 589824 | tf_op jit(solution)/shard_map/all_to_all | solution.py:646
  84.7 0.8 copy-start.17
  84.7 1.0 %copy-start.18 = (bf16[2,128,1024]{2,1,0:T(8,128)(2,1)}, bf16[2,128,1024]{2,1,0:T(8,128)(2,1)S(1)}, u32[]{:S(2)}) copy-start(bf16[2,128,1024]{2,1,0:T(8,128)(2,1)S(1)} %collective-permute-done.6.core_any) | copy-start | bytes 1572868
